TPU v7x, 32 devices: a whole 2x2x4 slice. The times are simulated.
32 devices in a mesh: dp: 16 (over z, y, core), mp: 2 (over x).
Axes of the slice: x: 2, y: 2, z: 4, core: 2. Of those that a mesh axis runs over, the one named last changes fastest.
Arguments:
- tokens: bfloat16 [1024, 32, 1024], P('mp', 'dp'), may hold values from -6 to 6
- memory: bfloat16 [1024, 32, 1024], P('mp', 'dp'), may hold values from -6 to 6
- cotangent: bfloat16 [1024, 32, 1024], P('mp', 'dp'), may hold values from -6 to 6
- lengths: int32 [32], P('dp'), may hold values from 1 to 1024, 24576 in all
- memory_lengths: int32 [32], P('dp'), may hold values from 1 to 1024, 24576 in all
- pair_ids: int32 [32], P('dp'), may hold values from 0 to 7
- pair_counts: int32 [8], replicated, may hold values from 128 to 1023
- self_in: bfloat16 [3, 1024, 1024], P(None, 'dp', 'mp'), may hold values from -0.1875 to 0.1875
- self_out: bfloat16 [1024, 1024], P('mp', 'dp'), may hold values from -3 to 3
- cross_in: bfloat16 [3, 1024, 1024], P(None, 'dp', 'mp'), may hold values from -0.1875 to 0.1875
- cross_out: bfloat16 [1024, 1024], P('mp', 'dp'), may hold values from -3 to 3
- fc_in: bfloat16 [1024, 4096], P('dp', 'mp'), may hold values from -0.1875 to 0.1875
- fc_out: bfloat16 [4096, 1024], P('mp', 'dp'), may hold values from -0.125 to 0.125
- head_biases: bfloat16 [4, 16, 64], P(None, 'mp', 'dp'), may hold values from -2 to 2
- inner_bias: bfloat16 [16, 256], P('mp', 'dp'), may hold values from -3 to 3
- norm_gains: float32 [3, 1024], P(None, ('dp', 'mp')), may hold values from 0.1 to 1.9
- feature_biases: float32 [6, 1024], P(None, ('dp', 'mp')), may hold values from -0.8 to 0.8
Outputs:
- output: bfloat16 [1024, 32, 1024], P('mp', 'dp')
- grad_tokens: float32 [1024, 32, 1024], P('mp', 'dp')
- grad_memory: float32 [1024, 32, 1024], P('mp', 'dp')
- grad_self_in: float32 [3, 1024, 1024], P(None, 'dp', 'mp')
- grad_self_out: float32 [1024, 1024], P('mp', 'dp')
- grad_cross_in: float32 [3, 1024, 1024], P(None, 'dp', 'mp')
- grad_cross_out: float32 [1024, 1024], P('mp', 'dp')
- grad_fc_in: float32 [1024, 4096], P('dp', 'mp')
- gradient_feedforward_output: float32 [4096, 1024], P('mp', 'dp')
- grad_head_biases: float32 [4, 16, 64], P(None, 'mp', 'dp')
- grad_inner_bias: float32 [16, 256], P('mp', 'dp')
- grad_norm_gains: float32 [3, 1024], P(None, ('dp', 'mp'))
- grad_feature_biases: float32 [6, 1024], P(None, ('dp', 'mp'))
Inputs may be any that keep to these rules, and one draw needn't show every extreme that they name: `lengths`: some sequence has all 1024 positions valid. `memory_lengths`: some sequence has all 1024 memory positions valid.
All inputs are finite; a program needn't handle non-finite values. No bound on the sum of `lengths` or of `memory_lengths` on one device may be relied on, other than what follows from the above.
Results may differ from a plain program's by a relative error of at most 0.033.
Values may be sent and summed in bfloat16 or wider, within the bound.
No kernel may reach another device: no remote copies, remote signals or barrier semaphores. Data moves between devices by JAX's collectives and lax.ppermute only.
A program may use at most 216 MiB of HBM per device.

v0:
```python
from functools import partial

import jax
import jax.numpy as jnp
from jax import lax
from jax.sharding import PartitionSpec as P

eps = 1e-05
floor_score = -1e30


def smooth_unit(values):
    return jax.nn.gelu(values, approximate=True)


def normalize(hidden, gain, shift):
    average = jnp.mean(hidden, -1, keepdims=True)
    centred = hidden - average
    inverse = lax.rsqrt(jnp.mean(centred * centred, -1, keepdims=True) + eps)
    unit = centred * inverse
    return (unit * gain + shift, unit, inverse)


def normalize_back(grad_normed, gain, unit, inverse):
    grad_unit = grad_normed * gain
    grad_hidden = inverse * (
        grad_unit
        - jnp.mean(grad_unit, -1, keepdims=True)
        - unit * jnp.mean(grad_unit * unit, -1, keepdims=True)
    )
    return (grad_hidden, jnp.sum(grad_normed * unit, (0, 1)), jnp.sum(grad_normed, (0, 1)))


def masked_scores(rows, keys, first, limit, causal):
    scores = jnp.einsum("qhd,khd->hqk", rows, keys, preferred_element_type=jnp.float32)
    key_place = jnp.arange(keys.shape[0], dtype=jnp.int32)[None, :]
    if causal:
        allowed = key_place <= first + jnp.arange(rows.shape[0], dtype=jnp.int32)[:, None]
    else:
        allowed = key_place < limit
    return jnp.where(allowed[None], scores, floor_score)


def attend_forward(queries, keys, values, limit, causal):
    length = queries.shape[0]
    block = min(512, length)
    outputs = []
    totals = []
    for first in range(0, length, block):
        span = first + block if causal else keys.shape[0]
        scores = masked_scores(queries[first : first + block], keys[:span], first, limit, causal)
        highest = jnp.max(scores, -1, keepdims=True)
        raised = jnp.exp(scores - highest)
        total = jnp.sum(raised, -1, keepdims=True)
        probs = (raised / total).astype(jnp.bfloat16)
        outputs.append(
            jnp.einsum("hqk,khd->qhd", probs, values[:span], preferred_element_type=jnp.float32)
        )
        totals.append((highest + jnp.log(total))[:, :, 0])
    return (jnp.concatenate(outputs, 0), jnp.concatenate(totals, 1))


def attend_backward(queries, keys, values, totals, grad_mixed, limit, causal):
    length = queries.shape[0]
    block = min(512, length)
    key_grads = jnp.zeros(keys.shape, jnp.float32)
    value_grads = jnp.zeros(values.shape, jnp.float32)
    query_grads = []
    for first in range(0, length, block):
        span = first + block if causal else keys.shape[0]
        rows = queries[first : first + block]
        grad_piece = grad_mixed[first : first + block]
        scores = masked_scores(rows, keys[:span], first, limit, causal)
        probs = jnp.exp(scores - totals[:, first : first + block, None])
        grad_probs = jnp.einsum(
            "qhd,khd->hqk", grad_piece, values[:span], preferred_element_type=jnp.float32
        )
        inner_sum = jnp.sum(probs * grad_probs, -1, keepdims=True)
        grad_scores = (probs * (grad_probs - inner_sum)).astype(jnp.bfloat16)
        query_grads.append(
            jnp.einsum("hqk,khd->qhd", grad_scores, keys[:span], preferred_element_type=jnp.float32)
        )
        key_grads = key_grads.at[:span].add(
            jnp.einsum("hqk,qhd->khd", grad_scores, rows, preferred_element_type=jnp.float32)
        )
        value_grads = value_grads.at[:span].add(
            jnp.einsum(
                "hqk,qhd->khd",
                probs.astype(jnp.bfloat16),
                grad_piece,
                preferred_element_type=jnp.float32,
            )
        )
    return (jnp.concatenate(query_grads, 0), key_grads, value_grads)


def run_forward(operands, causal):
    return attend_forward(operands[0], operands[1], operands[2], operands[3], causal)


def run_backward(operands, causal):
    return attend_backward(
        operands[0], operands[1], operands[2], operands[3], operands[4], operands[5], causal
    )


def gather_rows(normed):
    return lax.all_gather(normed, "mp", axis=0, tiled=True)


def spread_rows(term_fn, rows):
    return lax.psum_scatter(
        term_fn(jnp.int32(0), lax.axis_size("mp") * rows).astype(jnp.bfloat16),
        "mp",
        scatter_dimension=0,
        tiled=True,
    ).astype(jnp.float32)


def whole_rows(term_fn, local, start_row):
    full_rows = local.shape[0] * lax.axis_size("mp")
    term = term_fn(0, full_rows)
    placed = lax.dynamic_update_slice_in_dim(jnp.zeros_like(term), local, start_row, 0)
    return lax.psum((term + placed).astype(jnp.bfloat16), "mp").astype(jnp.float32)


def gather_grads(grad_branch):
    return lax.all_gather(grad_branch, "mp", axis=0, tiled=True)


def reduce_inputs(term_fn, rows):
    return lax.psum_scatter(
        term_fn(jnp.int32(0), lax.axis_size("mp") * rows).astype(jnp.bfloat16),
        "mp",
        scatter_dimension=0,
        tiled=True,
    ).astype(jnp.float32)


def body(
    tokens,
    memory,
    cotangent,
    lengths,
    memory_lengths,
    pair_ids,
    pair_counts,
    self_in,
    self_out,
    cross_in,
    cross_out,
    fc_in,
    fc_out,
    head_biases,
    inner_bias,
    norm_gains,
    feature_biases,
):
    shards = (self_in, self_out, cross_in, cross_out, fc_in, fc_out, head_biases, inner_bias)
    gathered = (
        lax.all_gather(shards[0], "dp", axis=1, tiled=True),
        lax.all_gather(shards[1], "dp", axis=1, tiled=True),
        lax.all_gather(shards[2], "dp", axis=1, tiled=True),
        lax.all_gather(shards[3], "dp", axis=1, tiled=True),
        lax.all_gather(shards[4], "dp", axis=0, tiled=True),
        lax.all_gather(shards[5], "dp", axis=1, tiled=True),
        lax.all_gather(shards[6], "dp", axis=2, tiled=True),
        lax.all_gather(shards[7], "dp", axis=1, tiled=True),
    )
    gains, shifts = (
        lax.all_gather(norm_gains, ("dp", "mp"), axis=1, tiled=True),
        lax.all_gather(feature_biases, ("dp", "mp"), axis=1, tiled=True),
    )
    local_rows, seq_count, width = tokens.shape
    memory_local = memory.shape[0]
    heads_here = head_biases.shape[1]
    head_size = gathered[6].shape[2]
    local_width = heads_here * head_size
    length = local_rows * lax.axis_size("mp")
    memory_length = memory_local * lax.axis_size("mp")
    shape_heads = (seq_count, length, heads_here, head_size)
    shape_memory = (seq_count, memory_length, heads_here, head_size)
    start_row = lax.axis_index("mp") * local_rows
    (
        w_self_in,
        w_self_out,
        w_cross_in,
        w_cross_out,
        feedforward_input_weight,
        feedforward_output_weight,
        w_heads,
        w_inner,
    ) = gathered
    bias_heads = w_heads.astype(jnp.float32).reshape(4, local_width)
    bias_inner = w_inner.astype(jnp.float32).reshape(-1)
    hidden_in = tokens.astype(jnp.float32)
    normed_one, unit_one, inverse_one = normalize(hidden_in, gains[0], shifts[0])
    rows_one = gather_rows(normed_one.astype(jnp.bfloat16))
    project = jnp.einsum("lsd,kde->ksle", rows_one, w_self_in, preferred_element_type=jnp.float32)
    queries_self = ((project[0] + bias_heads[0]) * 0.125).astype(jnp.bfloat16).reshape(shape_heads)
    keys_self = project[1].astype(jnp.bfloat16).reshape(shape_heads)
    values_self = (project[2] + bias_heads[1]).astype(jnp.bfloat16).reshape(shape_heads)
    mixed_self, totals_self = lax.map(
        partial(run_forward, causal=True), (queries_self, keys_self, values_self, lengths)
    )
    mixed_self = mixed_self.astype(jnp.bfloat16).reshape(seq_count, length, local_width)

    def self_term(start, count):
        slice_part = lax.dynamic_slice_in_dim(mixed_self, start, count, 1)
        return jnp.einsum("sle,ed->lsd", slice_part, w_self_out, preferred_element_type=jnp.float32)

    whole_one = whole_rows(self_term, hidden_in, start_row) + shifts[3]
    hidden_one = lax.dynamic_slice_in_dim(whole_one, start_row, local_rows, 0)
    normed_two, unit_two, inverse_two = normalize(hidden_one, gains[1], shifts[1])
    rows_two = normalize(whole_one, gains[1], shifts[1])[0].astype(jnp.bfloat16)
    memory_all = lax.all_gather(memory, "mp", axis=0, tiled=True)
    queries_cross = (
        (
            (
                jnp.einsum(
                    "lsd,de->sle", rows_two, w_cross_in[0], preferred_element_type=jnp.float32
                )
                + bias_heads[2]
            )
            * 0.125
        )
        .astype(jnp.bfloat16)
        .reshape(shape_heads)
    )
    memory_project = jnp.einsum(
        "msd,kde->ksme", memory_all, w_cross_in[1:], preferred_element_type=jnp.float32
    )
    keys_cross = memory_project[0].astype(jnp.bfloat16).reshape(shape_memory)
    values_cross = (memory_project[1] + bias_heads[3]).astype(jnp.bfloat16).reshape(shape_memory)
    mixed_cross, totals_cross = lax.map(
        partial(run_forward, causal=False),
        (queries_cross, keys_cross, values_cross, memory_lengths),
    )
    mixed_cross = mixed_cross.astype(jnp.bfloat16).reshape(seq_count, length, local_width)

    def cross_term(start, count):
        slice_part = lax.dynamic_slice_in_dim(mixed_cross, start, count, 1)
        return jnp.einsum(
            "sle,ed->lsd", slice_part, w_cross_out, preferred_element_type=jnp.float32
        )

    whole_two = whole_rows(cross_term, hidden_one, start_row) + shifts[4]
    hidden_two = lax.dynamic_slice_in_dim(whole_two, start_row, local_rows, 0)
    normed_three, unit_three, inverse_three = normalize(hidden_two, gains[2], shifts[2])
    third_rows = normalize(whole_two, gains[2], shifts[2])[0].astype(jnp.bfloat16)
    inner = (
        jnp.einsum(
            "wri,ix->wrx", third_rows, feedforward_input_weight, preferred_element_type=jnp.float32
        )
        + bias_inner
    )
    smooth_value, smooth_pull = jax.vjp(smooth_unit, inner)
    active_units = smooth_value.astype(jnp.bfloat16)

    def ffn_term(start, count):
        slice_part = lax.dynamic_slice_in_dim(active_units, start, count, 0)
        return jnp.einsum(
            "crx,xp->crp", slice_part, feedforward_output_weight, preferred_element_type=jnp.float32
        )

    output = (hidden_two + spread_rows(ffn_term, local_rows) + shifts[5]).astype(jnp.bfloat16)
    again = (
        lax.all_gather(shards[0], "dp", axis=1, tiled=True),
        lax.all_gather(shards[1], "dp", axis=1, tiled=True),
        lax.all_gather(shards[2], "dp", axis=1, tiled=True),
        lax.all_gather(shards[3], "dp", axis=1, tiled=True),
        lax.all_gather(shards[4], "dp", axis=0, tiled=True),
        lax.all_gather(shards[5], "dp", axis=1, tiled=True),
        lax.all_gather(shards[6], "dp", axis=2, tiled=True),
        lax.all_gather(shards[7], "dp", axis=1, tiled=True),
    )
    (
        w_self_in,
        w_self_out,
        w_cross_in,
        w_cross_out,
        feedforward_input_weight,
        feedforward_output_weight,
        w_heads,
        w_inner,
    ) = again
    counts = pair_counts.astype(jnp.float32)
    matches = (pair_ids[:, None] == jnp.arange(counts.shape[0], dtype=jnp.int32)[None, :]).astype(
        jnp.float32
    )
    own_count = jnp.sum(matches * counts[None, :], -1)
    scale = jnp.mean(counts) / own_count
    positions = start_row + jnp.arange(local_rows, dtype=jnp.int32)
    valid = (positions[:, None] < lengths[None, :]).astype(jnp.float32)
    grad_out = cotangent.astype(jnp.float32) * (valid * scale[None, :])[:, :, None]
    gradient_rows3 = gather_grads(grad_out.astype(jnp.bfloat16))
    gradient_feedforward_output = jnp.einsum(
        "ytb,yth->bh", active_units, gradient_rows3, preferred_element_type=jnp.float32
    )
    grad_active = jnp.einsum(
        "vmr,yr->vmy", gradient_rows3, feedforward_output_weight, preferred_element_type=jnp.float32
    )
    gradient_inner_hidden = smooth_pull(grad_active)[0].astype(jnp.bfloat16)
    grad_fc_in = jnp.einsum(
        "eoc,eoi->ci", third_rows, gradient_inner_hidden, preferred_element_type=jnp.float32
    )
    grad_inner_bias = jnp.sum(gradient_inner_hidden.astype(jnp.float32), (0, 1)).reshape(
        w_inner.shape
    )

    def ffn_back(start, count):
        slice_part = lax.dynamic_slice_in_dim(gradient_inner_hidden, start, count, 0)
        return jnp.einsum(
            "mou,tu->mot", slice_part, feedforward_input_weight, preferred_element_type=jnp.float32
        )

    grad_normed3 = reduce_inputs(ffn_back, local_rows)
    back_three, gain_three, shift_three = normalize_back(
        grad_normed3, gains[2], unit_three, inverse_three
    )
    grad_hidden2 = grad_out + back_three
    grad_rows2 = gather_grads(grad_hidden2.astype(jnp.bfloat16))
    grad_cross_out = jnp.einsum(
        "sle,lsd->ed", mixed_cross, grad_rows2, preferred_element_type=jnp.float32
    )
    grad_mixed = (
        jnp.einsum("lsd,ed->sle", grad_rows2, w_cross_out, preferred_element_type=jnp.float32)
        .astype(jnp.bfloat16)
        .reshape(shape_heads)
    )
    grad_query, grad_key, grad_value = lax.map(
        partial(run_backward, causal=False),
        (queries_cross, keys_cross, values_cross, totals_cross, grad_mixed, memory_lengths),
    )
    grad_query = (grad_query.astype(jnp.bfloat16) * 0.125).reshape(seq_count, length, local_width)
    memory_stack = jnp.stack(
        [
            grad_key.astype(jnp.bfloat16).reshape(seq_count, memory_length, local_width),
            grad_value.astype(jnp.bfloat16).reshape(seq_count, memory_length, local_width),
        ]
    )
    grad_cross_query = jnp.einsum(
        "lsd,sle->de", rows_two, grad_query, preferred_element_type=jnp.float32
    )
    grad_cross_pair = jnp.einsum(
        "msd,ksme->kde", memory_all, memory_stack, preferred_element_type=jnp.float32
    )
    grad_cross_in = jnp.concatenate([grad_cross_query[None], grad_cross_pair], 0)
    bias_query_cross = jnp.sum(grad_query.astype(jnp.float32), (0, 1))
    bias_value_cross = jnp.sum(memory_stack[1].astype(jnp.float32), (0, 1))

    def memory_back(start, count):
        return jnp.einsum(
            "ksme,kde->msd", memory_stack, w_cross_in[1:], preferred_element_type=jnp.float32
        )

    grad_memory = reduce_inputs(memory_back, memory_local)

    def cross_back(start, count):
        slice_part = lax.dynamic_slice_in_dim(grad_query, start, count, 1)
        return jnp.einsum(
            "sle,de->lsd", slice_part, w_cross_in[0], preferred_element_type=jnp.float32
        )

    grad_normed2 = reduce_inputs(cross_back, local_rows)
    back_two, gain_two, shift_two = normalize_back(grad_normed2, gains[1], unit_two, inverse_two)
    grad_hidden1 = grad_hidden2 + back_two
    grad_rows1 = gather_grads(grad_hidden1.astype(jnp.bfloat16))
    grad_self_out = jnp.einsum(
        "sle,lsd->ed", mixed_self, grad_rows1, preferred_element_type=jnp.float32
    )
    grad_mixed = (
        jnp.einsum("lsd,ed->sle", grad_rows1, w_self_out, preferred_element_type=jnp.float32)
        .astype(jnp.bfloat16)
        .reshape(shape_heads)
    )
    grad_query, grad_key, grad_value = lax.map(
        partial(run_backward, causal=True),
        (queries_self, keys_self, values_self, totals_self, grad_mixed, lengths),
    )
    flat_shape = (seq_count, length, local_width)
    self_stack = jnp.stack(
        [
            (grad_query.astype(jnp.bfloat16) * 0.125).reshape(flat_shape),
            grad_key.astype(jnp.bfloat16).reshape(flat_shape),
            grad_value.astype(jnp.bfloat16).reshape(flat_shape),
        ]
    )
    grad_self_in = jnp.einsum(
        "lsd,ksle->kde", rows_one, self_stack, preferred_element_type=jnp.float32
    )
    bias_query_self = jnp.sum(self_stack[0].astype(jnp.float32), (0, 1))
    bias_value_self = jnp.sum(self_stack[2].astype(jnp.float32), (0, 1))

    def self_back(start, count):
        slice_part = lax.dynamic_slice_in_dim(self_stack, start, count, 2)
        return jnp.einsum(
            "ksle,kde->lsd", slice_part, w_self_in, preferred_element_type=jnp.float32
        )

    grad_normed1 = reduce_inputs(self_back, local_rows)
    back_one, gain_one, shift_one = normalize_back(grad_normed1, gains[0], unit_one, inverse_one)
    grad_tokens = grad_hidden1 + back_one
    grad_heads = jnp.stack(
        [bias_query_self, bias_value_self, bias_query_cross, bias_value_cross]
    ).reshape(w_heads.shape)
    gain_grads = jnp.stack([gain_one, gain_two, gain_three])
    shift_grads = jnp.stack(
        [
            shift_one,
            shift_two,
            shift_three,
            jnp.sum(grad_hidden1, (0, 1)),
            jnp.sum(grad_hidden2, (0, 1)),
            jnp.sum(grad_out, (0, 1)),
        ]
    )
    grad_gains, grad_shifts = (
        lax.psum_scatter(gain_grads, ("dp", "mp"), scatter_dimension=1, tiled=True),
        lax.psum_scatter(shift_grads, ("dp", "mp"), scatter_dimension=1, tiled=True),
    )
    all_sums = (
        lax.psum_scatter(
            grad_self_in.astype(jnp.bfloat16), "dp", scatter_dimension=1, tiled=True
        ).astype(jnp.float32),
        lax.psum_scatter(
            grad_self_out.astype(jnp.bfloat16), "dp", scatter_dimension=1, tiled=True
        ).astype(jnp.float32),
        lax.psum_scatter(
            grad_cross_in.astype(jnp.bfloat16), "dp", scatter_dimension=1, tiled=True
        ).astype(jnp.float32),
        lax.psum_scatter(
            grad_cross_out.astype(jnp.bfloat16), "dp", scatter_dimension=1, tiled=True
        ).astype(jnp.float32),
        lax.psum_scatter(
            grad_fc_in.astype(jnp.bfloat16), "dp", scatter_dimension=0, tiled=True
        ).astype(jnp.float32),
        lax.psum_scatter(
            gradient_feedforward_output.astype(jnp.bfloat16), "dp", scatter_dimension=1, tiled=True
        ).astype(jnp.float32),
        lax.psum_scatter(
            grad_heads.astype(jnp.bfloat16), "dp", scatter_dimension=2, tiled=True
        ).astype(jnp.float32),
        lax.psum_scatter(
            grad_inner_bias.astype(jnp.bfloat16), "dp", scatter_dimension=1, tiled=True
        ).astype(jnp.float32),
    )
    (
        sum_self_in,
        sum_self_out,
        sum_cross_in,
        sum_cross_out,
        sum_fc_in,
        sum_fc_out,
        sum_heads,
        sum_inner,
    ) = all_sums
    return (
        output,
        grad_tokens,
        grad_memory,
        sum_self_in,
        sum_self_out,
        sum_cross_in,
        sum_cross_out,
        sum_fc_in,
        sum_fc_out,
        sum_heads,
        sum_inner,
        grad_gains,
        grad_shifts,
    )


def solution(mesh):
    in_specs = (
        P("mp", "dp", None),
        P("mp", "dp", None),
        P("mp", "dp", None),
        P("dp"),
        P("dp"),
        P("dp"),
        P(),
        P(None, "dp", "mp"),
        P("mp", "dp"),
        P(None, "dp", "mp"),
        P("mp", "dp"),
        P("dp", "mp"),
        P("mp", "dp"),
        P(None, "mp", "dp"),
        P("mp", "dp"),
        P(None, ("dp", "mp")),
        P(None, ("dp", "mp")),
    )
    out_specs = (
        P("mp", "dp", None),
        P("mp", "dp", None),
        P("mp", "dp", None),
        P(None, "dp", "mp"),
        P("mp", "dp"),
        P(None, "dp", "mp"),
        P("mp", "dp"),
        P("dp", "mp"),
        P("mp", "dp"),
        P(None, "mp", "dp"),
        P("mp", "dp"),
        P(None, ("dp", "mp")),
        P(None, ("dp", "mp")),
    )
    return jax.shard_map(body, mesh=mesh, in_specs=in_specs, out_specs=out_specs, check_vma=False)
```

profile of v0, /device:TPU:0, one launch (start us, length us, event | category | flops | bytes accessed | tf_op | source)
XLA Modules:
  0.0 2362.2 jit_solution(6198314216845979258)
XLA Ops:
  12.1 70.0 %all-gather = f32[32,32,3]{1,2,0:T(4,128)S(1)} all-gather(f32[1,32,3]{1,2,0:T(4,128)S(1)} %bitcast.645), channel_id=1, replica_groups=mesh['dp'=16,'mp'=2] {'dp','mp'}, dimensions={0}, use_global_device_ids=true | all-gather | bytes 12672 | tf_op jit(solution)/shard_map/all_gather | solution.py:171
  82.8 64.0 %all-gather.1 = f32[32,32,6]{1,2,0:T(8,128)S(1)} all-gather(f32[1,32,6]{1,2,0:T(8,128)S(1)} %bitcast.639), channel_id=1, replica_groups=mesh['dp'=16,'mp'=2] {'dp','mp'}, dimensions={0}, use_global_device_ids=true | all-gather | bytes 25344 | tf_op jit(solution)/shard_map/all_gather | solution.py:172
  173.6 31.0 %all-gather.19.cloned.1.call-done = bf16[1024,2,1024]{2,0,1:T(8,128)(2,1)} async-done(((bf16[512,2,1024]{2,0,1:T(8,128)(2,1)}), bf16[1024,2,1024]{2,0,1:T(8,128)(2,1)}) %all-gather.19.cloned.1.call-update) | async-done | bytes 4194320 | tf_op jit(solution)/shard_map/all_gather | solution.py:108
  204.7 47.4 %all-gather.21.cloned.1.call-done = bf16[3,1024,512]{2,1,0:T(8,128)(2,1)} async-done(((bf16[3,64,512]{2,1,0:T(8,128)(2,1)}), bf16[3,1024,512]{2,1,0:T(8,128)(2,1)}) %all-gather.21.cloned.1.call-update) | async-done | bytes 3145744 | tf_op jit(solution)/shard_map/all_gather | solution.py:161
  275.6 41.3 %while.72 = (s32[]{:T(128)}, bf16[2,1024,8,64]{1,3,2,0:T(8,128)(2,1)}, f32[2,8,1024]{2,1,0:T(8,128)S(1)}, bf16[2,1024,8,64]{1,3,2,0:T(8,128)(2,1)}, bf16[2,1024,...) while((s32[]{:T(128)}, ...), condition=%wide.region_7.8_spmd, body=%wide.region_2.7_spmd.sunk | while | flops 1670119936 | bytes 94706320 | solution.py:203
  329.2 19.5 all-gather.17.cloned.1.call-done
  348.7 47.3 %all-gather.15.cloned.1.call-done = bf16[3,1024,512]{2,1,0:T(8,128)(2,1)} async-done(((bf16[3,64,512]{2,1,0:T(8,128)(2,1)}), bf16[3,1024,512]{2,1,0:T(8,128)(2,1)}) %all-gather.15.cloned.1.call-update) | async-done | bytes 3145744 | tf_op jit(solution)/shard_map/all_gather | solution.py:163
  405.3 100.3 %all-reduce.10.cloned.1.call-done = bf16[1024,2,1024]{2,0,1:T(8,128)(2,1)} async-done(((bf16[1024,2,1024]{2,0,1:T(8,128)(2,1)}), bf16[1024,2,1024]{2,0,1:T(8,128)(2,1)}) %all-reduce.10.cloned.1.call-update) | async-done | bytes 4194320 | tf_op jit(solution)/shard_map/psum | solution.py:124
  521.2 87.3 %while.73 = (s32[]{:T(128)}, bf16[2,1024,8,64]{1,3,2,0:T(8,128)(2,1)}, f32[2,8,1024]{2,1,0:T(8,128)S(1)}, bf16[2,1024,8,64]{1,3,2,0:T(8,128)(2,1)}, s32[2]{0:T(1...) while((s32[]{:T(128)}, ...), condition=%wide.region_16.17_spmd, body=%wide.region_11.16_spmd.sunk | while | flops 2225079296 | bytes 201663232 | solution.py:235
  635.5 21.4 all-gather.2
  657.0 81.6 %all-reduce.12.cloned.1.call-done = bf16[1024,2,1024]{2,0,1:T(8,128)(2,1)} async-done(((bf16[1024,2,1024]{2,0,1:T(8,128)(2,1)}), bf16[1024,2,1024]{2,0,1:T(8,128)(2,1)}) %all-reduce.12.cloned.1.call-update) | async-done | bytes 4194320 | tf_op jit(solution)/shard_map/psum | solution.py:124
  746.9 44.5 %all-gather.27.cloned.1.call-done = bf16[1024,2048]{1,0:T(8,128)(2,1)} async-done(((bf16[64,2048]{1,0:T(8,128)(2,1)}), bf16[1024,2048]{1,0:T(8,128)(2,1)}) %all-gather.27.cloned.1.call-update) | async-done | bytes 4194320 | tf_op jit(solution)/shard_map/all_gather | solution.py:165
  791.4 20.1 multiply_convert_fusion.4
  811.5 37.1 %all-gather.31.cloned.1.call-done = bf16[1024,2,1024]{2,0,1:T(8,128)(2,1)} async-done(((bf16[512,2,1024]{2,0,1:T(8,128)(2,1)}), bf16[1024,2,1024]{2,0,1:T(8,128)(2,1)}) %all-gather.31.cloned.1.call-update) | async-done | bytes 4194320 | tf_op jit(solution)/shard_map/all_gather | solution.py:128
  848.6 52.8 %all-gather.29.cloned.1.call-done = bf16[2048,1024]{0,1:T(8,128)(2,1)} async-done(((bf16[2048,64]{0,1:T(8,128)(2,1)}), bf16[2048,1024]{0,1:T(8,128)(2,1)}) %all-gather.29.cloned.1.call-update) | async-done | bytes 4194320 | tf_op jit(solution)/shard_map/all_gather | solution.py:166
  901.4 24.0 %fusion.234 = (bf16[2048]{0:T(1024)(128)(2,1)}, bf16[1024,2,2048]{2,0,1:T(8,128)(2,1)S(1)}) fusion(f32[1024,2,2048]{2,0,1:T(8,128)} %get-tuple-element.757, f32[2048]{0:T(1024)S(1)} %bitcast.636, bf16[1024,2,1024]{2,0,1:T(8,128)(2,1)} %all-gather.31.cloned.1.call-done, bf16[2048,1024]{0,1:T(8,128)(2,1)} %all-gather.29.cloned.1.call-done), kind=kOutput, calls=%fused_computation.364 | convolution fusion | flops 8682207232 | bytes 33566720 | tf_op jit(solution)/shard_map/vmr,yr->vmy/dot_general | solution.py:300
  958.8 33.6 %reduce-scatter.22.cloned.1.call-done = bf16[512,2,1024]{2,0,1:T(8,128)(2,1)} async-done(((bf16[1024,2,1024]{2,0,1:T(8,128)(2,1)}), bf16[512,2,1024]{2,0,1:T(8,128)(2,1)}) %reduce-scatter.22.cloned.1.call-update) | async-done | bytes 2097168 | tf_op jit(solution)/shard_map/reduce_scatter | solution.py:132
  997.0 52.7 %reduce-scatter.20.cloned.1.call-done = bf16[512,2,1024]{2,0,1:T(8,128)(2,1)} async-done(((bf16[1024,2,1024]{2,0,1:T(8,128)(2,1)}), bf16[512,2,1024]{2,0,1:T(8,128)(2,1)}) %reduce-scatter.20.cloned.1.call-update) | async-done | bytes 2097168 | tf_op jit(solution)/shard_map/reduce_scatter | solution.py:112
  1060.1 56.9 %all-gather.33.cloned.1.call-done = bf16[1024,2,1024]{2,0,1:T(8,128)(2,1)} async-done(((bf16[512,2,1024]{2,0,1:T(8,128)(2,1)}), bf16[1024,2,1024]{2,0,1:T(8,128)(2,1)}) %all-gather.33.cloned.1.call-update) | async-done | bytes 4194320 | tf_op jit(solution)/shard_map/all_gather | solution.py:128
  1127.8 207.8 %while.74 = (s32[]{:T(128)}, bf16[2,1024,8,64]{1,3,2,0:T(8,128)(2,1)}, bf16[2,1024,8,64]{1,3,2,0:T(8,128)(2,1)}, bf16[2,1024,8,64]{1,3,2,0:T(8,128)(2,1)}, bf16[...) while((s32[]{:T(128)}, ...), condition=%wide.region_33.34_spmd, body=%wide.region_30.33_spmd.sunk | while | flops 5472510976 | bytes 487896064 | solution.py:331
  1186.8 28.8 %multiply_convert_fusion.10 = (bf16[8,512,1024]{2,1,0:T(8,128)(2,1)}, bf16[8,512,1024]{2,1,0:T(8,128)(2,1)}) fusion(f32[8,512,1024]{2,1,0:T(8,128)} %get-tuple-element.990, f32[8,512,1024]{2,1,0:T(8,128)} %fusion.331, f32[8,512]{1,0:T(8,128)S(1)} %get-tuple-element.991, f32[8,512]{1,0:T(8,128)S(1)} %get-tuple-element.988, ...), kind=kLoop, calls=%fused_computation.77.clone.1 | loop fusion | flops 41943040 | bytes 83952640 | tf_op jit(solution)/shard_map/while/body/eval_jaxpr/convert_element_type | solution.py:79
  1271.1 19.2 multiply_reduce_fusion.11
  1290.4 28.8 %multiply_convert_fusion.10 = (bf16[8,512,1024]{2,1,0:T(8,128)(2,1)}, bf16[8,512,1024]{2,1,0:T(8,128)(2,1)}) fusion(f32[8,512,1024]{2,1,0:T(8,128)} %get-tuple-element.990, f32[8,512,1024]{2,1,0:T(8,128)} %fusion.331, f32[8,512]{1,0:T(8,128)S(1)} %get-tuple-element.991, f32[8,512]{1,0:T(8,128)S(1)} %get-tuple-element.988, ...), kind=kLoop, calls=%fused_computation.77.clone.1 | loop fusion | flops 41943040 | bytes 83952640 | tf_op jit(solution)/shard_map/while/body/eval_jaxpr/convert_element_type | solution.py:79
  1346.0 53.8 %reduce-scatter.24.cloned.1.call-done = bf16[512,2,1024]{2,0,1:T(8,128)(2,1)} async-done(((bf16[1024,2,1024]{2,0,1:T(8,128)(2,1)}), bf16[512,2,1024]{2,0,1:T(8,128)(2,1)}) %reduce-scatter.24.cloned.1.call-update) | async-done | bytes 2097168 | tf_op jit(solution)/shard_map/reduce_scatter | solution.py:132
  1498.5 127.9 %while.75 = (s32[]{:T(128)}, bf16[2,1024,8,64]{1,3,2,0:T(8,128)(2,1)}, bf16[2,1024,8,64]{1,3,2,0:T(8,128)(2,1)}, bf16[2,1024,8,64]{1,3,2,0:T(8,128)(2,1)}, bf16[...) while((s32[]{:T(128)}, ...), condition=%wide.region_40.41_spmd, body=%wide.region_37.40_spmd.sunk | while | flops 4105953792 | bytes 336376224 | solution.py:377
  1687.6 48.4 %reduce-scatter.32.cloned.1.call-done = bf16[512,64]{0,1:T(8,128)(2,1)} async-done(((bf16[512,1024]{0,1:T(8,128)(2,1)}), bf16[512,64]{0,1:T(8,128)(2,1)}) %reduce-scatter.32.cloned.1.call-update) | async-done | bytes 65552 | tf_op jit(solution)/shard_map/reduce_scatter | solution.py:432
  1737.5 54.8 %reduce-scatter.28.cloned.1.call-done = bf16[512,2,1024]{2,0,1:T(8,128)(2,1)} async-done(((bf16[1024,2,1024]{2,0,1:T(8,128)(2,1)}), bf16[512,2,1024]{2,0,1:T(8,128)(2,1)}) %reduce-scatter.28.cloned.1.call-update) | async-done | bytes 2097168 | tf_op jit(solution)/shard_map/reduce_scatter | solution.py:132
  1800.3 61.5 %all-reduce.4 = bf16[4,8,64]{1,2,0:T(8,128)(2,1)S(1)} all-reduce(bf16[4,8,64]{1,2,0:T(8,128)(2,1)S(1)} %copy.194), channel_id=13, replica_groups=mesh['dp'=16,'mp'=2] {'dp'}, use_global_device_ids=true, to_apply=%region_55.56.clone | all-reduce | flops 2048 | bytes 8192
  1864.0 163.0 %all-reduce.14.cloned.1.call-done = (bf16[3,1024,512]{2,0,1:T(4,128)(2,1)}, bf16[3,1024,512]{2,0,1:T(4,128)(2,1)}) async-done(((bf16[3,1024,512]{2,0,1:T(4,128)(2,1)}, bf16[3,1024,512]{2,0,1:T(4,128)(2,1)}), (bf16[3,1024,512]{2,0,1:T(4,128)(2,1)}, bf16[3,1024,512]{2,0,1:T(4,128)(2,1)})) %all-reduce.14.cloned.1.call-update) | async-done | bytes 6291472
  2030.7 52.5 %reduce-scatter.26.cloned.1.call-done = bf16[512,2,1024]{2,0,1:T(8,128)(2,1)} async-done(((bf16[1024,2,1024]{2,0,1:T(8,128)(2,1)}), bf16[512,2,1024]{2,0,1:T(8,128)(2,1)}) %reduce-scatter.26.cloned.1.call-update) | async-done | bytes 2097168 | tf_op jit(solution)/shard_map/reduce_scatter | solution.py:132
  2098.3 123.6 %reduce-scatter.40.cloned.1.call-done = f32[32,3]{1,0:T(8,128)} async-done(((f32[1024,3]{1,0:T(8,128)}), f32[32,3]{1,0:T(8,128)}) %reduce-scatter.40.cloned.1.call-update) | async-done | bytes 400
  2223.3 130.7 %reduce-scatter.42.cloned.1.call-done = f32[32,6]{1,0:T(8,128)} async-done(((f32[1024,6]{1,0:T(8,128)}), f32[32,6]{1,0:T(8,128)}) %reduce-scatter.42.cloned.1.call-update) | async-done | bytes 784
  (581 shorter events, 772.0 us)
Async XLA Ops:
  7.2 197.5 %all-gather.19.cloned.1.call-start = ((), (), s32[]{:S(2)}) async-start(), calls=%async_computation.14 | async-start | bytes 6291456 | tf_op jit(solution)/shard_map/all_gather | solution.py:108
  149.7 102.4 %all-gather.21.cloned.1.call-start = ((), (), s32[]{:S(2)}) async-start(), calls=%async_computation.15 | async-start | bytes 3342336 | tf_op jit(solution)/shard_map/all_gather | solution.py:161
  150.5 166.5 %all-gather.23.cloned.1.call-start = ((), (), s32[]{:S(2)}) async-start(), calls=%async_computation.16 | async-start | bytes 1114112 | tf_op jit(solution)/shard_map/all_gather | solution.py:162
  151.2 197.5 %all-gather.17.cloned.1.call-start = ((), (), s32[]{:S(2)}) async-start(), calls=%async_computation.13 | async-start | bytes 6291456 | tf_op jit(solution)/shard_map/all_gather | solution.py:216
  154.8 241.2 %all-gather.15.cloned.1.call-start = ((), (), s32[]{:S(2)}) async-start(), calls=%async_computation.12 | async-start | bytes 3342336 | tf_op jit(solution)/shard_map/all_gather | solution.py:163
  155.4 350.2 %all-reduce.10.cloned.1.call-start = ((), (), s32[]{:S(2)}) async-start(), calls=%async_computation.17 | async-start | bytes 8388608 | tf_op jit(solution)/shard_map/psum | solution.py:124
  328.2 283.6 %all-gather.25.cloned.1.call-start = ((), (), s32[]{:S(2)}) async-start(), calls=%async_computation.18 | async-start | bytes 1114112 | tf_op jit(solution)/shard_map/all_gather | solution.py:164
  328.9 409.7 %all-reduce.12.cloned.1.call-start = ((), (), s32[]{:S(2)}) async-start(), calls=%async_computation.19 | async-start | bytes 8388608 | tf_op jit(solution)/shard_map/psum | solution.py:124
  630.5 160.9 %all-gather.27.cloned.1.call-start = ((), (), s32[]{:S(2)}) async-start(), calls=%async_computation.20 | async-start | bytes 4456448 | tf_op jit(solution)/shard_map/all_gather | solution.py:165
  631.2 217.4 %all-gather.31.cloned.1.call-start = ((), (), s32[]{:S(2)}) async-start(), calls=%async_computation.23 | async-start | bytes 6291456 | tf_op jit(solution)/shard_map/all_gather | solution.py:128
  634.7 266.7 %all-gather.29.cloned.1.call-start = ((), (), s32[]{:S(2)}) async-start(), calls=%async_computation.21 | async-start | bytes 4456448 | tf_op jit(solution)/shard_map/all_gather | solution.py:166
  635.4 357.1 %reduce-scatter.22.cloned.1.call-start = ((), (), s32[]{:S(2)}) async-start(), calls=%async_computation.24 | async-start | bytes 6291456 | tf_op jit(solution)/shard_map/reduce_scatter | solution.py:132
  939.5 110.3 %reduce-scatter.20.cloned.1.call-start = ((), (), s32[]{:S(2)}) async-start(), calls=%async_computation.22 | async-start | bytes 6291456 | tf_op jit(solution)/shard_map/reduce_scatter | solution.py:112
  953.5 163.5 %all-gather.33.cloned.1.call-start = ((), (), s32[]{:S(2)}) async-start(), calls=%async_computation.25 | async-start | bytes 6291456 | tf_op jit(solution)/shard_map/all_gather | solution.py:128
  1060.1 339.7 %reduce-scatter.24.cloned.1.call-start = ((), (), s32[]{:S(2)}) async-start(), calls=%async_computation.26 | async-start | bytes 6291456 | tf_op jit(solution)/shard_map/reduce_scatter | solution.py:132
  1345.3 141.3 %all-gather.35.cloned.1.call-start = ((), (), s32[]{:S(2)}) async-start(), calls=%async_computation.27 | async-start | bytes 6291456 | tf_op jit(solution)/shard_map/all_gather | solution.py:128
  1412.1 265.2 %reduce-scatter.38.cloned.1.call-start = ((), (), s32[]{:S(2)}) async-start(), calls=%async_computation.34 | async-start | bytes 69632
  1412.9 265.7 %reduce-scatter.34.cloned.1.call-start = ((), (), s32[]{:S(2)}) async-start(), calls=%async_computation.32 | async-start | bytes 4456448 | tf_op jit(solution)/shard_map/reduce_scatter | solution.py:435
  1428.4 252.0 %reduce-scatter.36.cloned.1.call-start = ((), (), s32[]{:S(2)}) async-start(), calls=%async_computation.33 | async-start | bytes 4456448 | tf_op jit(solution)/shard_map/reduce_scatter | solution.py:438
  1442.7 293.3 %reduce-scatter.32.cloned.1.call-start = ((), (), s32[]{:S(2)}) async-start(), calls=%async_computation.31 | async-start | bytes 1114112 | tf_op jit(solution)/shard_map/reduce_scatter | solution.py:432
  1463.1 329.3 %reduce-scatter.28.cloned.1.call-start = ((), (), s32[]{:S(2)}) async-start(), calls=%async_computation.29 | async-start | bytes 6291456 | tf_op jit(solution)/shard_map/reduce_scatter | solution.py:132
  1486.6 375.9 %reduce-scatter.30.cloned.1.call-start = ((), (), s32[]{:S(2)}) async-start(), calls=%async_computation.30 | async-start | bytes 1114112 | tf_op jit(solution)/shard_map/reduce_scatter | solution.py:426
  1636.0 390.9 %all-reduce.14.cloned.1.call-start = ((), (), s32[]{:S(2)}) async-start(), calls=%async_computation.37 | async-start | bytes 16777216
  1662.3 420.9 %reduce-scatter.26.cloned.1.call-start = ((), (), s32[]{:S(2)}) async-start(), calls=%async_computation.28 | async-start | bytes 6291456 | tf_op jit(solution)/shard_map/reduce_scatter | solution.py:132
  1674.7 547.2 %reduce-scatter.40.cloned.1.call-start = ((), (), s32[]{:S(2)}) async-start(), calls=%async_computation.35 | async-start | bytes 540672
  1798.1 285.2 %copy-start.16 = (bf16[512,2,1024]{2,1,0:T(2,128)(2,1)S(1)}, bf16[512,2,1024]{2,1,0:T(2,128)(2,1)}, u32[]{:S(2)}) copy-start(bf16[512,2,1024]{2,1,0:T(2,128)(2,1)} %param.53) | copy-start | bytes 6291460
  1798.1 285.2 %copy-start.54 = (f32[512,2]{0,1:T(2,128)S(1)}, f32[512,2]{0,1:T(2,128)}, u32[]{:S(2)}) copy-start(f32[512,2]{0,1:T(2,128)} %copy-done.53) | copy-start | bytes 12292
  1798.1 285.2 %copy-start.56 = (f32[512,2]{0,1:T(2,128)S(1)}, f32[512,2]{0,1:T(2,128)}, u32[]{:S(2)}) copy-start(f32[512,2]{0,1:T(2,128)} %copy-done.55) | copy-start | bytes 12292
  1798.1 285.2 %copy-start.60 = (f32[1,1024]{1,0:T(1,128)S(1)}, f32[1,1024]{1,0:T(1,128)}, u32[]{:S(2)}) copy-start(f32[1,1024]{1,0:T(1,128)} %copy-done.59) | copy-start | bytes 12292
  1800.2 286.7 %copy-start.77 = (f32[1024]{0:T(1024)S(1)}, f32[1024]{0:T(1024)}, u32[]{:S(2)}) copy-start(f32[1024]{0:T(1024)} %get-tuple-element.627) | copy-start | bytes 12292
  1800.2 286.7 %copy-start.78 = (f32[1024]{0:T(1024)S(1)}, f32[1024]{0:T(1024)}, u32[]{:S(2)}) copy-start(f32[1024]{0:T(1024)} %get-tuple-element.625) | copy-start | bytes 12292
  2087.9 266.1 %reduce-scatter.42.cloned.1.call-start = ((), (), s32[]{:S(2)}) async-start(), calls=%async_computation.36 | async-start | bytes 540672
  (130 other events, 2214.8 us)
Sparse Core Ops, SparseCore 0:
  149.8 54.7 all-gather.18
  206.9 45.2 all-gather.20
  254.3 36.7 all-gather.22
  293.0 55.6 all-gather.16
  350.8 45.2 all-gather.14
  398.9 106.6 all-reduce.9
  508.0 37.9 all-gather.24
  630.6 107.9 all-reduce.11
  740.8 50.5 all-gather.26
  793.3 55.2 all-gather.30
  850.8 50.5 all-gather.28
  939.6 52.7 reduce-scatter.21
  995.4 54.3 reduce-scatter.19
  1060.2 56.7 all-gather.32
  1345.4 54.2 reduce-scatter.23
  1412.2 56.7 all-gather.34
  1473.1 51.8 reduce-scatter.37
  1528.7 71.3 reduce-scatter.33
  1604.5 71.4 reduce-scatter.35
  1679.5 56.4 reduce-scatter.31
  1739.0 53.2 reduce-scatter.27
  1795.9 57.3 reduce-scatter.29
  1857.6 169.2 all-reduce.13
  2029.1 54.1 reduce-scatter.25
  2088.1 133.7 reduce-scatter.39
  2224.0 129.9 reduce-scatter.41
where the time goes:
time: 2370 us; the launch traced here: 2360 us
  waiting for transfers between devices  1240 us (52%)
  matrix products  519 us (22%)
  blocking collectives  234 us (10%)
  other arithmetic  212 us (9%)
  local copies, waits for them, and re-layouts  138 us (6%)
    unnamed x30, waiting for transfers between devices  422 us
    reduce_scatter x4, waiting for transfers between devices, reduce_inputs(): lax.psum_scatter(term_fn(jnp.int32(0), lax.axis_size('mp') * rows).astype...  195 us
    psum x2, waiting for transfers between devices, whole_rows(): lax.psum((term + placed).astype(jnp.bfloat16), 'mp').astype(jnp.float32)  182 us
    all_gather x3, waiting for transfers between devices, gather_grads(): return lax.all_gather(grad_branch, 'mp', axis=0, tiled=True)  94 us
    dot_general x16, matrix products, masked_scores(): jnp.einsum('qhd,khd->hqk', rows, keys, preferred_element_type=jnp.float32)  93.1 us
    dot_general x8, matrix products, attend_backward(): jnp.einsum('qhd,khd->hqk', grad_piece, values[:span], preferred_element_t...  89.6 us
    convert_element_type x6, other arithmetic, attend_backward(): grad_scores = (probs * (grad_probs - inner_sum)).astype(jnp.bfloat16)  88.6 us
    all_gather x1, blocking collectives, body(): lax.all_gather(norm_gains, ('dp', 'mp'), axis=1, tiled=True)  70 us
  transfers between devices with their start and end apart: 26, of which 19 were waited for; matrix products, arithmetic and copies ran while one was open for 22% of the time, Pallas kernels for 0%

commit v1 on v0

--- a/solution.py
+++ b/solution.py
@@ -3,6 +3,8 @@
 import jax
 import jax.numpy as jnp
 from jax import lax
+from jax.experimental import pallas as pl
+from jax.experimental.pallas import tpu as pltpu
 from jax.sharding import PartitionSpec as P
 
 eps = 1e-05
@@ -472,6 +474,1097 @@
     )
 
 
+LOG2E = 1.4426950408889634
+LN2 = 0.6931471805599453
+VM = pltpu.VMEM
+ANYM = pl.ANY
+F32 = jnp.float32
+BF = jnp.bfloat16
+NT_DIMS = (((1,), (1,)), ((), ()))
+TN_DIMS = (((0,), (0,)), ((), ()))
+
+
+def mm(a, b):
+    return jnp.dot(a, b, preferred_element_type=F32)
+
+
+def mm_nt(a, b):
+    return lax.dot_general(a, b, NT_DIMS, preferred_element_type=F32)
+
+
+def mm_tn(a, b):
+    return lax.dot_general(a, b, TN_DIMS, preferred_element_type=F32)
+
+
+def params_of(limit_mib, **more):
+    return pltpu.CompilerParams(vmem_limit_bytes=limit_mib * 1024 * 1024, **more)
+
+
+def cost(flops, data, exps=0):
+    return pl.CostEstimate(flops=int(flops), bytes_accessed=int(data), transcendentals=int(exps))
+
+
+def flow_meta(kind):
+    if kind == "zxy":
+        quads = [(0, 0), (1, 0), (0, 1), (1, 1)]
+        return [[(k, y, c, x) for k in range(4)] for c in range(2) for (x, y) in quads]
+    quads = [(0, 0), (1, 0), (0, 1), (1, 1)]
+    return [[(k, y, c, x) for (x, y) in quads] for c in range(2) for k in range(4)]
+
+
+def place_of(info, meta):
+    k, y, c, x = meta
+    slab = info[3] if x == 0 else 1 - info[3]
+    zz = lax.rem(info[0] - k + 4, 4)
+    yy = info[1] if y == 0 else 1 - info[1]
+    cc = info[2] if c == 0 else 1 - info[2]
+    return (slab, pl.multiple_of(zz * 256 + yy * 128 + cc * 64, 64))
+
+
+def start_weight(info, pieces, kind, first, width, buffer, sems):
+    for ref, metas in zip(pieces, flow_meta(kind)):
+        for j, meta in enumerate(metas):
+            slab, row = place_of(info, meta)
+            pltpu.make_async_copy(
+                ref.at[j, :, pl.ds(first, width)],
+                buffer.at[slab, pl.ds(row, 64), :],
+                sems.at[slab],
+            ).start()
+
+
+def wait_weight(buffer, sems, slab):
+    pltpu.make_async_copy(buffer.at[slab], buffer.at[slab], sems.at[slab]).wait()
+
+
+def ln_parts(hidden):
+    average = jnp.mean(hidden, -1, keepdims=True)
+    centred = hidden - average
+    inverse = lax.rsqrt(jnp.mean(centred * centred, -1, keepdims=True) + eps)
+    return (centred * inverse, inverse)
+
+
+def ln_back(grad_normed, gain, unit, inverse):
+    grad_unit = grad_normed * gain
+    return inverse * (
+        grad_unit
+        - jnp.mean(grad_unit, -1, keepdims=True)
+        - unit * jnp.mean(grad_unit * unit, -1, keepdims=True)
+    )
+
+
+def row_sum(values):
+    return jnp.sum(values, 0, keepdims=True)
+
+
+def transposed(values):
+    return values.T
+
+
+ROWS = 256
+
+
+def qkv_kernel(info, par, x_ref, *rest):
+    pieces, rest = rest[:24], rest[24:]
+    q_ref, k_ref, v_ref, nt_ref, wq, wk, wv, sems = rest
+    weights = (wq, wk, wv)
+
+    @pl.when(pl.program_id(0) == 0)
+    def _():
+        for t in range(3):
+            start_weight(info, pieces[8 * t : 8 * t + 8], KINDS[t], 0, 512, weights[t], sems.at[t])
+
+    unit, _ = ln_parts(x_ref[...].astype(F32))
+    normed = (unit * par[0:1, :] + par[3:4, :]).astype(BF)
+    nt_ref[...] = transposed(normed)
+    for t in range(3):
+        for slab in range(2):
+
+            @pl.when(pl.program_id(0) == 0)
+            def _():
+                wait_weight(weights[t], sems.at[t], slab)
+
+            cols = slice(slab * 512, slab * 512 + 512)
+            value = mm(normed, weights[t][slab])
+            if t == 0:
+                value = (value + par[9:10, cols]) * (0.125 * LOG2E)
+            if t == 2:
+                value = value + par[10:11, cols]
+            (q_ref, k_ref, v_ref)[t][:, cols] = value.astype(BF)
+
+
+KINDS = ("zxy", "xyz", "zxy")
+
+
+def call_qkv(info, par, x, pieces):
+    n = x.shape[0]
+    out = jax.ShapeDtypeStruct((n, 1024), BF)
+    rows = pl.BlockSpec((ROWS, 1024), lambda i, s: (i, 0))
+    return pl.pallas_call(
+        qkv_kernel,
+        grid_spec=pltpu.PrefetchScalarGridSpec(
+            num_scalar_prefetch=1,
+            grid=(n // ROWS,),
+            in_specs=[pl.BlockSpec((24, 1024), lambda i, s: (0, 0)), rows]
+            + [pl.BlockSpec(memory_space=ANYM)] * 24,
+            out_specs=[rows, rows, rows, pl.BlockSpec((1024, ROWS), lambda i, s: (0, i))],
+            scratch_shapes=[VM((2, 1024, 512), BF)] * 3 + [pltpu.SemaphoreType.DMA((3, 2))],
+        ),
+        out_shape=[out, out, out, jax.ShapeDtypeStruct((1024, n), BF)],
+        compiler_params=params_of(48),
+        cost_estimate=cost(6.4e9, 16e6),
+        name="project_self",
+    )(info, par, x, *pieces)
+
+
+def kv_kernel(info, par, x_ref, *rest):
+    pieces, rest = rest[:8], rest[8:]
+    k_ref, v_ref, nt_ref, wk, wv, sems = rest
+    weights = (wk, wv)
+
+    @pl.when(pl.program_id(0) == 0)
+    def _():
+        for t in range(2):
+            start_weight(info, pieces, "zxy", t * 512, 512, weights[t], sems.at[t])
+
+    rows = x_ref[...]
+    nt_ref[...] = transposed(rows)
+    for t in range(2):
+        for slab in range(2):
+
+            @pl.when(pl.program_id(0) == 0)
+            def _():
+                wait_weight(weights[t], sems.at[t], slab)
+
+            cols = slice(slab * 512, slab * 512 + 512)
+            value = mm(rows, weights[t][slab])
+            if t == 1:
+                value = value + par[12:13, cols]
+            (k_ref, v_ref)[t][:, cols] = value.astype(BF)
+
+
+def call_kv(info, par, x, pieces):
+    n = x.shape[0]
+    out = jax.ShapeDtypeStruct((n, 1024), BF)
+    rows = pl.BlockSpec((ROWS, 1024), lambda i, s: (i, 0))
+    return pl.pallas_call(
+        kv_kernel,
+        grid_spec=pltpu.PrefetchScalarGridSpec(
+            num_scalar_prefetch=1,
+            grid=(n // ROWS,),
+            in_specs=[pl.BlockSpec((24, 1024), lambda i, s: (0, 0)), rows]
+            + [pl.BlockSpec(memory_space=ANYM)] * 8,
+            out_specs=[rows, rows, pl.BlockSpec((1024, ROWS), lambda i, s: (0, i))],
+            scratch_shapes=[VM((2, 1024, 512), BF)] * 2 + [pltpu.SemaphoreType.DMA((2, 2))],
+        ),
+        out_shape=[out, out, jax.ShapeDtypeStruct((1024, n), BF)],
+        compiler_params=params_of(48),
+        cost_estimate=cost(4.3e9, 12e6),
+        name="project_memory",
+    )(info, par, x, *pieces)
+
+
+def lane_ids(rows):
+    return lax.broadcasted_iota(jnp.int32, (rows, 128), 1)
+
+
+def split3(column):
+    high = column.astype(BF)
+    rest = column - high.astype(F32)
+    middle = rest.astype(BF)
+    return (high, middle, (rest - middle.astype(F32)).astype(BF))
+
+
+def attend_kernel(causal, info, q_ref, k_ref, v_ref, o_ref, lse_ref):
+    n, nk = q_ref.shape[0], k_ref.shape[0]
+    pair = pl.program_id(0)
+    lanes_k, lanes_q = lane_ids(nk), lane_ids(ROWS)
+    lane_all = lane_ids(n)
+
+    @pl.when(pair == 0)
+    def _():
+        lse_ref[...] = jnp.zeros(lse_ref.shape, F32)
+
+    one = jnp.ones((), BF)
+    zero = jnp.zeros((), BF)
+    k_aug, v_aug = [], []
+    for head in range(2):
+        own = (lanes_k >= 64) if head else (lanes_k < 64)
+        spare = 0 if head else 64
+        keys = jnp.where(own, k_ref[...], zero)
+        if not causal:
+            place = lax.broadcasted_iota(jnp.int32, (nk, 128), 0)
+            shut = jnp.where(place < info[4], 0.0, floor_score).astype(BF)
+            keys = jnp.where(lanes_k == spare, shut, keys)
+        k_aug.append(keys)
+        v_aug.append(jnp.where(own, v_ref[...], jnp.where(lanes_k == spare, one, zero)))
+    for first in range(0, n, ROWS):
+        span = first + ROWS if causal else nk
+        block = q_ref[first : first + ROWS, :]
+        outs, lses = [], []
+        for head in range(2):
+            spare = 0 if head else 64
+            query = block if causal else jnp.where(lanes_q == spare, one, block)
+            scores = mm_nt(query, k_aug[head][:span])
+            if causal:
+                row = lax.broadcasted_iota(jnp.int32, (ROWS, ROWS), 0)
+                col = lax.broadcasted_iota(jnp.int32, (ROWS, ROWS), 1)
+                last = jnp.where(col <= row, scores[:, first:], floor_score)
+                scores = jnp.concatenate([scores[:, :first], last], 1) if first else last
+            highest = jnp.max(scores, -1, keepdims=True)
+            raised = jnp.exp2(scores - highest).astype(BF)
+            mixed = mm(raised, v_aug[head][:span])
+            total = jnp.sum(jnp.where(lanes_q == spare, mixed, 0.0), -1, keepdims=True)
+            outs.append(mixed * (1.0 / total))
+            lses.append(highest + jnp.log2(total))
+        o_ref[first : first + ROWS, :] = jnp.where(lanes_q < 64, outs[0], outs[1]).astype(BF)
+        held = lse_ref[first : first + ROWS, :]
+        held = jnp.where(lanes_q == 2 * pair, lses[0], held)
+        lse_ref[first : first + ROWS, :] = jnp.where(lanes_q == 2 * pair + 1, lses[1], held)
+
+
+def call_attend(info, q, k, v, causal):
+    n, nk = q.shape[0], k.shape[0]
+    part = 0.625 if causal else 1.0
+    heads = lambda rows: pl.BlockSpec((rows, 128), lambda i, s: (0, i))
+    return pl.pallas_call(
+        partial(attend_kernel, causal),
+        grid_spec=pltpu.PrefetchScalarGridSpec(
+            num_scalar_prefetch=1,
+            grid=(q.shape[1] // 128,),
+            in_specs=[heads(n), heads(nk), heads(nk)],
+            out_specs=[heads(n), pl.BlockSpec((n, 128), lambda i, s: (0, 0))],
+        ),
+        out_shape=[jax.ShapeDtypeStruct((n, 1024), BF), jax.ShapeDtypeStruct((n, 128), F32)],
+        compiler_params=params_of(48),
+        cost_estimate=cost(16e9 * part, 9e6, 17e6 * part),
+        name="attend_self" if causal else "attend_cross",
+    )(info, q, k, v)
+
+
+def attend_back_kernel(causal, info, q_ref, k_ref, v_ref, o_ref, g_ref, lse_ref, dq_ref, dk_ref, dv_ref, bias_ref, acc):
+    n, nk = q_ref.shape[0], k_ref.shape[0]
+    pair = pl.program_id(0)
+    lanes_k, lanes_q = lane_ids(nk), lane_ids(n)
+    one = jnp.ones((), BF)
+    zero = jnp.zeros((), BF)
+    block_rows = 256
+    q_all, g_all = q_ref[...], g_ref[...]
+    product = g_all.astype(F32) * o_ref[...].astype(F32)
+    sets = []
+    for head in range(2):
+        own_k = (lanes_k >= 64) if head else (lanes_k < 64)
+        own_q = (lanes_q >= 64) if head else (lanes_q < 64)
+        at = 0 if head else 64
+        inner = jnp.sum(jnp.where(own_q, product, 0.0), -1, keepdims=True)
+        lse = jnp.sum(jnp.where(lanes_q == 2 * pair + head, lse_ref[...], 0.0), -1, keepdims=True)
+        q_own = jnp.where(own_q, q_all, zero)
+        g_own = jnp.where(own_q, g_all, zero)
+        q_aug, g_aug = q_own, g_own
+        for step, (part_q, part_g) in enumerate(zip(split3(-lse), split3(-inner))):
+            q_aug = jnp.where(lanes_q == at + step, part_q, q_aug)
+            g_aug = jnp.where(lanes_q == at + step, part_g, g_aug)
+        q_aug = jnp.where(lanes_q == at + 3, one, q_aug)
+        ones_k = (lanes_k >= at) & (lanes_k < at + 3)
+        k_own = jnp.where(own_k, k_ref[...], zero)
+        k_aug = jnp.where(ones_k, one, k_own)
+        if not causal:
+            place = lax.broadcasted_iota(jnp.int32, (nk, 128), 0)
+            shut = jnp.where(place < info[4], 0.0, floor_score).astype(BF)
+            k_aug = jnp.where(lanes_k == at + 3, shut, k_aug)
+        v_aug = jnp.where(ones_k, one, jnp.where(own_k, v_ref[...], zero))
+        sets.append((q_own, g_own, q_aug, g_aug, k_own, k_aug, v_aug))
+    for first in range(0, nk, block_rows):
+        from_q = first if causal else 0
+        dv = dk = None
+        dq = None
+        for head in range(2):
+            q_own, g_own, q_aug, g_aug, k_own, k_aug, v_aug = sets[head]
+            keys = slice(first, first + block_rows)
+            scores = mm_nt(k_aug[keys], q_aug[from_q:])
+            if causal:
+                row = lax.broadcasted_iota(jnp.int32, (block_rows, block_rows), 0)
+                col = lax.broadcasted_iota(jnp.int32, (block_rows, block_rows), 1)
+                head_part = jnp.where(col >= row, scores[:, :block_rows], floor_score)
+                if first + block_rows < n:
+                    scores = jnp.concatenate([head_part, scores[:, block_rows:]], 1)
+                else:
+                    scores = head_part
+            probs = jnp.exp2(scores)
+            grad_probs = mm_nt(v_aug[keys], g_aug[from_q:])
+            grad_scores = (probs * grad_probs).astype(BF)
+            add_v = mm(probs.astype(BF), g_own[from_q:])
+            add_k = mm(grad_scores, q_own[from_q:])
+            add_q = mm_tn(grad_scores, k_own[keys])
+            dv = add_v if dv is None else dv + add_v
+            dk = add_k if dk is None else dk + add_k
+            dq = add_q if dq is None else dq + add_q
+        dv = dv.astype(BF)
+        dv_ref[first : first + block_rows, :] = dv
+        dk_ref[first : first + block_rows, :] = (dk * LN2).astype(BF)
+        sums = row_sum(dv.astype(F32))
+        if first == 0:
+            acc[...] = dq
+            bias_ref[1:2, :] = sums
+        else:
+            acc[from_q:, :] += dq
+            bias_ref[1:2, :] += sums
+    dq = acc[...].astype(BF) * jnp.asarray(0.125, BF)
+    dq_ref[...] = dq
+    bias_ref[0:1, :] = row_sum(dq.astype(F32))
+
+
+def call_attend_back(info, q, k, v, o, g, lse, causal):
+    n, nk = q.shape[0], k.shape[0]
+    part = 0.625 if causal else 1.0
+    heads = lambda rows: pl.BlockSpec((rows, 128), lambda i, s: (0, i))
+    out = lambda rows: jax.ShapeDtypeStruct((rows, 1024), BF)
+    return pl.pallas_call(
+        partial(attend_back_kernel, causal),
+        grid_spec=pltpu.PrefetchScalarGridSpec(
+            num_scalar_prefetch=1,
+            grid=(q.shape[1] // 128,),
+            in_specs=[heads(n), heads(nk), heads(nk), heads(n), heads(n), pl.BlockSpec((n, 128), lambda i, s: (0, 0))],
+            out_specs=[heads(n), heads(nk), heads(nk), heads(8)],
+            scratch_shapes=[VM((n, 128), F32)],
+        ),
+        out_shape=[out(n), out(nk), out(nk), jax.ShapeDtypeStruct((8, 1024), F32)],
+        compiler_params=params_of(56),
+        cost_estimate=cost(40e9 * part, 20e6, 17e6 * part),
+        name="attend_back_self" if causal else "attend_back_cross",
+    )(info, q, k, v, o, g, lse)
+
+
+def after_self_kernel(info, par, x_ref, o_ref, *rest):
+    pieces, rest = rest[:8], rest[8:]
+    h_ref, q_ref, nt_ref, wo, wq, sems = rest
+
+    @pl.when(pl.program_id(0) == 0)
+    def _():
+        start_weight(info, pieces, "zxy", 1024, 512, wo, sems.at[0])
+        start_weight(info, pieces, "zxy", 1536, 512, wq, sems.at[1])
+
+    total = x_ref[...].astype(F32) + par[6:7, :]
+    for slab in range(2):
+
+        @pl.when(pl.program_id(0) == 0)
+        def _():
+            wait_weight(wo, sems.at[0], slab)
+
+        total = total + mm_nt(o_ref[:, slab * 512 : slab * 512 + 512], wo[slab])
+    h_ref[...] = total
+    unit, _ = ln_parts(total)
+    normed = (unit * par[1:2, :] + par[4:5, :]).astype(BF)
+    nt_ref[...] = transposed(normed)
+    for slab in range(2):
+
+        @pl.when(pl.program_id(0) == 0)
+        def _():
+            wait_weight(wq, sems.at[1], slab)
+
+        cols = slice(slab * 512, slab * 512 + 512)
+        value = (mm(normed, wq[slab]) + par[11:12, cols]) * (0.125 * LOG2E)
+        q_ref[:, cols] = value.astype(BF)
+
+
+def call_after_self(info, par, x, o, pieces):
+    n = x.shape[0]
+    rows = pl.BlockSpec((ROWS, 1024), lambda i, s: (i, 0))
+    return pl.pallas_call(
+        after_self_kernel,
+        grid_spec=pltpu.PrefetchScalarGridSpec(
+            num_scalar_prefetch=1,
+            grid=(n // ROWS,),
+            in_specs=[pl.BlockSpec((24, 1024), lambda i, s: (0, 0)), rows, rows]
+            + [pl.BlockSpec(memory_space=ANYM)] * 8,
+            out_specs=[rows, rows, pl.BlockSpec((1024, ROWS), lambda i, s: (0, i))],
+            scratch_shapes=[VM((2, 1024, 512), BF)] * 2 + [pltpu.SemaphoreType.DMA((2, 2))],
+        ),
+        out_shape=[
+            jax.ShapeDtypeStruct((n, 1024), F32),
+            jax.ShapeDtypeStruct((n, 1024), BF),
+            jax.ShapeDtypeStruct((1024, n), BF),
+        ],
+        compiler_params=params_of(48),
+        cost_estimate=cost(4.3e9, 16e6),
+        name="after_self",
+    )(info, par, x, o, *pieces)
+
+
+def after_cross_kernel(info, par, scale, h_in, o_ref, cot_ref, *rest):
+    pieces, rest = rest[:8], rest[8:]
+    h_ref, n_ref, nt_ref, g_ref, gt_ref, gsum_ref, wo, sems = rest
+    step = pl.program_id(0)
+
+    @pl.when(step == 0)
+    def _():
+        start_weight(info, pieces, "zxy", 2048, 512, wo, sems)
+
+    place = step * ROWS + lax.broadcasted_iota(jnp.int32, (ROWS, 1), 0)
+    weight = jnp.where(place < info[5], scale[0, 0], 0.0)
+    grad = cot_ref[...].astype(F32) * weight
+    rounded = grad.astype(BF)
+    g_ref[...] = rounded
+    gt_ref[...] = transposed(rounded)
+    sums = row_sum(grad)
+
+    @pl.when(step == 0)
+    def _():
+        gsum_ref[...] = jnp.zeros(gsum_ref.shape, F32)
+
+    gsum_ref[0:1, :] += sums
+    total = h_in[...] + par[7:8, :]
+    for slab in range(2):
+
+        @pl.when(step == 0)
+        def _():
+            wait_weight(wo, sems, slab)
+
+        total = total + mm_nt(o_ref[:, slab * 512 : slab * 512 + 512], wo[slab])
+    h_ref[...] = total
+    unit, _ = ln_parts(total)
+    normed = (unit * par[2:3, :] + par[5:6, :]).astype(BF)
+    n_ref[...] = normed
+    nt_ref[...] = transposed(normed)
+
+
+def call_after_cross(info, par, scale, h, o, cot, pieces):
+    n = h.shape[0]
+    rows = pl.BlockSpec((ROWS, 1024), lambda i, s: (i, 0))
+    turned = pl.BlockSpec((1024, ROWS), lambda i, s: (0, i))
+    act = jax.ShapeDtypeStruct((n, 1024), BF)
+    act_t = jax.ShapeDtypeStruct((1024, n), BF)
+    return pl.pallas_call(
+        after_cross_kernel,
+        grid_spec=pltpu.PrefetchScalarGridSpec(
+            num_scalar_prefetch=1,
+            grid=(n // ROWS,),
+            in_specs=[
+                pl.BlockSpec((24, 1024), lambda i, s: (0, 0)),
+                pl.BlockSpec((8, 128), lambda i, s: (0, 0)),
+                rows,
+                rows,
+                rows,
+            ]
+            + [pl.BlockSpec(memory_space=ANYM)] * 8,
+            out_specs=[rows, rows, turned, rows, turned, pl.BlockSpec((8, 1024), lambda i, s: (0, 0))],
+            scratch_shapes=[VM((2, 1024, 512), BF), pltpu.SemaphoreType.DMA((2,))],
+        ),
+        out_shape=[
+            jax.ShapeDtypeStruct((n, 1024), F32),
+            act,
+            act_t,
+            act,
+            act_t,
+            jax.ShapeDtypeStruct((8, 1024), F32),
+        ],
+        compiler_params=params_of(48),
+        cost_estimate=cost(2.2e9, 26e6),
+        name="after_cross",
+    )(info, par, scale, h, o, cot, *pieces)
+
+
+GELU_A = 0.7978845608028654
+GELU_B = 0.044715
+
+
+def store_blocks(info, temp, send_ref, keep_ref, zrel, kind, width):
+    for yrel in range(2):
+        yy = info[1] if yrel == 0 else 1 - info[1]
+        for crel in range(2):
+            cc = info[2] if crel == 0 else 1 - info[2]
+            row = pl.multiple_of(yy * 128 + cc * 64, 64)
+            block = temp[pl.ds(row, 64), :]
+            target = send_ref if crel else keep_ref
+            if kind == "zxy":
+                target[yrel, 0, zrel, :, :] = block
+            else:
+                target[zrel, yrel, 0, :, :] = block
+
+
+FFB = 512
+
+
+def ffn_kernel(info, par, bias_ref, n_ref, nt_ref, g_ref, gt_ref, h_ref, *rest):
+    pieces_in, pieces_out, rest = rest[:8], rest[8:16], rest[16:]
+    (out_ref, dn_ref, send_in, keep_in, send_out, keep_out, dbias_ref, w_in, w_out, acc, active, du, temp, sems) = rest
+    half, part = pl.program_id(0), pl.program_id(1)
+    parts = pl.num_programs(1)
+    n = n_ref.shape[0]
+    slab = lax.rem(half + info[3], 2)
+    first_step = (half == 0) & (part == 0)
+
+    @pl.when(first_step)
+    def _():
+        start_weight(info, pieces_in, "zxy", 0, 2048, w_in, sems.at[0])
+        start_weight(info, pieces_out, "xyz", 0, 2048, w_out, sems.at[1])
+
+    @pl.when(part == 0)
+    def _():
+        wait_weight(w_in, sems.at[0], slab)
+        wait_weight(w_out, sems.at[1], slab)
+
+    cols = pl.ds(pl.multiple_of(part * FFB, FFB), FFB)
+    first = w_in.at[slab, :, cols]
+    second = w_out.at[slab, :, cols]
+    total_bias = None
+    for chunk in range(n // ROWS):
+        rows = slice(chunk * ROWS, chunk * ROWS + ROWS)
+        u = mm(n_ref[rows, :], first[...]) + bias_ref[0:1, :]
+        square = u * u
+        bend = jnp.tanh(u * (GELU_A + GELU_A * GELU_B * square))
+        half_up = 0.5 + 0.5 * bend
+        r = (u * half_up).astype(BF)
+        active[rows, :] = r
+        slope = half_up + 0.5 * u * (1.0 - bend * bend) * (GELU_A + 3.0 * GELU_A * GELU_B * square)
+        dr = mm(g_ref[rows, :], second[...])
+        d = (dr * slope).astype(BF)
+        du[rows, :] = d
+        sums = row_sum(d.astype(F32))
+        total_bias = sums if total_bias is None else total_bias + sums
+        up = mm_nt(r, second[...])
+        down = mm_nt(d, first[...])
+
+        @pl.when(first_step)
+        def _():
+            acc[rows, :] = up
+            dn_ref[rows, :] = down
+
+        @pl.when(jnp.logical_not(first_step))
+        def _():
+            acc[rows, :] += up
+            dn_ref[rows, :] += down
+
+    dbias_ref[0:1, :] = total_bias
+    for zrel in range(4):
+        zz = lax.rem(info[0] + zrel, 4)
+        rows = pl.ds(pl.multiple_of(zz * 256, 256), 256)
+        temp[...] = mm(nt_ref[rows, :], du[...]).astype(BF)
+        store_blocks(info, temp, send_in, keep_in, zrel, "zxy", FFB)
+        temp[...] = mm(gt_ref[rows, :], active[...]).astype(BF)
+        store_blocks(info, temp, send_out, keep_out, zrel, "xyz", FFB)
+
+    @pl.when((half == 1) & (part == parts - 1))
+    def _():
+        for chunk in range(n // ROWS):
+            rows = slice(chunk * ROWS, chunk * ROWS + ROWS)
+            out_ref[rows, :] = (h_ref[rows, :] + acc[rows, :] + par[8:9, :]).astype(BF)
+
+
+def block_out(kind, width, total):
+    if kind == "zxy":
+        shape, block = (2, 2, 4, 64, total), (2, 1, 4, 64, width)
+        spec = lambda index: pl.BlockSpec(block, index(lambda x, t: (0, x, 0, 0, t)))
+    else:
+        shape, block = (4, 2, 2, 64, total), (4, 2, 1, 64, width)
+        spec = lambda index: pl.BlockSpec(block, index(lambda x, t: (0, 0, x, 0, t)))
+    return (jax.ShapeDtypeStruct(shape, BF), spec)
+
+
+def call_ffn(info, par, bias, normed, normed_t, grad, grad_t, hidden, pieces_in, pieces_out):
+    n = normed.shape[0]
+    parts = 2048 // FFB
+    whole = lambda shape: pl.BlockSpec(shape, lambda x, t, s: (0, 0))
+    shape_in, spec_in = block_out("zxy", FFB, 2048)
+    shape_out, spec_out = block_out("xyz", FFB, 2048)
+    index = lambda f: (lambda x, t, s: f(x, t))
+    bias_spec = lambda rows: pl.BlockSpec((rows, FFB), lambda x, t, s: (0, lax.rem(x + s[3], 2) * parts + t))
+    return pl.pallas_call(
+        ffn_kernel,
+        grid_spec=pltpu.PrefetchScalarGridSpec(
+            num_scalar_prefetch=1,
+            grid=(2, parts),
+            in_specs=[
+                whole((24, 1024)),
+                bias_spec(8),
+                whole((n, 1024)),
+                whole((1024, n)),
+                whole((n, 1024)),
+                whole((1024, n)),
+                whole((n, 1024)),
+            ]
+            + [pl.BlockSpec(memory_space=ANYM)] * 16,
+            out_specs=[
+                whole((n, 1024)),
+                whole((n, 1024)),
+                spec_in(index),
+                spec_in(index),
+                spec_out(index),
+                spec_out(index),
+                bias_spec(8),
+            ],
+            scratch_shapes=[
+                VM((2, 1024, 2048), BF),
+                VM((2, 1024, 2048), BF),
+                VM((n, 1024), F32),
+                VM((n, FFB), BF),
+                VM((n, FFB), BF),
+                VM((256, FFB), BF),
+                pltpu.SemaphoreType.DMA((2, 2)),
+            ],
+        ),
+        out_shape=[
+            jax.ShapeDtypeStruct((n, 1024), BF),
+            jax.ShapeDtypeStruct((n, 1024), F32),
+            shape_in,
+            shape_in,
+            shape_out,
+            shape_out,
+            jax.ShapeDtypeStruct((8, 4096), F32),
+        ],
+        compiler_params=params_of(60),
+        cost_estimate=cost(51.5e9, 60e6, 4e6),
+        name="feedforward",
+    )(info, par, bias, normed, normed_t, grad, grad_t, hidden, *pieces_in, *pieces_out)
+
+
+def back_three_kernel(info, par, dn_ref, h_ref, g_ref, *rest):
+    pieces, rest = rest[:8], rest[8:]
+    dh_ref, do_ref, gt_ref, sum_ref, wo, sems = rest
+    step = pl.program_id(0)
+
+    @pl.when(step == 0)
+    def _():
+        start_weight(info, pieces, "zxy", 2048, 512, wo, sems)
+        sum_ref[...] = jnp.zeros(sum_ref.shape, F32)
+
+    back_rows(par, 2, dn_ref[...], h_ref[...], g_ref[...].astype(F32), dh_ref, gt_ref, sum_ref, do_ref, wo, sems)
+
+
+def back_rows(par, index, dn, hidden, residual, dh_ref, gt_ref, sum_ref, do_ref, wo, sems):
+    unit, inverse = ln_parts(hidden)
+    grad = residual + ln_back(dn, par[index : index + 1, :], unit, inverse)
+    dh_ref[...] = grad
+    sum_ref[0:1, :] += row_sum(dn * unit)
+    sum_ref[1:2, :] += row_sum(dn)
+    sum_ref[2:3, :] += row_sum(grad)
+    rounded = grad.astype(BF)
+    gt_ref[...] = transposed(rounded)
+    for slab in range(2):
+
+        @pl.when(pl.program_id(0) == 0)
+        def _():
+            wait_weight(wo, sems, slab)
+
+        do_ref[:, slab * 512 : slab * 512 + 512] = mm(rounded, wo[slab]).astype(BF)
+
+
+def call_back_three(info, par, dn, h, g, pieces):
+    n = h.shape[0]
+    rows = pl.BlockSpec((ROWS, 1024), lambda i, s: (i, 0))
+    return pl.pallas_call(
+        back_three_kernel,
+        grid_spec=pltpu.PrefetchScalarGridSpec(
+            num_scalar_prefetch=1,
+            grid=(n // ROWS,),
+            in_specs=[pl.BlockSpec((24, 1024), lambda i, s: (0, 0)), rows, rows, rows]
+            + [pl.BlockSpec(memory_space=ANYM)] * 8,
+            out_specs=[
+                rows,
+                rows,
+                pl.BlockSpec((1024, ROWS), lambda i, s: (0, i)),
+                pl.BlockSpec((8, 1024), lambda i, s: (0, 0)),
+            ],
+            scratch_shapes=[VM((2, 1024, 512), BF), pltpu.SemaphoreType.DMA((2,))],
+        ),
+        out_shape=[
+            jax.ShapeDtypeStruct((n, 1024), F32),
+            jax.ShapeDtypeStruct((n, 1024), BF),
+            jax.ShapeDtypeStruct((1024, n), BF),
+            jax.ShapeDtypeStruct((8, 1024), F32),
+        ],
+        compiler_params=params_of(48),
+        cost_estimate=cost(2.2e9, 20e6),
+        name="back_three",
+    )(info, par, dn, h, g, *pieces)
+
+
+def back_two_kernel(info, par, dq_ref, h_ref, dh2_ref, *rest):
+    pieces, rest = rest[:8], rest[8:]
+    dh_ref, do_ref, gt_ref, sum_ref, wq, wo, sems = rest
+    step = pl.program_id(0)
+
+    @pl.when(step == 0)
+    def _():
+        start_weight(info, pieces, "zxy", 1536, 512, wq, sems.at[0])
+        start_weight(info, pieces, "zxy", 1024, 512, wo, sems.at[1])
+        sum_ref[...] = jnp.zeros(sum_ref.shape, F32)
+
+    dn = None
+    for slab in range(2):
+
+        @pl.when(step == 0)
+        def _():
+            wait_weight(wq, sems.at[0], slab)
+
+        term = mm_nt(dq_ref[:, slab * 512 : slab * 512 + 512], wq[slab])
+        dn = term if dn is None else dn + term
+    back_rows(par, 1, dn, h_ref[...], dh2_ref[...], dh_ref, gt_ref, sum_ref, do_ref, wo, sems.at[1])
+
+
+def call_back_two(info, par, dq, h, dh2, pieces):
+    n = h.shape[0]
+    rows = pl.BlockSpec((ROWS, 1024), lambda i, s: (i, 0))
+    return pl.pallas_call(
+        back_two_kernel,
+        grid_spec=pltpu.PrefetchScalarGridSpec(
+            num_scalar_prefetch=1,
+            grid=(n // ROWS,),
+            in_specs=[pl.BlockSpec((24, 1024), lambda i, s: (0, 0)), rows, rows, rows]
+            + [pl.BlockSpec(memory_space=ANYM)] * 8,
+            out_specs=[
+                rows,
+                rows,
+                pl.BlockSpec((1024, ROWS), lambda i, s: (0, i)),
+                pl.BlockSpec((8, 1024), lambda i, s: (0, 0)),
+            ],
+            scratch_shapes=[VM((2, 1024, 512), BF)] * 2 + [pltpu.SemaphoreType.DMA((2, 2))],
+        ),
+        out_shape=[
+            jax.ShapeDtypeStruct((n, 1024), F32),
+            jax.ShapeDtypeStruct((n, 1024), BF),
+            jax.ShapeDtypeStruct((1024, n), BF),
+            jax.ShapeDtypeStruct((8, 1024), F32),
+        ],
+        compiler_params=params_of(48),
+        cost_estimate=cost(4.3e9, 24e6),
+        name="back_two",
+    )(info, par, dq, h, dh2, *pieces)
+
+
+def memory_back_kernel(info, dk_ref, dv_ref, *rest):
+    pieces, rest = rest[:8], rest[8:]
+    out_ref, wk, wv, sems = rest
+
+    @pl.when(pl.program_id(0) == 0)
+    def _():
+        start_weight(info, pieces, "zxy", 0, 512, wk, sems.at[0])
+        start_weight(info, pieces, "zxy", 512, 512, wv, sems.at[1])
+
+    total = None
+    for t, (ref, weight) in enumerate(((dk_ref, wk), (dv_ref, wv))):
+        for slab in range(2):
+
+            @pl.when(pl.program_id(0) == 0)
+            def _():
+                wait_weight(weight, sems.at[t], slab)
+
+            term = mm_nt(ref[:, slab * 512 : slab * 512 + 512], weight[slab])
+            total = term if total is None else total + term
+    out_ref[...] = total.astype(BF)
+
+
+def call_memory_back(info, dk, dv, pieces):
+    n = dk.shape[0]
+    rows = pl.BlockSpec((ROWS, 1024), lambda i, s: (i, 0))
+    return pl.pallas_call(
+        memory_back_kernel,
+        grid_spec=pltpu.PrefetchScalarGridSpec(
+            num_scalar_prefetch=1,
+            grid=(n // ROWS,),
+            in_specs=[rows, rows] + [pl.BlockSpec(memory_space=ANYM)] * 8,
+            out_specs=rows,
+            scratch_shapes=[VM((2, 1024, 512), BF)] * 2 + [pltpu.SemaphoreType.DMA((2, 2))],
+        ),
+        out_shape=jax.ShapeDtypeStruct((n, 1024), BF),
+        compiler_params=params_of(48),
+        cost_estimate=cost(4.3e9, 12e6),
+        name="memory_back",
+    )(info, dk, dv, *pieces)
+
+
+def back_one_kernel(info, par, dq_ref, dk_ref, dv_ref, x_ref, dh1_ref, *rest):
+    pieces, rest = rest[:24], rest[24:]
+    out_ref, sum_ref, wq, wk, wv, sems = rest
+    weights = (wq, wk, wv)
+    step = pl.program_id(0)
+
+    @pl.when(step == 0)
+    def _():
+        for t in range(3):
+            start_weight(info, pieces[8 * t : 8 * t + 8], KINDS[t], 0, 512, weights[t], sems.at[t])
+        sum_ref[...] = jnp.zeros(sum_ref.shape, F32)
+
+    dn = None
+    for t, ref in enumerate((dq_ref, dk_ref, dv_ref)):
+        for slab in range(2):
+
+            @pl.when(step == 0)
+            def _():
+                wait_weight(weights[t], sems.at[t], slab)
+
+            term = mm_nt(ref[:, slab * 512 : slab * 512 + 512], weights[t][slab])
+            dn = term if dn is None else dn + term
+    unit, inverse = ln_parts(x_ref[...].astype(F32))
+    grad = dh1_ref[...] + ln_back(dn, par[0:1, :], unit, inverse)
+    out_ref[...] = grad.astype(BF)
+    sum_ref[0:1, :] += row_sum(dn * unit)
+    sum_ref[1:2, :] += row_sum(dn)
+
+
+def call_back_one(info, par, dq, dk, dv, x, dh1, pieces):
+    n = x.shape[0]
+    rows = pl.BlockSpec((ROWS, 1024), lambda i, s: (i, 0))
+    return pl.pallas_call(
+        back_one_kernel,
+        grid_spec=pltpu.PrefetchScalarGridSpec(
+            num_scalar_prefetch=1,
+            grid=(n // ROWS,),
+            in_specs=[pl.BlockSpec((24, 1024), lambda i, s: (0, 0)), rows, rows, rows, rows, rows]
+            + [pl.BlockSpec(memory_space=ANYM)] * 24,
+            out_specs=[rows, pl.BlockSpec((8, 1024), lambda i, s: (0, 0))],
+            scratch_shapes=[VM((2, 1024, 512), BF)] * 3 + [pltpu.SemaphoreType.DMA((3, 2))],
+        ),
+        out_shape=[jax.ShapeDtypeStruct((n, 1024), BF), jax.ShapeDtypeStruct((8, 1024), F32)],
+        compiler_params=params_of(48),
+        cost_estimate=cost(6.4e9, 20e6),
+        name="back_one",
+    )(info, par, dq, dk, dv, x, dh1, *pieces)
+
+
+def weight_grad_kernel(kind, picks, count, info, *refs):
+    lefts, rights = refs[:count], refs[count : count + len(picks)]
+    send_ref, keep_ref, temp = refs[count + len(picks) :]
+    for t, pick in enumerate(picks):
+
+        @pl.when(pl.program_id(1) == t)
+        def _():
+            for zrel in range(4):
+                zz = lax.rem(info[0] + zrel, 4)
+                rows = pl.ds(pl.multiple_of(zz * 256, 256), 256)
+                temp[...] = mm(lefts[pick][rows, :], rights[t][...]).astype(BF)
+                store_blocks(info, temp, send_ref, keep_ref, zrel, kind, 512)
+
+
+def call_weight_grad(info, kind, lefts, rights, picks, name):
+    n = rights[0].shape[0]
+    shape, spec = block_out(kind, 512, 512 * len(rights))
+    index = lambda f: (lambda x, t, s: f(x, t))
+    return pl.pallas_call(
+        partial(weight_grad_kernel, kind, picks, len(lefts)),
+        grid_spec=pltpu.PrefetchScalarGridSpec(
+            num_scalar_prefetch=1,
+            grid=(2, len(rights)),
+            in_specs=[pl.BlockSpec((1024, n), lambda x, t, s: (0, 0))] * len(lefts)
+            + [pl.BlockSpec((n, 512), lambda x, t, s: (0, lax.rem(x + s[3], 2)))] * len(rights),
+            out_specs=[spec(index), spec(index)],
+            scratch_shapes=[VM((256, 512), BF)],
+        ),
+        out_shape=[shape, shape],
+        compiler_params=params_of(48),
+        cost_estimate=cost(2.15e9 * len(rights), 4e6 * len(rights) + 2e6 * len(lefts)),
+        name=name,
+    )(info, *lefts, *rights)
+
+
+def along(axis_bit):
+    return [(i, i ^ axis_bit) for i in range(16)]
+
+
+RING = [(i, (i + 4) % 16) for i in range(16)]
+
+
+def swap_x(value):
+    return lax.ppermute(value, "mp", [(0, 1), (1, 0)])
+
+
+def swap_y(value):
+    return lax.ppermute(value, "dp", along(2))
+
+
+def swap_core(value):
+    return lax.ppermute(value, "dp", along(1))
+
+
+def next_z(value):
+    return lax.ppermute(value, "dp", RING)
+
+
+def gather_flow(shard, kind):
+    if kind == "zxy":
+        one = next_z(shard)
+        two = next_z(one)
+        three = next_z(two)
+        base = jnp.stack([shard, one, two, three])
+        over_x = swap_x(base)
+        quads = [base, over_x, swap_y(base), swap_y(over_x)]
+    else:
+        over_x = swap_x(shard)
+        base = jnp.stack([shard, over_x, swap_y(shard), swap_y(over_x)])
+        one = next_z(base)
+        two = next_z(one)
+        quads = [base, one, two, next_z(two)]
+    return quads + [swap_core(quad) for quad in quads]
+
+
+def join(kept, received):
+    return (kept.astype(F32) + received.astype(F32)).astype(kept.dtype)
+
+
+def reduce_ring(parts):
+    moving = next_z(parts[3])
+    moving = next_z(join(parts[2], moving))
+    moving = next_z(join(parts[1], moving))
+    return (parts[0], moving)
+
+
+def reduce_flow(send, keep, kind):
+    received = swap_core(send)
+    if kind == "zxy":
+        arrived = swap_y(join(keep[1], received[1]))
+        kept = join(keep[0], received[0])
+        across = swap_x(join(kept[1], arrived[1]))
+        kept = join(kept[0], arrived[0])
+        parts = [join(kept[k], across[k]) for k in range(4)]
+        last, moving = reduce_ring(parts)
+        return last.astype(F32) + moving.astype(F32)
+    parts = [join(keep[k], received[k]) for k in range(4)]
+    last, moving = reduce_ring(parts)
+    whole = join(last, moving)
+    arrived = swap_y(whole[1])
+    kept = join(whole[0], arrived)
+    return kept[0].astype(F32) + swap_x(kept[1]).astype(F32)
+
+
+def join_halves(mine, other, me):
+    return jnp.where(me == 0, jnp.concatenate([mine, other], 0), jnp.concatenate([other, mine], 0))
+
+
+def whole_sequence(local, me):
+    mine = lax.dynamic_index_in_dim(local, me, 1, keepdims=False)
+    theirs = lax.dynamic_index_in_dim(local, 1 - me, 1, keepdims=False)
+    return join_halves(mine, swap_x(theirs), me)
+
+
+def both_sequences(whole, me):
+    half = whole.shape[0] // 2
+    mine = lax.dynamic_slice_in_dim(whole, me * half, half, 0)
+    theirs = lax.dynamic_slice_in_dim(whole, (1 - me) * half, half, 0)
+    other = swap_x(theirs)
+    return jnp.where(me == 0, jnp.stack([mine, other], 1), jnp.stack([other, mine], 1))
+
+
+def own_first(values, dp, me):
+    rest = values.shape[2:]
+    v = values.reshape((4, 2, 2, 2) + rest)
+    z, y, c = dp // 4, (dp // 2) % 2, dp % 2
+    v = lax.dynamic_slice_in_dim(jnp.concatenate([v, v], 0), z, 4, 0)
+    v = jnp.where(y == 1, v[:, ::-1], v)
+    v = jnp.where(c == 1, v[:, :, ::-1], v)
+    v = jnp.where(me == 1, v[:, :, :, ::-1], v)
+    return jnp.transpose(v, (2, 1, 3, 0) + tuple(range(4, v.ndim)))
+
+
+def one_sequence_body(
+    tokens,
+    memory,
+    cotangent,
+    lengths,
+    memory_lengths,
+    pair_ids,
+    pair_counts,
+    self_in,
+    self_out,
+    cross_in,
+    cross_out,
+    fc_in,
+    fc_out,
+    head_biases,
+    inner_bias,
+    norm_gains,
+    feature_biases,
+):
+    dp, me = lax.axis_index("dp"), lax.axis_index("mp")
+    own_length = lax.dynamic_index_in_dim(lengths, me, 0, keepdims=False)
+    own_memory = lax.dynamic_index_in_dim(memory_lengths, me, 0, keepdims=False)
+    info = jnp.stack([dp // 4, (dp // 2) % 2, dp % 2, me, own_memory, own_length, dp, dp]).astype(jnp.int32)
+    counts = pair_counts.astype(F32)
+    matches = (pair_ids[:, None] == jnp.arange(counts.shape[0], dtype=jnp.int32)[None, :]).astype(F32)
+    scales = jnp.mean(counts) / jnp.sum(matches * counts[None, :], -1)
+    scale = jnp.broadcast_to(lax.dynamic_index_in_dim(scales, me, 0, keepdims=False), (8, 128))
+
+    small = jnp.concatenate(
+        [
+            norm_gains.reshape(-1),
+            feature_biases.reshape(-1),
+            head_biases.astype(F32).reshape(-1),
+            inner_bias.astype(F32).reshape(-1),
+        ]
+    )
+    small = lax.all_gather(small, ("dp", "mp"), axis=0, tiled=False)
+    gains = small[:, :96].reshape(32, 3, 32).transpose(1, 0, 2).reshape(3, 1024)
+    shifts = small[:, 96:288].reshape(32, 6, 32).transpose(1, 0, 2).reshape(6, 1024)
+    heads = small[:, 288:416].reshape(16, 2, 4, 8, 4).transpose(2, 1, 3, 0, 4).reshape(4, 1024)
+    inner = small[:, 416:544].reshape(16, 2, 8, 16).transpose(1, 2, 0, 3).reshape(1, 4096)
+    par = jnp.concatenate([gains, shifts, heads, jnp.zeros((11, 1024), F32)], 0)
+    inner = jnp.broadcast_to(inner, (8, 4096))
+
+    x = whole_sequence(tokens, me)
+    w_self = [gather_flow(self_in[t], KINDS[t]) for t in range(3)]
+    pieces_self = [piece for flow in w_self for piece in flow]
+    mixed_shard = jnp.concatenate([cross_in[1], cross_in[2], self_out.T, cross_in[0], cross_out.T], 1)
+    w_mid = gather_flow(mixed_shard, "zxy")
+    mem = whole_sequence(memory, me)
+    w_in = gather_flow(fc_in, "zxy")
+    w_out = gather_flow(fc_out.T, "xyz")
+    cot = whole_sequence(cotangent, me)
+
+    q1, k1, v1, n1_t = call_qkv(info, par, x, pieces_self)
+    o1, lse1 = call_attend(info, q1, k1, v1, True)
+    k2, v2, mem_t = call_kv(info, par, mem, w_mid)
+    h1, q2, n2_t = call_after_self(info, par, x, o1, w_mid)
+    o2, lse2 = call_attend(info, q2, k2, v2, False)
+    h2, n3, n3_t, g3, g3_t, g_sum = call_after_cross(info, par, scale, h1, o2, cot, w_mid)
+    out, dn3, send_in, keep_in, send_out, keep_out, d_inner = call_ffn(
+        info, par, inner, n3, n3_t, g3, g3_t, h2, w_in, w_out
+    )
+    output = both_sequences(out, me)
+    sum_fc_in = reduce_flow(send_in, keep_in, "zxy")
+    sum_fc_out = reduce_flow(send_out, keep_out, "xyz")
+    dh2, do2, g2_t, sums3 = call_back_three(info, par, dn3, h2, g3, w_mid)
+    dq2, dk2, dv2, bias2 = call_attend_back(info, q2, k2, v2, o2, do2, lse2, False)
+    grad_memory = both_sequences(call_memory_back(info, dk2, dv2, w_mid), me).astype(F32)
+    cross_grads = call_weight_grad(
+        info, "zxy", [mem_t, n2_t, g2_t], [dk2, dv2, dq2, o2], (0, 0, 1, 2), "weight_grad_cross"
+    )
+    sum_cross = reduce_flow(*cross_grads, "zxy")
+    dh1, do1, g1_t, sums2 = call_back_two(info, par, dq2, h1, dh2, w_mid)
+    dq1, dk1, dv1, bias1 = call_attend_back(info, q1, k1, v1, o1, do1, lse1, True)
+    self_grads = call_weight_grad(info, "zxy", [n1_t, g1_t], [dq1, dk1, dv1, o1], (0, 0, 0, 1), "weight_grad_self")
+    sum_self = reduce_flow(*self_grads, "zxy")
+    grad_x, sums1 = call_back_one(info, par, dq1, dk1, dv1, x, dh1, pieces_self)
+    grad_tokens = both_sequences(grad_x, me).astype(F32)
+
+    d_gains = jnp.stack([sums1[0], sums2[0], sums3[0]])
+    d_shifts = jnp.stack([sums1[1], sums2[1], sums3[1], sums2[2], sums3[2], g_sum[0]])
+    d_heads = jnp.concatenate([bias1[:2], bias2[:2]], 0)
+    d_small = jnp.concatenate(
+        [
+            d_gains.reshape(3, 32, 32).transpose(1, 0, 2).reshape(32, 96),
+            d_shifts.reshape(6, 32, 32).transpose(1, 0, 2).reshape(32, 192),
+            d_heads.reshape(4, 2, 8, 16, 4).transpose(3, 1, 0, 2, 4).reshape(32, 128),
+            d_inner[0].reshape(2, 8, 16, 16).transpose(2, 0, 1, 3).reshape(32, 128),
+        ],
+        1,
+    )
+    d_small = own_first(d_small.reshape(16, 2, 544), dp, me)
+    total = reduce_flow(d_small[1], d_small[0], "zxy")
+    return (
+        output,
+        grad_tokens,
+        grad_memory,
+        jnp.stack([sum_self[:, :512], sum_self[:, 512:1024], sum_self[:, 1024:1536]]),
+        sum_self[:, 1536:].T,
+        jnp.stack([sum_cross[:, 1024:1536], sum_cross[:, :512], sum_cross[:, 512:1024]]),
+        sum_cross[:, 1536:].T,
+        sum_fc_in,
+        sum_fc_out.T,
+        total[288:416].reshape(4, 8, 4),
+        total[416:].reshape(8, 16),
+        total[:96].reshape(3, 32),
+        total[96:288].reshape(6, 32),
+    )
+
+
 def solution(mesh):
     in_specs = (
         P("mp", "dp", None),
@@ -507,4 +1600,6 @@
         P(None, ("dp", "mp")),
         P(None, ("dp", "mp")),
     )
-    return jax.shard_map(body, mesh=mesh, in_specs=in_specs, out_specs=out_specs, check_vma=False)
+    sizes = dict(mesh.shape)
+    chosen = one_sequence_body if (sizes["dp"], sizes["mp"]) == (16, 2) else body
+    return jax.shard_map(chosen, mesh=mesh, in_specs=in_specs, out_specs=out_specs, check_vma=False)

time: 2370 us -> 1020 us (0.43)
  waiting for transfers between devices: 1240 us -> 385 us
  matrix products: 519 us -> 0 us
  Pallas kernels: 0 us -> 397 us
  blocking collectives: 234 us -> 0 us
  other arithmetic: 212 us -> 51.8 us
  starting transfers between devices: 1.85 us -> 65.8 us
  local copies, waits for them, and re-layouts: 138 us -> 96.3 us
    dot_general x77 -> x0, matrix products: 519 us -> none  [the longest x16 93.1 us: masked_scores(): jnp.einsum('qhd,khd->hqk', rows, keys, preferred_element_type=jnp.float32)]
    pallas_call x0 -> x15, Pallas kernels: none -> 397 us  [the longest x2 92.7 us: call_attend_back(): pl.pallas_call(partial(attend_back_kernel, causal), grid_spec=pltpu.Prefe...]
    all_gather x11 -> x0, waiting for transfers between devices: 337 us -> none  [the longest x3 94 us: gather_grads(): return lax.all_gather(grad_branch, 'mp', axis=0, tiled=True)]
    unnamed x30 -> x2, waiting for transfers between devices: 422 us -> 105 us
    reduce_scatter x9 -> x0, waiting for transfers between devices: 296 us -> none  [the longest x4 195 us: reduce_inputs(): lax.psum_scatter(term_fn(jnp.int32(0), lax.axis_size('mp') * rows).astype...]
    ppermute x0 -> x96, waiting for transfers between devices: none -> 280 us  [the longest x33 92.8 us: next_z(): return lax.ppermute(value, 'dp', RING)]
    psum x2 -> x0, waiting for transfers between devices: 182 us -> none  [whole_rows(): lax.psum((term + placed).astype(jnp.bfloat16), 'mp').astype(jnp.float32)]
    all_gather x4 -> x0, blocking collectives: 173 us -> none  [the longest x1 70 us: body(): lax.all_gather(norm_gains, ('dp', 'mp'), axis=1, tiled=True)]
  transfers between devices with their start and end apart: 26 -> 97, of which waited for: 19 -> 40; matrix products, arithmetic and copies ran while one was open for 22% -> 13% of each run, Pallas kernels for 0% -> 17%
where the time goes in v1:
time: 1020 us; the launch traced here: 1010 us
  Pallas kernels  397 us (39%)
  waiting for transfers between devices  385 us (38%)
  local copies, waits for them, and re-layouts  96.3 us (9%)
  starting transfers between devices  65.8 us (6%)
  other arithmetic  51.8 us (5%)
  between operations  17.1 us (2%)
    unnamed x2, waiting for transfers between devices  105 us
    ppermute x33, waiting for transfers between devices, next_z(): return lax.ppermute(value, 'dp', RING)  92.8 us
    pallas_call x2, Pallas kernels, call_attend_back(): pl.pallas_call(partial(attend_back_kernel, causal), grid_spec=pltpu.Prefe...  92.7 us
    ppermute x17, waiting for transfers between devices, swap_y(): return lax.ppermute(value, 'dp', along(2))  92.1 us
    pallas_call x1, Pallas kernels, call_ffn(): pl.pallas_call(ffn_kernel, grid_spec=pltpu.PrefetchScalarGridSpec(num_sca...  87.3 us
    ppermute x17, waiting for transfers between devices, swap_x(): return lax.ppermute(value, 'mp', [(0, 1), (1, 0)])  86.5 us
    pallas_call x2, Pallas kernels, call_attend(): pl.pallas_call(partial(attend_kernel, causal), grid_spec=pltpu.PrefetchSc...  64.3 us
    unnamed x242, local copies, waits for them, and re-layouts  38.2 us
  transfers between devices with their start and end apart: 97, of which 40 were waited for; matrix products, arithmetic and copies ran while one was open for 13% of the time, Pallas kernels for 17%

profile of v1, /device:TPU:0, one launch (start us, length us, event | category | flops | bytes accessed | tf_op | source)
XLA Modules:
  0.0 1013.2 jit_solution(2507874955359115740)
XLA Ops:
  34.3 7.1 collective-permute-done.3
  42.3 5.7 collective-permute-done.23
  82.8 13.3 %constant_dynamic-slice_fusion.4 = (bf16[512,1,1024]{2,1,0:T(2,128)(2,1)}, bf16[512,1,1024]{2,1,0:T(2,128)(2,1)S(1)}, bf16[512,1,1024]{2,1,0:T(2,128)(2,1)S(1)}, bf16[512,1,1024]{2,1,0:T(2,128)(2,1)}) fusion(bf16[512,2,1024]{2,1,0:T(2,128)(2,1)S(1)} %copy-done.71, s32[]{:T(128)S(6)} %select_n.110, s32[]{:T(128)S(6)} %select_n.112, ...), kind=kLoop, calls=%fused_computation.192 | loop fusion | bytes 8388616 | tf_op jit(solution)/shard_map/jit(dynamic_index_in_dim)/dynamic_slice | solution.py:1433
  99.8 5.6 constant_dynamic-slice_fusion.8
  118.2 17.3 %collective-permute-done.41 = bf16[512,1024]{1,0:T(8,128)(2,1)S(1)} collective-permute-done((bf16[512,1024]{1,0:T(8,128)(2,1)S(1)}, bf16[512,1024]{1,0:T(8,128)(2,1)S(1)}, u32[]{:S(2)}, u32[]{:S(2)}) %collective-permute-start.41) | collective-permute-done | bytes 1048608 | tf_op jit(solution)/shard_map/ppermute | solution.py:1367
  139.7 18.2 %collective-permute-done = bf16[512,1024]{1,0:T(8,128)(2,1)S(1)} collective-permute-done((bf16[512,1024]{1,0:T(8,128)(2,1)S(1)}, bf16[512,1024]{1,0:T(8,128)(2,1)S(1)}, u32[]{:S(2)}, u32[]{:S(2)}) %collective-permute-start) | collective-permute-done | bytes 1048608 | tf_op jit(solution)/shard_map/ppermute | solution.py:1367
  157.9 21.6 %collective-permute-done.42 = bf16[512,1024]{1,0:T(8,128)(2,1)S(1)} collective-permute-done((bf16[512,1024]{1,0:T(8,128)(2,1)S(1)}, bf16[512,1024]{1,0:T(8,128)(2,1)S(1)}, u32[]{:S(2)}, u32[]{:S(2)}) %collective-permute-start.42) | collective-permute-done | bytes 1048608 | tf_op jit(solution)/shard_map/ppermute | solution.py:1367
  195.4 104.5 %all-reduce.3.cloned.1.call-done = f32[17408]{0:T(1024)} async-done(((f32[17408]{0:T(1024)}), f32[17408]{0:T(1024)}) %all-reduce.3.cloned.1.call-update) | async-done | bytes 69648
  332.8 23.7 %project_self.1 = (bf16[1024,1024]{1,0:T(8,128)(2,1)}, bf16[1024,1024]{1,0:T(8,128)(2,1)}, bf16[1024,1024]{1,0:T(8,128)(2,1)}, bf16[1024,1024]{1,0:T(8,128)(2,1)}) custom-call(s32[8]{0:T(128)S(1)} %stack.179.info, f32[24,1024]{1,0:T(8,128)S(1)} %maximum_maximum_fusion.par, bf16[1024,1024]{1,0:T(8,128)(2,1)} %maximum_select_fusion.x_ref, ...), custom_call_target="tpu_custom_call" | custom-call | flops 6400000000 | bytes 16000000 | tf_op jit(solution)/shard_map/project_self/pallas_call | solution.py:602
  361.2 28.9 %attend_self.1 = (bf16[1024,1024]{1,0:T(8,128)(2,1)S(1)}, f32[1024,128]{1,0:T(8,128)S(1)}) custom-call(s32[8]{0:T(128)S(1)} %stack.179.info, bf16[1024,1024]{1,0:T(8,128)(2,1)S(1)} %copy-done.65, bf16[1024,1024]{1,0:T(8,128)(2,1)} %get-tuple-element.63.k_ref, bf16[1024,1024]{1,0:T(8,128)(2,1)} %get-tuple-element.64.v_ref), custom_call_target="tpu_custom_call" | custom-call | flops 10000000000 | bytes 9000000 | tf_op jit(solution)/shard_map/attend_self/pallas_call | solution.py:729
  392.2 11.7 %project_memory.1 = (bf16[1024,1024]{1,0:T(8,128)(2,1)}, bf16[1024,1024]{1,0:T(8,128)(2,1)}, bf16[1024,1024]{1,0:T(8,128)(2,1)}) custom-call(s32[8]{0:T(128)S(1)} %stack.179.info, f32[24,1024]{1,0:T(8,128)S(1)} %maximum_maximum_fusion.par, bf16[1024,1024]{1,0:T(8,128)(2,1)} %maximum_select_fusion.1.x_ref, bf16[4,64,2560]{2,1,0:T(8,128)(2,1)S(1)} %pad_maximum_fusion.rest_0_, ...), custom_call_target="tpu_custom_call" | custom-call | flops 4300000256 | bytes 12000000 | tf_op jit(solution)/shard_map/project_memory/pallas_call | solution.py:649
  403.9 13.0 %after_self.1 = (f32[1024,1024]{1,0:T(8,128)}, bf16[1024,1024]{1,0:T(8,128)(2,1)}, bf16[1024,1024]{1,0:T(8,128)(2,1)}) custom-call(s32[8]{0:T(128)S(1)} %stack.179.info, f32[24,1024]{1,0:T(8,128)S(1)} %maximum_maximum_fusion.par, bf16[1024,1024]{1,0:T(8,128)(2,1)} %maximum_select_fusion.x_ref, bf16[1024,1024]{1,0:T(8,128)(2,1)} %copy-done.60, ...), custom_call_target="tpu_custom_call" | custom-call | flops 4300000256 | bytes 16000000 | tf_op jit(solution)/shard_map/after_self/pallas_call | solution.py:872
  420.3 35.4 %attend_cross.1 = (bf16[1024,1024]{1,0:T(8,128)(2,1)S(1)}, f32[1024,128]{1,0:T(8,128)S(1)}) custom-call(s32[8]{0:T(128)S(1)} %stack.179.info, bf16[1024,1024]{1,0:T(8,128)(2,1)S(1)} %copy-done.62, bf16[1024,1024]{1,0:T(8,128)(2,1)} %get-tuple-element.68.k_ref, bf16[1024,1024]{1,0:T(8,128)(2,1)} %get-tuple-element.69.v_ref), custom_call_target="tpu_custom_call" | custom-call | flops 16000000000 | bytes 9000000 | tf_op jit(solution)/shard_map/attend_cross/pallas_call | solution.py:729
  458.6 12.4 %after_cross.1 = (f32[1024,1024]{1,0:T(8,128)}, bf16[1024,1024]{1,0:T(8,128)(2,1)}, bf16[1024,1024]{1,0:T(8,128)(2,1)}, bf16[1024,1024]{1,0:T(8,128)(2,1)}, bf16...) custom-call(s32[8]{0:T(128)S(1)} %stack.179.info, f32[24,1024]{1,0:T(8,128)S(1)} %maximum_maximum_fusion.par, ...), custom_call_target="tpu_custom_call" | custom-call | flops 2200000000 | bytes 26000000 | tf_op jit(solution)/shard_map/after_cross/pallas_call | solution.py:936
  471.8 87.3 %feedforward.1 = (bf16[1024,1024]{1,0:T(8,128)(2,1)}, f32[1024,1024]{1,0:T(8,128)}, bf16[2,2,4,64,2048]{4,3,2,1,0:T(8,128)(2,1)}, bf16[2,2,4,64,2048]{4,3,2,1,0:...) custom-call(s32[8]{0:T(128)} %copy-done.3, ...), custom_call_target="tpu_custom_call" | custom-call | flops 51499999232 | bytes 60000000 | tf_op jit(solution)/shard_map/feedforward/pallas_call | solution.py:1071
  559.1 11.4 %back_three.1 = (f32[1024,1024]{1,0:T(8,128)}, bf16[1024,1024]{1,0:T(8,128)(2,1)}, bf16[1024,1024]{1,0:T(8,128)(2,1)}, f32[8,1024]{1,0:T(8,128)S(1)}) custom-call(s32[8]{0:T(128)S(1)} %copy-done.4, f32[24,1024]{1,0:T(8,128)S(1)} %copy-done.2, f32[1024,1024]{1,0:T(8,128)} %get-tuple-element.77.dn_ref, f32[1024,1024]{1,0:T(8,128)} %get-tuple-element.75.h_ref, ...), custom_call_target="tpu_custom_call" | custom-call | flops 2200000000 | bytes 20000000 | tf_op jit(solution)/shard_map/back_three/pallas_call | solution.py:1154
  570.5 53.9 %attend_back_cross.1 = (bf16[1024,1024]{1,0:T(8,128)(2,1)}, bf16[1024,1024]{1,0:T(8,128)(2,1)}, bf16[1024,1024]{1,0:T(8,128)(2,1)}, f32[8,1024]{1,0:T(8,128)}) custom-call(s32[8]{0:T(128)} %copy-done.3, bf16[1024,1024]{1,0:T(8,128)(2,1)} %get-tuple-element.67.q_ref, bf16[1024,1024]{1,0:T(8,128)(2,1)} %get-tuple-element.68.k_ref, ...), custom_call_target="tpu_custom_call" | custom-call | flops 40000000000 | bytes 20000000 | tf_op jit(solution)/shard_map/attend_back_cross/pallas_call | solution.py:821
  624.5 13.8 %back_two.1 = (f32[1024,1024]{1,0:T(8,128)}, bf16[1024,1024]{1,0:T(8,128)(2,1)}, bf16[1024,1024]{1,0:T(8,128)(2,1)}, f32[8,1024]{1,0:T(8,128)S(1)}) custom-call(s32[8]{0:T(128)S(1)} %copy-done.5, f32[24,1024]{1,0:T(8,128)S(1)} %copy-done.2, bf16[1024,1024]{1,0:T(8,128)(2,1)} %get-tuple-element.80.dq_ref.refs_5_, f32[1024,1024]{1,0:T(8,128)} %get-tuple-element.66.h_in.h_ref, ...), custom_call_target="tpu_custom_call" | custom-call | flops 4300000256 | bytes 24000000 | tf_op jit(solution)/shard_map/back_two/pallas_call | solution.py:1207
  638.5 38.7 %attend_back_self.1 = (bf16[1024,1024]{1,0:T(8,128)(2,1)}, bf16[1024,1024]{1,0:T(8,128)(2,1)}, bf16[1024,1024]{1,0:T(8,128)(2,1)}, f32[8,1024]{1,0:T(8,128)}) custom-call(s32[8]{0:T(128)} %copy-done.3, bf16[1024,1024]{1,0:T(8,128)(2,1)} %get-tuple-element.62.q_ref, bf16[1024,1024]{1,0:T(8,128)(2,1)} %get-tuple-element.63.k_ref, ...), custom_call_target="tpu_custom_call" | custom-call | flops 24999999488 | bytes 20000000 | tf_op jit(solution)/shard_map/attend_back_self/pallas_call | solution.py:821
  678.9 23.0 %back_one.1 = (bf16[1024,1024]{1,0:T(8,128)(2,1)}, f32[8,1024]{1,0:T(8,128)S(1)}) custom-call(s32[8]{0:T(128)S(1)} %copy-done.6, f32[24,1024]{1,0:T(8,128)S(1)} %copy-done.2, bf16[1024,1024]{1,0:T(8,128)(2,1)} %get-tuple-element.84.dq_ref.refs_2_, bf16[1024,1024]{1,0:T(8,128)(2,1)} %get-tuple-element.85.dk_ref.refs_3_, ...), custom_call_target="tpu_custom_call" | custom-call | flops 6400000000 | bytes 20000000 | tf_op jit(solution)/shard_map/back_one/pallas_call | solution.py:1307
  702.6 17.5 %weight_grad_cross.1 = (bf16[2,2,4,64,2048]{4,3,2,1,0:T(8,128)(2,1)}, bf16[2,2,4,64,2048]{4,3,2,1,0:T(8,128)(2,1)}) custom-call(s32[8]{0:T(128)S(1)} %copy-done.6, bf16[1024,1024]{1,0:T(8,128)(2,1)S(1)} %copy-done.63, bf16[1024,1024]{1,0:T(8,128)(2,1)S(1)} %copy-done.61, bf16[1024,1024]{1,0:T(8,128)(2,1)} %get-tuple-element.97.refs_2_, ...), custom_call_target="tpu_custom_call" | custom-call | flops 8600000512 | bytes 22000000 | tf_op jit(solution)/shard_map/weight_grad_cross/pallas_call | solution.py:1342
  729.2 16.2 %weight_grad_self.1 = (bf16[2,2,4,64,2048]{4,3,2,1,0:T(8,128)(2,1)}, bf16[2,2,4,64,2048]{4,3,2,1,0:T(8,128)(2,1)}) custom-call(s32[8]{0:T(128)S(1)} %copy-done.6, bf16[1024,1024]{1,0:T(8,128)(2,1)S(1)} %copy-done.64, bf16[1024,1024]{1,0:T(8,128)(2,1)S(1)} %copy-done.7, bf16[1024,1024]{1,0:T(8,128)(2,1)} %get-tuple-element.84.dq_ref.refs_2_, ...), custom_call_target="tpu_custom_call" | custom-call | flops 8600000512 | bytes 20000000 | tf_op jit(solution)/shard_map/weight_grad_self/pallas_call | solution.py:1342
  756.6 10.2 %memory_back.1 = bf16[1024,1024]{1,0:T(8,128)(2,1)} custom-call(s32[8]{0:T(128)S(1)} %copy-done.6, bf16[1024,1024]{1,0:T(8,128)(2,1)} %get-tuple-element.89.dk_ref.refs_3_, bf16[1024,1024]{1,0:T(8,128)(2,1)} %get-tuple-element.90.dv_ref.refs_4_, bf16[4,64,2560]{2,1,0:T(8,128)(2,1)S(1)} %pad_maximum_fusion.rest_0_, ...), custom_call_target="tpu_custom_call" | custom-call | flops 4300000256 | bytes 12000000 | tf_op jit(solution)/shard_map/memory_back/pallas_call | solution.py:1259
  790.4 5.4 add_convert_fusion.1
  800.0 12.7 %collective-permute-done.85 = bf16[2,2,64,2048]{3,2,1,0:T(8,128)(2,1)S(1)} collective-permute-done((bf16[2,2,64,2048]{3,2,1,0:T(8,128)(2,1)S(1)}, bf16[2,2,64,2048]{3,2,1,0:T(8,128)(2,1)S(1)}, u32[]{:S(2)}, u32[]{:S(2)}) %collective-permute-start.85) | collective-permute-done | bytes 1048608 | tf_op jit(solution)/shard_map/ppermute | solution.py:1379
  821.9 10.3 %collective-permute-done.64 = bf16[512,1024]{1,0:T(8,128)(2,1)S(1)} collective-permute-done((bf16[512,1024]{1,0:T(8,128)(2,1)}, bf16[512,1024]{1,0:T(8,128)(2,1)S(1)}, u32[]{:S(2)}, u32[]{:S(2)}) %collective-permute-start.64) | collective-permute-done | bytes 1048608 | tf_op jit(solution)/shard_map/ppermute | solution.py:1367
  862.8 43.7 %collective-permute-done.73 = bf16[2,4,64,2048]{3,2,1,0:T(8,128)(2,1)S(1)} collective-permute-done((bf16[2,4,64,2048]{3,2,1,0:T(8,128)(2,1)}, bf16[2,4,64,2048]{3,2,1,0:T(8,128)(2,1)S(1)}, u32[]{:S(2)}, u32[]{:S(2)}) %collective-permute-start.73) | collective-permute-done | bytes 2097184 | tf_op jit(solution)/shard_map/ppermute | solution.py:1371
  907.7 37.3 %collective-permute-done.67 = bf16[2,4,64,2048]{3,2,1,0:T(8,128)(2,1)} collective-permute-done((bf16[2,4,64,2048]{3,2,1,0:T(8,128)(2,1)}, bf16[2,4,64,2048]{3,2,1,0:T(8,128)(2,1)}, u32[]{:S(2)}, u32[]{:S(2)}) %collective-permute-start.67) | collective-permute-done | bytes 2097184 | tf_op jit(solution)/shard_map/ppermute | solution.py:1371
  951.7 14.5 %collective-permute-done.68 = bf16[4,64,2048]{2,1,0:T(8,128)(2,1)S(1)} collective-permute-done((bf16[4,64,2048]{2,1,0:T(8,128)(2,1)S(1)}, bf16[4,64,2048]{2,1,0:T(8,128)(2,1)S(1)}, u32[]{:S(2)}, u32[]{:S(2)}) %collective-permute-start.68) | collective-permute-done | bytes 1048608 | tf_op jit(solution)/shard_map/ppermute | solution.py:1367
  967.3 10.0 collective-permute-done.69
  983.1 5.4 collective-permute-done.76
  988.7 5.4 collective-permute-done.70
  (545 shorter events, 260.8 us)
Async XLA Ops:
  7.2 292.7 %all-reduce.3.cloned.1.call-start = ((), (), s32[]{:S(2)}) async-start(), calls=%async_computation | async-start | bytes 139264
  81.2 54.7 %collective-permute-start.34 = (bf16[4,64,2560]{2,1,0:T(8,128)(2,1)S(1)}, bf16[4,64,2560]{2,1,0:T(8,128)(2,1)S(1)}, u32[]{:S(2)}, u32[]{:S(2)}) collective-permute-start(bf16[4,64,2560]{2,1,0:T(8,128)(2,1)S(1)} %pad_maximum_fusion.rest_0_), channel_id=1, source_target_pairs={{0,1},{1,0},{2,3},{3,2},{4,5},{5,4},{6,7},{7,6},{8,9},{9,8},{10,11... | collective-permute-start | bytes 3932168 | tf_op jit(solution)/shard_map/ppermute | solution.py:1367
  106.3 51.6 %collective-permute-start = (bf16[512,1024]{1,0:T(8,128)(2,1)S(1)}, bf16[512,1024]{1,0:T(8,128)(2,1)S(1)}, u32[]{:S(2)}, u32[]{:S(2)}) collective-permute-start(bf16[512,1024]{1,0:T(8,128)(2,1)S(1)} %bitcast.345), channel_id=1, source_target_pairs={{0,1},{1,0},{2,3},{3,2},{4,5},{5,4},{6,7},{7,6},{8,9},{9,8},{10,11... | collective-permute-start | bytes 3145736 | tf_op jit(solution)/shard_map/ppermute | solution.py:1367
  108.2 71.3 %collective-permute-start.42 = (bf16[512,1024]{1,0:T(8,128)(2,1)S(1)}, bf16[512,1024]{1,0:T(8,128)(2,1)S(1)}, u32[]{:S(2)}, u32[]{:S(2)}) collective-permute-start(bf16[512,1024]{1,0:T(8,128)(2,1)S(1)} %bitcast.344), channel_id=1, source_target_pairs={{0,1},{1,0},{2,3},{3,2},{4,5},{5,4},{6,7},{7,6},{8,9},{9,8},{10,11... | collective-permute-start | bytes 3145736 | tf_op jit(solution)/shard_map/ppermute | solution.py:1367
  118.0 62.7 %collective-permute-start.20 = (bf16[4,64,512]{2,1,0:T(8,128)(2,1)S(1)}, bf16[4,64,512]{2,1,0:T(8,128)(2,1)S(1)}, u32[]{:S(2)}, u32[]{:S(2)}) collective-permute-start(bf16[4,64,512]{2,1,0:T(8,128)(2,1)S(1)} %collective-permute-done.16.rest_11_), channel_id=1, source_target_pairs={{0,2},{2,0},{4,6},{6,4},{8,10},{10,8},{12,14},{14,12},{16,18},{18,... | collective-permute-start | bytes 786440 | tf_op jit(solution)/shard_map/ppermute | solution.py:1375
  135.4 178.4 %collective-permute-start.35 = (bf16[4,64,2560]{2,1,0:T(8,128)(2,1)S(1)}, bf16[4,64,2560]{2,1,0:T(8,128)(2,1)}, u32[]{:S(2)}, u32[]{:S(2)}) collective-permute-start(bf16[4,64,2560]{2,1,0:T(8,128)(2,1)S(1)} %pad_maximum_fusion.rest_0_), channel_id=1, source_target_pairs={{0,4},{2,6},{4,0},{6,2},{8,12},{10,14},{12,8},{14,10},{16,20},{18,... | collective-permute-start | bytes 3932168 | tf_op jit(solution)/shard_map/ppermute | solution.py:1371
  136.0 178.3 %collective-permute-start.36 = (bf16[4,64,2560]{2,1,0:T(8,128)(2,1)S(1)}, bf16[4,64,2560]{2,1,0:T(8,128)(2,1)}, u32[]{:S(2)}, u32[]{:S(2)}) collective-permute-start(bf16[4,64,2560]{2,1,0:T(8,128)(2,1)S(1)} %collective-permute-done.34.rest_1_), channel_id=1, source_target_pairs={{0,4},{2,6},{4,0},{6,2},{8,12},{10,14},{12,8},{14,10},{16,20},{18,... | collective-permute-start | bytes 3932168 | tf_op jit(solution)/shard_map/ppermute | solution.py:1371
  157.9 154.5 %collective-permute-start.56 = (bf16[4,64,2048]{2,1,0:T(8,128)(2,1)}, bf16[4,64,2048]{2,1,0:T(8,128)(2,1)}, u32[]{:S(2)}, u32[]{:S(2)}) collective-permute-start(bf16[4,64,2048]{2,1,0:T(8,128)(2,1)} %pad_maximum_fusion.2.rest_8_), channel_id=1, source_target_pairs={{0,8},{2,10},{4,12},{6,14},{8,16},{10,18},{12,20},{14,22},{16,24},... | collective-permute-start | bytes 3145736 | tf_op jit(solution)/shard_map/ppermute | solution.py:1379
  179.5 134.2 %collective-permute-start.59 = (bf16[4,64,2048]{2,1,0:T(8,128)(2,1)}, bf16[4,64,2048]{2,1,0:T(8,128)(2,1)}, u32[]{:S(2)}, u32[]{:S(2)}) collective-permute-start(bf16[4,64,2048]{2,1,0:T(8,128)(2,1)} %pad_maximum_fusion.2.rest_8_), channel_id=1, source_target_pairs={{0,2},{2,0},{4,6},{6,4},{8,10},{10,8},{12,14},{14,12},{16,18},{18,... | collective-permute-start | bytes 3145736 | tf_op jit(solution)/shard_map/ppermute | solution.py:1375
  181.4 138.4 %collective-permute-start.46 = (bf16[4,64,2048]{2,1,0:T(8,128)(2,1)}, bf16[4,64,2048]{2,1,0:T(8,128)(2,1)}, u32[]{:S(2)}, u32[]{:S(2)}) collective-permute-start(bf16[4,64,2048]{2,1,0:T(8,128)(2,1)} %pad_maximum_fusion.1.rest_0_), channel_id=1, source_target_pairs={{0,1},{1,0},{2,3},{3,2},{4,5},{5,4},{6,7},{7,6},{8,9},{9,8},{10,11... | collective-permute-start | bytes 3145736 | tf_op jit(solution)/shard_map/ppermute | solution.py:1367
  314.2 44.9 %collective-permute-start.40 = (bf16[4,64,2560]{2,1,0:T(8,128)(2,1)}, bf16[4,64,2560]{2,1,0:T(8,128)(2,1)}, u32[]{:S(2)}, u32[]{:S(2)}) collective-permute-start(bf16[4,64,2560]{2,1,0:T(8,128)(2,1)} %collective-permute-done.36.rest_3_), channel_id=1, source_target_pairs={{0,2},{2,0},{4,6},{6,4},{8,10},{10,8},{12,14},{14,12},{16,18},{18,... | collective-permute-start | bytes 3932168 | tf_op jit(solution)/shard_map/ppermute | solution.py:1375
  356.5 60.5 %collective-permute-start.47 = (bf16[4,64,2048]{2,1,0:T(8,128)(2,1)}, bf16[4,64,2048]{2,1,0:T(8,128)(2,1)S(1)}, u32[]{:S(2)}, u32[]{:S(2)}) collective-permute-start(bf16[4,64,2048]{2,1,0:T(8,128)(2,1)} %pad_maximum_fusion.1.rest_0_), channel_id=1, source_target_pairs={{0,4},{2,6},{4,0},{6,2},{8,12},{10,14},{12,8},{14,10},{16,20},{18,... | collective-permute-start | bytes 3145736 | tf_op jit(solution)/shard_map/ppermute | solution.py:1371
  358.1 59.0 %collective-permute-start.49 = (bf16[4,64,2048]{2,1,0:T(8,128)(2,1)}, bf16[4,64,2048]{2,1,0:T(8,128)(2,1)S(1)}, u32[]{:S(2)}, u32[]{:S(2)}) collective-permute-start(bf16[4,64,2048]{2,1,0:T(8,128)(2,1)} %pad_maximum_fusion.1.rest_0_), channel_id=1, source_target_pairs={{0,2},{2,0},{4,6},{6,4},{8,10},{10,8},{12,14},{14,12},{16,18},{18,... | collective-permute-start | bytes 3145736 | tf_op jit(solution)/shard_map/ppermute | solution.py:1375
  358.1 59.5 %collective-permute-start.60 = (bf16[4,64,2048]{2,1,0:T(8,128)(2,1)}, bf16[4,64,2048]{2,1,0:T(8,128)(2,1)S(1)}, u32[]{:S(2)}, u32[]{:S(2)}) collective-permute-start(bf16[4,64,2048]{2,1,0:T(8,128)(2,1)} %collective-permute-done.56.rest_9_), channel_id=1, source_target_pairs={{0,2},{2,0},{4,6},{6,4},{8,10},{10,8},{12,14},{14,12},{16,18},{18,... | collective-permute-start | bytes 3145736 | tf_op jit(solution)/shard_map/ppermute | solution.py:1375
  358.6 59.2 %collective-permute-start.48 = (bf16[4,64,2048]{2,1,0:T(8,128)(2,1)}, bf16[4,64,2048]{2,1,0:T(8,128)(2,1)S(1)}, u32[]{:S(2)}, u32[]{:S(2)}) collective-permute-start(bf16[4,64,2048]{2,1,0:T(8,128)(2,1)} %collective-permute-done.46.rest_1_), channel_id=1, source_target_pairs={{0,4},{2,6},{4,0},{6,2},{8,12},{10,14},{12,8},{14,10},{16,20},{18,... | collective-permute-start | bytes 3145736 | tf_op jit(solution)/shard_map/ppermute | solution.py:1371
  359.1 59.0 %collective-permute-start.58 = (bf16[4,64,2048]{2,1,0:T(8,128)(2,1)S(1)}, bf16[4,64,2048]{2,1,0:T(8,128)(2,1)S(1)}, u32[]{:S(2)}, u32[]{:S(2)}) collective-permute-start(bf16[4,64,2048]{2,1,0:T(8,128)(2,1)S(1)} %collective-permute-done.57.rest_10_), channel_id=1, source_target_pairs={{0,8},{2,10},{4,12},{6,14},{8,16},{10,18},{12,20},{14,22},{16,24},... | collective-permute-start | bytes 3145736 | tf_op jit(solution)/shard_map/ppermute | solution.py:1379
  417.0 54.1 %collective-permute-start.50 = (bf16[4,64,2048]{2,1,0:T(8,128)(2,1)}, bf16[4,64,2048]{2,1,0:T(8,128)(2,1)}, u32[]{:S(2)}, u32[]{:S(2)}) collective-permute-start(bf16[4,64,2048]{2,1,0:T(8,128)(2,1)} %collective-permute-done.46.rest_1_), channel_id=1, source_target_pairs={{0,2},{2,0},{4,6},{6,4},{8,10},{10,8},{12,14},{14,12},{16,18},{18,... | collective-permute-start | bytes 3145736 | tf_op jit(solution)/shard_map/ppermute | solution.py:1375
  417.1 54.0 %collective-permute-start.51 = (bf16[4,64,2048]{2,1,0:T(8,128)(2,1)S(1)}, bf16[4,64,2048]{2,1,0:T(8,128)(2,1)}, u32[]{:S(2)}, u32[]{:S(2)}) collective-permute-start(bf16[4,64,2048]{2,1,0:T(8,128)(2,1)S(1)} %collective-permute-done.47.rest_2_), channel_id=1, source_target_pairs={{0,2},{2,0},{4,6},{6,4},{8,10},{10,8},{12,14},{14,12},{16,18},{18,... | collective-permute-start | bytes 3145736 | tf_op jit(solution)/shard_map/ppermute | solution.py:1375
  417.6 53.5 %collective-permute-start.61 = (bf16[4,64,2048]{2,1,0:T(8,128)(2,1)S(1)}, bf16[4,64,2048]{2,1,0:T(8,128)(2,1)}, u32[]{:S(2)}, u32[]{:S(2)}) collective-permute-start(bf16[4,64,2048]{2,1,0:T(8,128)(2,1)S(1)} %collective-permute-done.57.rest_10_), channel_id=1, source_target_pairs={{0,2},{2,0},{4,6},{6,4},{8,10},{10,8},{12,14},{14,12},{16,18},{18,... | collective-permute-start | bytes 3145736 | tf_op jit(solution)/shard_map/ppermute | solution.py:1375
  417.7 53.3 %collective-permute-start.52 = (bf16[4,64,2048]{2,1,0:T(8,128)(2,1)S(1)}, bf16[4,64,2048]{2,1,0:T(8,128)(2,1)}, u32[]{:S(2)}, u32[]{:S(2)}) collective-permute-start(bf16[4,64,2048]{2,1,0:T(8,128)(2,1)S(1)} %collective-permute-done.48.rest_3_), channel_id=1, source_target_pairs={{0,2},{2,0},{4,6},{6,4},{8,10},{10,8},{12,14},{14,12},{16,18},{18,... | collective-permute-start | bytes 3145736 | tf_op jit(solution)/shard_map/ppermute | solution.py:1375
  418.2 52.9 %collective-permute-start.62 = (bf16[4,64,2048]{2,1,0:T(8,128)(2,1)S(1)}, bf16[4,64,2048]{2,1,0:T(8,128)(2,1)}, u32[]{:S(2)}, u32[]{:S(2)}) collective-permute-start(bf16[4,64,2048]{2,1,0:T(8,128)(2,1)S(1)} %collective-permute-done.58.rest_11_), channel_id=1, source_target_pairs={{0,2},{2,0},{4,6},{6,4},{8,10},{10,8},{12,14},{14,12},{16,18},{18,... | collective-permute-start | bytes 3145736 | tf_op jit(solution)/shard_map/ppermute | solution.py:1375
  702.0 84.5 %collective-permute-start.84 = (bf16[4,2,2,64,2048]{4,3,2,1,0:T(8,128)(2,1)}, bf16[4,2,2,64,2048]{4,3,2,1,0:T(8,128)(2,1)}, u32[]{:S(2)}, u32[]{:S(2)}) collective-permute-start(bf16[4,2,2,64,2048]{4,3,2,1,0:T(8,128)(2,1)} %get-tuple-element.103), channel_id=1, source_target_pairs={{0,2},{2,0},{4,6},{6,4},{8,10},{10,8},{12,14},{14,12},{16,18},{18,... | collective-permute-start | bytes 12582920 | tf_op jit(solution)/shard_map/ppermute | solution.py:1375
  702.3 88.0 %collective-permute-start.78 = (bf16[2,2,4,64,2048]{4,3,2,1,0:T(8,128)(2,1)}, bf16[2,2,4,64,2048]{4,3,2,1,0:T(8,128)(2,1)}, u32[]{:S(2)}, u32[]{:S(2)}) collective-permute-start(bf16[2,2,4,64,2048]{4,3,2,1,0:T(8,128)(2,1)} %get-tuple-element.101), channel_id=1, source_target_pairs={{0,2},{2,0},{4,6},{6,4},{8,10},{10,8},{12,14},{14,12},{16,18},{18,... | collective-permute-start | bytes 12582920 | tf_op jit(solution)/shard_map/ppermute | solution.py:1375
  724.8 70.9 %collective-permute-start.72 = (bf16[2,2,4,64,2048]{4,3,2,1,0:T(8,128)(2,1)}, bf16[2,2,4,64,2048]{4,3,2,1,0:T(8,128)(2,1)}, u32[]{:S(2)}, u32[]{:S(2)}) collective-permute-start(bf16[2,2,4,64,2048]{4,3,2,1,0:T(8,128)(2,1)} %get-tuple-element.99), channel_id=1, source_target_pairs={{0,2},{2,0},{4,6},{6,4},{8,10},{10,8},{12,14},{14,12},{16,18},{18,... | collective-permute-start | bytes 12582920 | tf_op jit(solution)/shard_map/ppermute | solution.py:1375
  745.4 72.3 %collective-permute-start.66 = (bf16[2,2,4,64,2048]{4,3,2,1,0:T(8,128)(2,1)}, bf16[2,2,4,64,2048]{4,3,2,1,0:T(8,128)(2,1)}, u32[]{:S(2)}, u32[]{:S(2)}) collective-permute-start(bf16[2,2,4,64,2048]{4,3,2,1,0:T(8,128)(2,1)} %get-tuple-element.94), channel_id=1, source_target_pairs={{0,2},{2,0},{4,6},{6,4},{8,10},{10,8},{12,14},{14,12},{16,18},{18,... | collective-permute-start | bytes 12582920 | tf_op jit(solution)/shard_map/ppermute | solution.py:1375
  786.4 45.7 %collective-permute-start.64 = (bf16[512,1024]{1,0:T(8,128)(2,1)}, bf16[512,1024]{1,0:T(8,128)(2,1)S(1)}, u32[]{:S(2)}, u32[]{:S(2)}) collective-permute-start(bf16[512,1024]{1,0:T(8,128)(2,1)} %get-tuple-element.182), channel_id=1, source_target_pairs={{0,1},{1,0},{2,3},{3,2},{4,5},{5,4},{6,7},{7,6},{8,9},{9,8},{10,11... | collective-permute-start | bytes 3145736 | tf_op jit(solution)/shard_map/ppermute | solution.py:1367
  795.7 54.0 %collective-permute-start.63 = (bf16[512,1024]{1,0:T(8,128)(2,1)}, bf16[512,1024]{1,0:T(8,128)(2,1)}, u32[]{:S(2)}, u32[]{:S(2)}) collective-permute-start(bf16[512,1024]{1,0:T(8,128)(2,1)} %get-tuple-element.184), channel_id=1, source_target_pairs={{0,1},{1,0},{2,3},{3,2},{4,5},{5,4},{6,7},{7,6},{8,9},{9,8},{10,11... | collective-permute-start | bytes 3145736 | tf_op jit(solution)/shard_map/ppermute | solution.py:1367
  812.7 48.8 %collective-permute-start.79 = (bf16[2,4,64,2048]{3,2,1,0:T(8,128)(2,1)}, bf16[2,4,64,2048]{3,2,1,0:T(8,128)(2,1)S(1)}, u32[]{:S(2)}, u32[]{:S(2)}) collective-permute-start(bf16[2,4,64,2048]{3,2,1,0:T(8,128)(2,1)} %get-tuple-element.168), channel_id=1, source_target_pairs={{0,4},{2,6},{4,0},{6,2},{8,12},{10,14},{12,8},{14,10},{16,20},{18,... | collective-permute-start | bytes 6291464 | tf_op jit(solution)/shard_map/ppermute | solution.py:1371
  817.2 89.2 %collective-permute-start.73 = (bf16[2,4,64,2048]{3,2,1,0:T(8,128)(2,1)}, bf16[2,4,64,2048]{3,2,1,0:T(8,128)(2,1)S(1)}, u32[]{:S(2)}, u32[]{:S(2)}) collective-permute-start(bf16[2,4,64,2048]{3,2,1,0:T(8,128)(2,1)} %get-tuple-element.170), channel_id=1, source_target_pairs={{0,4},{2,6},{4,0},{6,2},{8,12},{10,14},{12,8},{14,10},{16,20},{18,... | collective-permute-start | bytes 6291464 | tf_op jit(solution)/shard_map/ppermute | solution.py:1371
  832.2 112.9 %collective-permute-start.67 = (bf16[2,4,64,2048]{3,2,1,0:T(8,128)(2,1)}, bf16[2,4,64,2048]{3,2,1,0:T(8,128)(2,1)}, u32[]{:S(2)}, u32[]{:S(2)}) collective-permute-start(bf16[2,4,64,2048]{3,2,1,0:T(8,128)(2,1)} %get-tuple-element.172), channel_id=1, source_target_pairs={{0,4},{2,6},{4,0},{6,2},{8,12},{10,14},{12,8},{14,10},{16,20},{18,... | collective-permute-start | bytes 6291464 | tf_op jit(solution)/shard_map/ppermute | solution.py:1371
  857.2 90.9 %collective-permute-start.87 = (bf16[2,2,64,2048]{3,2,1,0:T(8,128)(2,1)S(1)}, bf16[2,2,64,2048]{3,2,1,0:T(8,128)(2,1)S(1)}, u32[]{:S(2)}, u32[]{:S(2)}) collective-permute-start(bf16[2,2,64,2048]{3,2,1,0:T(8,128)(2,1)S(1)} %fusion.6), channel_id=1, source_target_pairs={{0,8},{2,10},{4,12},{6,14},{8,16},{10,18},{12,20},{14,22},{16,24},... | collective-permute-start | bytes 3145736 | tf_op jit(solution)/shard_map/ppermute | solution.py:1379
  862.3 89.1 %collective-permute-start.80 = (bf16[4,64,2048]{2,1,0:T(8,128)(2,1)S(1)}, bf16[4,64,2048]{2,1,0:T(8,128)(2,1)S(1)}, u32[]{:S(2)}, u32[]{:S(2)}) collective-permute-start(bf16[4,64,2048]{2,1,0:T(8,128)(2,1)S(1)} %get-tuple-element.174), channel_id=1, source_target_pairs={{0,1},{1,0},{2,3},{3,2},{4,5},{5,4},{6,7},{7,6},{8,9},{9,8},{10,11... | collective-permute-start | bytes 3145736 | tf_op jit(solution)/shard_map/ppermute | solution.py:1367
  (178 other events, 4171.8 us)
Sparse Core Ops, SparseCore 0:
  184.4 115.4 all-reduce.2

commit v2 on v1

--- a/solution.py
+++ b/solution.py
@@ -477,7 +477,7 @@
 LOG2E = 1.4426950408889634
 LN2 = 0.6931471805599453
 VM = pltpu.VMEM
-ANYM = pl.ANY
+ANYM = pltpu.HBM
 F32 = jnp.float32
 BF = jnp.bfloat16
 NT_DIMS = (((1,), (1,)), ((), ()))
@@ -504,12 +504,50 @@
     return pl.CostEstimate(flops=int(flops), bytes_accessed=int(data), transcendentals=int(exps))
 
 
+def gated_call(after, kernel, *, grid_spec, out_shape, through=(), input_output_aliases=None, **settings):
+    scalars, reads = grid_spec["num_scalar_prefetch"], len(grid_spec["in_specs"])
+    used = scalars + reads
+    after, through = values_of(after), list(through)
+    single = not isinstance(out_shape, list)
+    shapes = [out_shape] if single else out_shape
+    out_specs = [grid_spec["out_specs"]] if single else list(grid_spec["out_specs"])
+    outs, waits = len(shapes), len(after) + len(through)
+
+    def body_of(*refs):
+        kernel(*refs[:used], *refs[used + waits : used + waits + outs], *refs[used + waits + outs + len(through) :])
+
+    anywhere = pl.BlockSpec(memory_space=ANYM)
+    spec = dict(
+        grid_spec,
+        in_specs=list(grid_spec["in_specs"]) + [anywhere] * waits,
+        out_specs=out_specs + [anywhere] * len(through),
+    )
+    aliases = dict(input_output_aliases or {})
+    aliases.update({used + len(after) + i: outs + i for i in range(len(through))})
+    passed = values_of(through)
+    call = pl.pallas_call(body_of,
+        grid_spec=pltpu.PrefetchScalarGridSpec(**spec),
+        out_shape=list(shapes) + [jax.ShapeDtypeStruct(value.shape, value.dtype) for value in passed],
+        input_output_aliases=aliases,
+        **settings,
+    )
+
+    def run(*operands):
+        results = call(*values_of(operands), *after, *passed)
+        for cell, value in zip(through, results[outs:]):
+            cell.value = value
+        return results[0] if single else results[:outs]
+
+    return run
+
+
 def flow_meta(kind):
+    corners = [(0, 0), (1, 0), (0, 1), (1, 1)]
     if kind == "zxy":
-        quads = [(0, 0), (1, 0), (0, 1), (1, 1)]
-        return [[(k, y, c, x) for k in range(4)] for c in range(2) for (x, y) in quads]
-    quads = [(0, 0), (1, 0), (0, 1), (1, 1)]
-    return [[(k, y, c, x) for (x, y) in quads] for c in range(2) for k in range(4)]
+        near = [[(k, y, 0, x) for k in range(4)] for (x, y) in corners]
+    else:
+        near = [[(k, y, 0, x) for (x, y) in corners] for k in range(4)]
+    return near + [[(k, y, 1, x) for quad in near for (k, y, _, x) in quad]]
 
 
 def place_of(info, meta):
@@ -532,6 +570,16 @@
             ).start()
 
 
+def start_all(pieces, first, width, buffer, sems):
+    (ref,) = pieces
+    for device in range(32):
+        pltpu.make_async_copy(
+            ref.at[device, :, pl.ds(first, width)],
+            buffer.at[device % 2, pl.ds(device // 2 * 64, 64), :],
+            sems.at[device % 2],
+        ).start()
+
+
 def wait_weight(buffer, sems, slab):
     pltpu.make_async_copy(buffer.at[slab], buffer.at[slab], sems.at[slab]).wait()
 
@@ -561,17 +609,20 @@
 
 
 ROWS = 256
+QB = 256
 
 
 def qkv_kernel(info, par, x_ref, *rest):
-    pieces, rest = rest[:24], rest[24:]
+    pieces, rest = rest[:10], rest[10:]
     q_ref, k_ref, v_ref, nt_ref, wq, wk, wv, sems = rest
     weights = (wq, wk, wv)
 
     @pl.when(pl.program_id(0) == 0)
     def _():
+        start_self(info, pieces, weights, sems)
         for t in range(3):
-            start_weight(info, pieces[8 * t : 8 * t + 8], KINDS[t], 0, 512, weights[t], sems.at[t])
+            for slab in range(2):
+                wait_weight(weights[t], sems.at[t], slab)
 
     unit, _ = ln_parts(x_ref[...].astype(F32))
     normed = (unit * par[0:1, :] + par[3:4, :]).astype(BF)
@@ -579,9 +630,6 @@
     for t in range(3):
         for slab in range(2):
 
-            @pl.when(pl.program_id(0) == 0)
-            def _():
-                wait_weight(weights[t], sems.at[t], slab)
 
             cols = slice(slab * 512, slab * 512 + 512)
             value = mm(normed, weights[t][slab])
@@ -592,48 +640,53 @@
             (q_ref, k_ref, v_ref)[t][:, cols] = value.astype(BF)
 
 
-KINDS = ("zxy", "xyz", "zxy")
-
-
-def call_qkv(info, par, x, pieces):
+def start_self(info, pieces, weights, sems):
+    start_weight(info, pieces[:5], "zxy", 0, 512, weights[0], sems.at[0])
+    start_weight(info, pieces[5:], "xyz", 0, 512, weights[1], sems.at[1])
+    start_weight(info, pieces[:5], "zxy", 512, 512, weights[2], sems.at[2])
+
+
+def call_qkv(info, par, x, pieces, after=(), through=()):
     n = x.shape[0]
     out = jax.ShapeDtypeStruct((n, 1024), BF)
     rows = pl.BlockSpec((ROWS, 1024), lambda i, s: (i, 0))
-    return pl.pallas_call(
+    return gated_call(
+        after,
         qkv_kernel,
-        grid_spec=pltpu.PrefetchScalarGridSpec(
+        grid_spec=dict(
             num_scalar_prefetch=1,
             grid=(n // ROWS,),
             in_specs=[pl.BlockSpec((24, 1024), lambda i, s: (0, 0)), rows]
-            + [pl.BlockSpec(memory_space=ANYM)] * 24,
+            + [pl.BlockSpec(memory_space=ANYM)] * 10,
             out_specs=[rows, rows, rows, pl.BlockSpec((1024, ROWS), lambda i, s: (0, i))],
             scratch_shapes=[VM((2, 1024, 512), BF)] * 3 + [pltpu.SemaphoreType.DMA((3, 2))],
         ),
         out_shape=[out, out, out, jax.ShapeDtypeStruct((1024, n), BF)],
-        compiler_params=params_of(48),
+        compiler_params=params_of(60),
         cost_estimate=cost(6.4e9, 16e6),
+        through=through,
         name="project_self",
     )(info, par, x, *pieces)
 
 
 def kv_kernel(info, par, x_ref, *rest):
-    pieces, rest = rest[:8], rest[8:]
+    pieces, rest = rest[:1], rest[1:]
     k_ref, v_ref, nt_ref, wk, wv, sems = rest
     weights = (wk, wv)
 
     @pl.when(pl.program_id(0) == 0)
     def _():
         for t in range(2):
-            start_weight(info, pieces, "zxy", t * 512, 512, weights[t], sems.at[t])
+            start_all(pieces, t * 512, 512, weights[t], sems.at[t])
+        for t in range(2):
+            for slab in range(2):
+                wait_weight(weights[t], sems.at[t], slab)
 
     rows = x_ref[...]
     nt_ref[...] = transposed(rows)
     for t in range(2):
         for slab in range(2):
 
-            @pl.when(pl.program_id(0) == 0)
-            def _():
-                wait_weight(weights[t], sems.at[t], slab)
 
             cols = slice(slab * 512, slab * 512 + 512)
             value = mm(rows, weights[t][slab])
@@ -642,23 +695,25 @@
             (k_ref, v_ref)[t][:, cols] = value.astype(BF)
 
 
-def call_kv(info, par, x, pieces):
+def call_kv(info, par, x, pieces, after=(), through=()):
     n = x.shape[0]
     out = jax.ShapeDtypeStruct((n, 1024), BF)
     rows = pl.BlockSpec((ROWS, 1024), lambda i, s: (i, 0))
-    return pl.pallas_call(
+    return gated_call(
+        after,
         kv_kernel,
-        grid_spec=pltpu.PrefetchScalarGridSpec(
+        grid_spec=dict(
             num_scalar_prefetch=1,
             grid=(n // ROWS,),
             in_specs=[pl.BlockSpec((24, 1024), lambda i, s: (0, 0)), rows]
-            + [pl.BlockSpec(memory_space=ANYM)] * 8,
+            + [pl.BlockSpec(memory_space=ANYM)],
             out_specs=[rows, rows, pl.BlockSpec((1024, ROWS), lambda i, s: (0, i))],
             scratch_shapes=[VM((2, 1024, 512), BF)] * 2 + [pltpu.SemaphoreType.DMA((2, 2))],
         ),
         out_shape=[out, out, jax.ShapeDtypeStruct((1024, n), BF)],
-        compiler_params=params_of(48),
+        compiler_params=params_of(60),
         cost_estimate=cost(4.3e9, 12e6),
+        through=through,
         name="project_memory",
     )(info, par, x, *pieces)
 
@@ -674,15 +729,12 @@
     return (high, middle, (rest - middle.astype(F32)).astype(BF))
 
 
-def attend_kernel(causal, info, q_ref, k_ref, v_ref, o_ref, lse_ref):
+def attend_kernel(causal, info, q_ref, k_ref, v_ref, *rest):
+    o_ref, lse_ref = rest[-2:]
+    lse_ref = lse_ref.at[0]
     n, nk = q_ref.shape[0], k_ref.shape[0]
-    pair = pl.program_id(0)
-    lanes_k, lanes_q = lane_ids(nk), lane_ids(ROWS)
+    lanes_k, lanes_q = lane_ids(nk), lane_ids(QB)
     lane_all = lane_ids(n)
-
-    @pl.when(pair == 0)
-    def _():
-        lse_ref[...] = jnp.zeros(lse_ref.shape, F32)
 
     one = jnp.ones((), BF)
     zero = jnp.zeros((), BF)
@@ -697,158 +749,198 @@
             keys = jnp.where(lanes_k == spare, shut, keys)
         k_aug.append(keys)
         v_aug.append(jnp.where(own, v_ref[...], jnp.where(lanes_k == spare, one, zero)))
-    for first in range(0, n, ROWS):
-        span = first + ROWS if causal else nk
-        block = q_ref[first : first + ROWS, :]
-        outs, lses = [], []
-        for head in range(2):
-            spare = 0 if head else 64
-            query = block if causal else jnp.where(lanes_q == spare, one, block)
-            scores = mm_nt(query, k_aug[head][:span])
-            if causal:
-                row = lax.broadcasted_iota(jnp.int32, (ROWS, ROWS), 0)
-                col = lax.broadcasted_iota(jnp.int32, (ROWS, ROWS), 1)
-                last = jnp.where(col <= row, scores[:, first:], floor_score)
-                scores = jnp.concatenate([scores[:, :first], last], 1) if first else last
-            highest = jnp.max(scores, -1, keepdims=True)
-            raised = jnp.exp2(scores - highest).astype(BF)
-            mixed = mm(raised, v_aug[head][:span])
-            total = jnp.sum(jnp.where(lanes_q == spare, mixed, 0.0), -1, keepdims=True)
-            outs.append(mixed * (1.0 / total))
-            lses.append(highest + jnp.log2(total))
-        o_ref[first : first + ROWS, :] = jnp.where(lanes_q < 64, outs[0], outs[1]).astype(BF)
-        held = lse_ref[first : first + ROWS, :]
-        held = jnp.where(lanes_q == 2 * pair, lses[0], held)
-        lse_ref[first : first + ROWS, :] = jnp.where(lanes_q == 2 * pair + 1, lses[1], held)
-
-
-def call_attend(info, q, k, v, causal):
+    items = [(first, head) for first in range(0, n, QB) for head in range(2)]
+
+    def scores_of(first, head):
+        span = first + QB if causal else nk
+        block = q_ref[first : first + QB, :]
+        query = block if causal else jnp.where(lanes_q == (0 if head else 64), one, block)
+        scores = mm_nt(query, k_aug[head][:span])
+        if causal:
+            row = lax.broadcasted_iota(jnp.int32, (QB, QB), 0)
+            col = lax.broadcasted_iota(jnp.int32, (QB, QB), 1)
+            last = jnp.where(col <= row, scores[:, first:], floor_score)
+            scores = jnp.concatenate([scores[:, :first], last], 1) if first else last
+        return scores
+
+    ahead = scores_of(*items[0])
+    for index, (first, head) in enumerate(items):
+        scores = ahead
+        if index + 1 < len(items):
+            ahead = scores_of(*items[index + 1])
+        span = first + QB if causal else nk
+        highest = jnp.max(scores, -1, keepdims=True)
+        raised = jnp.exp2(scores - highest).astype(BF)
+        mixed = mm(raised, v_aug[head][:span])
+        total = jnp.sum(jnp.where(lanes_q == (0 if head else 64), mixed, 0.0), -1, keepdims=True)
+        out, lse = mixed * (1.0 / total), highest + jnp.log2(total)
+        if head == 0:
+            out_a, lse_a = out, lse
+        else:
+            o_ref[first : first + QB, :] = jnp.where(lanes_q < 64, out_a, out).astype(BF)
+            lse_ref[first : first + QB, :] = jnp.where(lanes_q < 64, lse, lse_a)
+
+
+def call_attend(info, q, k, v, causal, first, count, earlier=None, after=(), through=()):
     n, nk = q.shape[0], k.shape[0]
-    part = 0.625 if causal else 1.0
-    heads = lambda rows: pl.BlockSpec((rows, 128), lambda i, s: (0, i))
-    return pl.pallas_call(
+    part = (0.625 if causal else 1.0) * count / 8
+    heads = lambda rows: pl.BlockSpec((rows, 128), lambda i, s: (0, i + first))
+    held = () if earlier is None else tuple(earlier)
+    return gated_call(
+        after,
         partial(attend_kernel, causal),
-        grid_spec=pltpu.PrefetchScalarGridSpec(
+        grid_spec=dict(
             num_scalar_prefetch=1,
-            grid=(q.shape[1] // 128,),
-            in_specs=[heads(n), heads(nk), heads(nk)],
-            out_specs=[heads(n), pl.BlockSpec((n, 128), lambda i, s: (0, 0))],
+            grid=(count,),
+            in_specs=[heads(n), heads(nk), heads(nk)] + [pl.BlockSpec(memory_space=ANYM)] * len(held),
+            out_specs=[heads(n), pl.BlockSpec((1, n, 128), lambda i, s: (i + first, 0, 0))],
         ),
-        out_shape=[jax.ShapeDtypeStruct((n, 1024), BF), jax.ShapeDtypeStruct((n, 128), F32)],
-        compiler_params=params_of(48),
-        cost_estimate=cost(16e9 * part, 9e6, 17e6 * part),
+        out_shape=[jax.ShapeDtypeStruct((n, 1024), BF), jax.ShapeDtypeStruct((8, n, 128), F32)],
+        input_output_aliases={4: 0, 5: 1} if held else {},
+        compiler_params=params_of(60),
+        cost_estimate=cost(110.4e9 * part, 1e6),
         name="attend_self" if causal else "attend_cross",
-    )(info, q, k, v)
-
-
-def attend_back_kernel(causal, info, q_ref, k_ref, v_ref, o_ref, g_ref, lse_ref, dq_ref, dk_ref, dv_ref, bias_ref, acc):
+    )(info, q, k, v, *held)
+
+
+def attend_back_kernel(causal, info, q_ref, k_ref, v_ref, o_ref, g_ref, lse_ref, *rest):
+    dq_ref, dk_ref, dv_ref, bias_ref, acc = rest[-5:]
+    lse_ref = lse_ref.at[0]
     n, nk = q_ref.shape[0], k_ref.shape[0]
-    pair = pl.program_id(0)
     lanes_k, lanes_q = lane_ids(nk), lane_ids(n)
     one = jnp.ones((), BF)
     zero = jnp.zeros((), BF)
-    block_rows = 256
+    block_rows = 256 if causal else 512
     q_all, g_all = q_ref[...], g_ref[...]
+    k_turned = k_ref[...].T
     product = g_all.astype(F32) * o_ref[...].astype(F32)
+    row = lax.broadcasted_iota(jnp.int32, (128, 128), 0)
+    col = lax.broadcasted_iota(jnp.int32, (128, 128), 1)
+    crossing = jnp.where((row < 64) != (col < 64), one, zero)
+    inner = sum(mm(part, crossing) for part in split3(product))
+    slot_q, slot_k = lanes_q % 64, lanes_k % 64
+
+    def in_slots(column):
+        first, second, third = split3(-column)
+        rest = jnp.where(slot_q == 2, third, jnp.where(slot_q == 3, one, zero))
+        return jnp.where(slot_q == 0, first, jnp.where(slot_q == 1, second, rest))
+
+    spare_q, spare_g = in_slots(lse_ref[...]), in_slots(inner)
+    spare_v = jnp.where(slot_k < 3, one, zero)
+    spare_k = spare_v
+    if not causal:
+        place = lax.broadcasted_iota(jnp.int32, (nk, 128), 0)
+        shut = jnp.where(place < info[4], 0.0, floor_score).astype(BF)
+        spare_k = jnp.where(slot_k == 3, shut, spare_k)
+    k_all, v_all = k_ref[...], v_ref[...]
     sets = []
     for head in range(2):
         own_k = (lanes_k >= 64) if head else (lanes_k < 64)
         own_q = (lanes_q >= 64) if head else (lanes_q < 64)
-        at = 0 if head else 64
-        inner = jnp.sum(jnp.where(own_q, product, 0.0), -1, keepdims=True)
-        lse = jnp.sum(jnp.where(lanes_q == 2 * pair + head, lse_ref[...], 0.0), -1, keepdims=True)
-        q_own = jnp.where(own_q, q_all, zero)
-        g_own = jnp.where(own_q, g_all, zero)
-        q_aug, g_aug = q_own, g_own
-        for step, (part_q, part_g) in enumerate(zip(split3(-lse), split3(-inner))):
-            q_aug = jnp.where(lanes_q == at + step, part_q, q_aug)
-            g_aug = jnp.where(lanes_q == at + step, part_g, g_aug)
-        q_aug = jnp.where(lanes_q == at + 3, one, q_aug)
-        ones_k = (lanes_k >= at) & (lanes_k < at + 3)
-        k_own = jnp.where(own_k, k_ref[...], zero)
-        k_aug = jnp.where(ones_k, one, k_own)
-        if not causal:
-            place = lax.broadcasted_iota(jnp.int32, (nk, 128), 0)
-            shut = jnp.where(place < info[4], 0.0, floor_score).astype(BF)
-            k_aug = jnp.where(lanes_k == at + 3, shut, k_aug)
-        v_aug = jnp.where(ones_k, one, jnp.where(own_k, v_ref[...], zero))
-        sets.append((q_own, g_own, q_aug, g_aug, k_own, k_aug, v_aug))
-    for first in range(0, nk, block_rows):
+        sets.append(
+            (
+                jnp.where(own_q, q_all, zero),
+                jnp.where(own_q, g_all, zero),
+                jnp.where(own_q, q_all, spare_q),
+                jnp.where(own_q, g_all, spare_g),
+                jnp.where(own_k, k_all, spare_k),
+                jnp.where(own_k, v_all, spare_v),
+            )
+        )
+    items = [(first, head) for first in range(0, nk, block_rows) for head in range(2)]
+
+    def scores_of(first, head):
         from_q = first if causal else 0
-        dv = dk = None
-        dq = None
-        for head in range(2):
-            q_own, g_own, q_aug, g_aug, k_own, k_aug, v_aug = sets[head]
-            keys = slice(first, first + block_rows)
-            scores = mm_nt(k_aug[keys], q_aug[from_q:])
-            if causal:
-                row = lax.broadcasted_iota(jnp.int32, (block_rows, block_rows), 0)
-                col = lax.broadcasted_iota(jnp.int32, (block_rows, block_rows), 1)
-                head_part = jnp.where(col >= row, scores[:, :block_rows], floor_score)
-                if first + block_rows < n:
-                    scores = jnp.concatenate([head_part, scores[:, block_rows:]], 1)
-                else:
-                    scores = head_part
-            probs = jnp.exp2(scores)
-            grad_probs = mm_nt(v_aug[keys], g_aug[from_q:])
-            grad_scores = (probs * grad_probs).astype(BF)
-            add_v = mm(probs.astype(BF), g_own[from_q:])
-            add_k = mm(grad_scores, q_own[from_q:])
-            add_q = mm_tn(grad_scores, k_own[keys])
-            dv = add_v if dv is None else dv + add_v
-            dk = add_k if dk is None else dk + add_k
-            dq = add_q if dq is None else dq + add_q
-        dv = dv.astype(BF)
-        dv_ref[first : first + block_rows, :] = dv
-        dk_ref[first : first + block_rows, :] = (dk * LN2).astype(BF)
-        sums = row_sum(dv.astype(F32))
-        if first == 0:
-            acc[...] = dq
-            bias_ref[1:2, :] = sums
+        q_own, g_own, q_aug, g_aug, k_aug, v_aug = sets[head]
+        keys = slice(first, first + block_rows)
+        scores = mm_nt(k_aug[keys], q_aug[from_q:])
+        if causal:
+            row = lax.broadcasted_iota(jnp.int32, (block_rows, block_rows), 0)
+            col = lax.broadcasted_iota(jnp.int32, (block_rows, block_rows), 1)
+            head_part = jnp.where(col >= row, scores[:, :block_rows], floor_score)
+            if first + block_rows < n:
+                scores = jnp.concatenate([head_part, scores[:, block_rows:]], 1)
+            else:
+                scores = head_part
+        return (scores, mm_nt(v_aug[keys], g_aug[from_q:]))
+
+    ahead = scores_of(*items[0])
+    acc[...] = jnp.zeros(acc.shape, F32)
+    bias = None
+    for index, (first, head) in enumerate(items):
+        scores, grad_probs = ahead
+        if index + 1 < len(items):
+            ahead = scores_of(*items[index + 1])
+        from_q = first if causal else 0
+        q_own, g_own, q_aug, g_aug, k_aug, v_aug = sets[head]
+        keys = slice(first, first + block_rows)
+        probs = jnp.exp2(scores)
+        grad_scores = (probs * grad_probs).astype(BF)
+        add_v = mm(probs.astype(BF), g_own[from_q:])
+        add_k = mm(grad_scores, q_own[from_q:])
+        own = slice(64 * head, 64 * head + 64)
+        acc[own, from_q:] += mm(k_turned[own, keys], grad_scores)
+        if head == 0:
+            dv, dk = add_v, add_k
         else:
-            acc[from_q:, :] += dq
-            bias_ref[1:2, :] += sums
-    dq = acc[...].astype(BF) * jnp.asarray(0.125, BF)
+            dv = (dv + add_v).astype(BF)
+            dv_ref[keys, :] = dv
+            dk_ref[keys, :] = ((dk + add_k) * LN2).astype(BF)
+            sums = row_sum(dv.astype(F32))
+            bias = sums if bias is None else bias + sums
+    bias_ref[1:2, :] = bias
+    dq = acc[...].T.astype(BF) * jnp.asarray(0.125, BF)
     dq_ref[...] = dq
     bias_ref[0:1, :] = row_sum(dq.astype(F32))
 
 
-def call_attend_back(info, q, k, v, o, g, lse, causal):
+def own_or_other(info, other):
+    return 1 - info[3] if other else info[3]
+
+
+def call_attend_back(info, q, k, v, o, g, lse, causal, first, count, earlier=None, other=None, after=(), through=()):
     n, nk = q.shape[0], k.shape[0]
-    part = 0.625 if causal else 1.0
-    heads = lambda rows: pl.BlockSpec((rows, 128), lambda i, s: (0, i))
+    part = (0.625 if causal else 1.0) * count / 8
+    place = lambda i, s: i + first if other is None else i + first + 4 * own_or_other(s, other)
+    heads = lambda rows: pl.BlockSpec((rows, 128), lambda i, s: (0, place(i, s)))
     out = lambda rows: jax.ShapeDtypeStruct((rows, 1024), BF)
-    return pl.pallas_call(
+    held = () if earlier is None else tuple(earlier)
+    return gated_call(
+        after,
         partial(attend_back_kernel, causal),
-        grid_spec=pltpu.PrefetchScalarGridSpec(
+        grid_spec=dict(
             num_scalar_prefetch=1,
-            grid=(q.shape[1] // 128,),
-            in_specs=[heads(n), heads(nk), heads(nk), heads(n), heads(n), pl.BlockSpec((n, 128), lambda i, s: (0, 0))],
+            grid=(count,),
+            in_specs=[heads(n), heads(nk), heads(nk), heads(n), heads(n)]
+            + [pl.BlockSpec((1, n, 128), lambda i, s: (place(i, s), 0, 0))]
+            + [pl.BlockSpec(memory_space=ANYM)] * len(held),
             out_specs=[heads(n), heads(nk), heads(nk), heads(8)],
-            scratch_shapes=[VM((n, 128), F32)],
+            scratch_shapes=[VM((128, n), F32)],
         ),
         out_shape=[out(n), out(nk), out(nk), jax.ShapeDtypeStruct((8, 1024), F32)],
-        compiler_params=params_of(56),
-        cost_estimate=cost(40e9 * part, 20e6, 17e6 * part),
+        input_output_aliases={7: 0, 8: 1, 9: 2, 10: 3} if held else {},
+        compiler_params=params_of(60),
+        cost_estimate=cost(142.6e9 * part, 1e6),
         name="attend_back_self" if causal else "attend_back_cross",
-    )(info, q, k, v, o, g, lse)
+    )(info, q, k, v, o, g, lse, *held)
 
 
 def after_self_kernel(info, par, x_ref, o_ref, *rest):
-    pieces, rest = rest[:8], rest[8:]
+    pieces, rest = rest[:1], rest[1:]
     h_ref, q_ref, nt_ref, wo, wq, sems = rest
 
     @pl.when(pl.program_id(0) == 0)
     def _():
-        start_weight(info, pieces, "zxy", 1024, 512, wo, sems.at[0])
-        start_weight(info, pieces, "zxy", 1536, 512, wq, sems.at[1])
+        start_all(pieces, 1024, 512, wo, sems.at[0])
+        start_all(pieces, 1536, 512, wq, sems.at[1])
+        for slab in range(2):
+            wait_weight(wo, sems.at[0], slab)
+        for slab in range(2):
+            wait_weight(wq, sems.at[1], slab)
 
     total = x_ref[...].astype(F32) + par[6:7, :]
     for slab in range(2):
 
-        @pl.when(pl.program_id(0) == 0)
-        def _():
-            wait_weight(wo, sems.at[0], slab)
 
         total = total + mm_nt(o_ref[:, slab * 512 : slab * 512 + 512], wo[slab])
     h_ref[...] = total
@@ -857,25 +949,23 @@
     nt_ref[...] = transposed(normed)
     for slab in range(2):
 
-        @pl.when(pl.program_id(0) == 0)
-        def _():
-            wait_weight(wq, sems.at[1], slab)
 
         cols = slice(slab * 512, slab * 512 + 512)
         value = (mm(normed, wq[slab]) + par[11:12, cols]) * (0.125 * LOG2E)
         q_ref[:, cols] = value.astype(BF)
 
 
-def call_after_self(info, par, x, o, pieces):
+def call_after_self(info, par, x, o, pieces, after=(), through=()):
     n = x.shape[0]
     rows = pl.BlockSpec((ROWS, 1024), lambda i, s: (i, 0))
-    return pl.pallas_call(
+    return gated_call(
+        after,
         after_self_kernel,
-        grid_spec=pltpu.PrefetchScalarGridSpec(
+        grid_spec=dict(
             num_scalar_prefetch=1,
             grid=(n // ROWS,),
             in_specs=[pl.BlockSpec((24, 1024), lambda i, s: (0, 0)), rows, rows]
-            + [pl.BlockSpec(memory_space=ANYM)] * 8,
+            + [pl.BlockSpec(memory_space=ANYM)],
             out_specs=[rows, rows, pl.BlockSpec((1024, ROWS), lambda i, s: (0, i))],
             scratch_shapes=[VM((2, 1024, 512), BF)] * 2 + [pltpu.SemaphoreType.DMA((2, 2))],
         ),
@@ -884,20 +974,23 @@
             jax.ShapeDtypeStruct((n, 1024), BF),
             jax.ShapeDtypeStruct((1024, n), BF),
         ],
-        compiler_params=params_of(48),
+        compiler_params=params_of(60),
         cost_estimate=cost(4.3e9, 16e6),
+        through=through,
         name="after_self",
     )(info, par, x, o, *pieces)
 
 
 def after_cross_kernel(info, par, scale, h_in, o_ref, cot_ref, *rest):
-    pieces, rest = rest[:8], rest[8:]
+    pieces, rest = rest[:1], rest[1:]
     h_ref, n_ref, nt_ref, g_ref, gt_ref, gsum_ref, wo, sems = rest
     step = pl.program_id(0)
 
     @pl.when(step == 0)
     def _():
-        start_weight(info, pieces, "zxy", 2048, 512, wo, sems)
+        start_all(pieces, 4096, 512, wo, sems)
+        for slab in range(2):
+            wait_weight(wo, sems, slab)
 
     place = step * ROWS + lax.broadcasted_iota(jnp.int32, (ROWS, 1), 0)
     weight = jnp.where(place < info[5], scale[0, 0], 0.0)
@@ -915,9 +1008,6 @@
     total = h_in[...] + par[7:8, :]
     for slab in range(2):
 
-        @pl.when(step == 0)
-        def _():
-            wait_weight(wo, sems, slab)
 
         total = total + mm_nt(o_ref[:, slab * 512 : slab * 512 + 512], wo[slab])
     h_ref[...] = total
@@ -927,15 +1017,16 @@
     nt_ref[...] = transposed(normed)
 
 
-def call_after_cross(info, par, scale, h, o, cot, pieces):
+def call_after_cross(info, par, scale, h, o, cot, pieces, after=(), through=()):
     n = h.shape[0]
     rows = pl.BlockSpec((ROWS, 1024), lambda i, s: (i, 0))
     turned = pl.BlockSpec((1024, ROWS), lambda i, s: (0, i))
     act = jax.ShapeDtypeStruct((n, 1024), BF)
     act_t = jax.ShapeDtypeStruct((1024, n), BF)
-    return pl.pallas_call(
+    return gated_call(
+        after,
         after_cross_kernel,
-        grid_spec=pltpu.PrefetchScalarGridSpec(
+        grid_spec=dict(
             num_scalar_prefetch=1,
             grid=(n // ROWS,),
             in_specs=[
@@ -945,7 +1036,7 @@
                 rows,
                 rows,
             ]
-            + [pl.BlockSpec(memory_space=ANYM)] * 8,
+            + [pl.BlockSpec(memory_space=ANYM)],
             out_specs=[rows, rows, turned, rows, turned, pl.BlockSpec((8, 1024), lambda i, s: (0, 0))],
             scratch_shapes=[VM((2, 1024, 512), BF), pltpu.SemaphoreType.DMA((2,))],
         ),
@@ -957,8 +1048,9 @@
             act_t,
             jax.ShapeDtypeStruct((8, 1024), F32),
         ],
-        compiler_params=params_of(48),
+        compiler_params=params_of(60),
         cost_estimate=cost(2.2e9, 26e6),
+        through=through,
         name="after_cross",
     )(info, par, scale, h, o, cot, *pieces)
 
@@ -985,8 +1077,8 @@
 
 
 def ffn_kernel(info, par, bias_ref, n_ref, nt_ref, g_ref, gt_ref, h_ref, *rest):
-    pieces_in, pieces_out, rest = rest[:8], rest[8:16], rest[16:]
-    (out_ref, dn_ref, send_in, keep_in, send_out, keep_out, dbias_ref, w_in, w_out, acc, active, du, temp, sems) = rest
+    pieces, rest = rest[:1], rest[1:]
+    (out_ref, dn_ref, send_ref, keep_ref, dbias_ref, w_in, w_out, acc, active, du, temp, sems) = rest
     half, part = pl.program_id(0), pl.program_id(1)
     parts = pl.num_programs(1)
     n = n_ref.shape[0]
@@ -995,8 +1087,10 @@
 
     @pl.when(first_step)
     def _():
-        start_weight(info, pieces_in, "zxy", 0, 2048, w_in, sems.at[0])
-        start_weight(info, pieces_out, "xyz", 0, 2048, w_out, sems.at[1])
+        start_all(pieces, 0, 2048, w_in, sems.at[0])
+        start_all(pieces, 2048, 2048, w_out, sems.at[1])
+        acc[...] = jnp.zeros(acc.shape, F32)
+        dn_ref[...] = jnp.zeros(dn_ref.shape, F32)
 
     @pl.when(part == 0)
     def _():
@@ -1024,53 +1118,36 @@
         up = mm_nt(r, second[...])
         down = mm_nt(d, first[...])
 
-        @pl.when(first_step)
-        def _():
-            acc[rows, :] = up
-            dn_ref[rows, :] = down
-
-        @pl.when(jnp.logical_not(first_step))
-        def _():
-            acc[rows, :] += up
-            dn_ref[rows, :] += down
+        acc[rows, :] += up
+        dn_ref[rows, :] += down
 
     dbias_ref[0:1, :] = total_bias
     for zrel in range(4):
         zz = lax.rem(info[0] + zrel, 4)
         rows = pl.ds(pl.multiple_of(zz * 256, 256), 256)
-        temp[...] = mm(nt_ref[rows, :], du[...]).astype(BF)
-        store_blocks(info, temp, send_in, keep_in, zrel, "zxy", FFB)
-        temp[...] = mm(gt_ref[rows, :], active[...]).astype(BF)
-        store_blocks(info, temp, send_out, keep_out, zrel, "xyz", FFB)
+        temp[zrel % 2, :, :FFB] = mm(nt_ref[rows, :], du[...]).astype(BF)
+        temp[zrel % 2, :, FFB:] = mm(gt_ref[rows, :], active[...]).astype(BF)
+        store_blocks(info, temp.at[zrel % 2], send_ref, keep_ref, zrel, "zxy", 2 * FFB)
 
     @pl.when((half == 1) & (part == parts - 1))
     def _():
         for chunk in range(n // ROWS):
-            rows = slice(chunk * ROWS, chunk * ROWS + ROWS)
-            out_ref[rows, :] = (h_ref[rows, :] + acc[rows, :] + par[8:9, :]).astype(BF)
-
-
-def block_out(kind, width, total):
-    if kind == "zxy":
-        shape, block = (2, 2, 4, 64, total), (2, 1, 4, 64, width)
-        spec = lambda index: pl.BlockSpec(block, index(lambda x, t: (0, x, 0, 0, t)))
-    else:
-        shape, block = (4, 2, 2, 64, total), (4, 2, 1, 64, width)
-        spec = lambda index: pl.BlockSpec(block, index(lambda x, t: (0, 0, x, 0, t)))
-    return (jax.ShapeDtypeStruct(shape, BF), spec)
-
-
-def call_ffn(info, par, bias, normed, normed_t, grad, grad_t, hidden, pieces_in, pieces_out):
+            start = lax.rem(info[3] * (n // 2) + chunk * ROWS, n)
+            rows = pl.ds(pl.multiple_of(start, ROWS), ROWS)
+            value = h_ref[rows, :] + acc[rows, :] + par[8:9, :]
+            out_ref[chunk * ROWS : chunk * ROWS + ROWS, :] = value.astype(BF)
+
+
+def call_ffn(info, par, bias, normed, normed_t, grad, grad_t, hidden, pieces, after=(), through=()):
     n = normed.shape[0]
     parts = 2048 // FFB
     whole = lambda shape: pl.BlockSpec(shape, lambda x, t, s: (0, 0))
-    shape_in, spec_in = block_out("zxy", FFB, 2048)
-    shape_out, spec_out = block_out("xyz", FFB, 2048)
-    index = lambda f: (lambda x, t, s: f(x, t))
+    blocks = pl.BlockSpec((2, 1, 4, 64, 2 * FFB), lambda x, t, s: (0, x, 0, 0, t))
     bias_spec = lambda rows: pl.BlockSpec((rows, FFB), lambda x, t, s: (0, lax.rem(x + s[3], 2) * parts + t))
-    return pl.pallas_call(
+    return gated_call(
+        after,
         ffn_kernel,
-        grid_spec=pltpu.PrefetchScalarGridSpec(
+        grid_spec=dict(
             num_scalar_prefetch=1,
             grid=(2, parts),
             in_specs=[
@@ -1082,14 +1159,12 @@
                 whole((1024, n)),
                 whole((n, 1024)),
             ]
-            + [pl.BlockSpec(memory_space=ANYM)] * 16,
+            + [pl.BlockSpec(memory_space=ANYM)],
             out_specs=[
                 whole((n, 1024)),
                 whole((n, 1024)),
-                spec_in(index),
-                spec_in(index),
-                spec_out(index),
-                spec_out(index),
+                blocks,
+                blocks,
                 bias_spec(8),
             ],
             scratch_shapes=[
@@ -1098,34 +1173,35 @@
                 VM((n, 1024), F32),
                 VM((n, FFB), BF),
                 VM((n, FFB), BF),
-                VM((256, FFB), BF),
+                VM((2, 256, 2 * FFB), BF),
                 pltpu.SemaphoreType.DMA((2, 2)),
             ],
         ),
         out_shape=[
             jax.ShapeDtypeStruct((n, 1024), BF),
             jax.ShapeDtypeStruct((n, 1024), F32),
-            shape_in,
-            shape_in,
-            shape_out,
-            shape_out,
+            jax.ShapeDtypeStruct((2, 2, 4, 64, 4096), BF),
+            jax.ShapeDtypeStruct((2, 2, 4, 64, 4096), BF),
             jax.ShapeDtypeStruct((8, 4096), F32),
         ],
         compiler_params=params_of(60),
         cost_estimate=cost(51.5e9, 60e6, 4e6),
+        through=through,
         name="feedforward",
-    )(info, par, bias, normed, normed_t, grad, grad_t, hidden, *pieces_in, *pieces_out)
+    )(info, par, bias, normed, normed_t, grad, grad_t, hidden, *pieces)
 
 
 def back_three_kernel(info, par, dn_ref, h_ref, g_ref, *rest):
-    pieces, rest = rest[:8], rest[8:]
+    pieces, rest = rest[:1], rest[1:]
     dh_ref, do_ref, gt_ref, sum_ref, wo, sems = rest
     step = pl.program_id(0)
 
     @pl.when(step == 0)
     def _():
-        start_weight(info, pieces, "zxy", 2048, 512, wo, sems)
+        start_all(pieces, 4096, 512, wo, sems)
         sum_ref[...] = jnp.zeros(sum_ref.shape, F32)
+        for slab in range(2):
+            wait_weight(wo, sems, slab)
 
     back_rows(par, 2, dn_ref[...], h_ref[...], g_ref[...].astype(F32), dh_ref, gt_ref, sum_ref, do_ref, wo, sems)
 
@@ -1141,23 +1217,21 @@
     gt_ref[...] = transposed(rounded)
     for slab in range(2):
 
-        @pl.when(pl.program_id(0) == 0)
-        def _():
-            wait_weight(wo, sems, slab)
 
         do_ref[:, slab * 512 : slab * 512 + 512] = mm(rounded, wo[slab]).astype(BF)
 
 
-def call_back_three(info, par, dn, h, g, pieces):
+def call_back_three(info, par, dn, h, g, pieces, after=(), through=()):
     n = h.shape[0]
     rows = pl.BlockSpec((ROWS, 1024), lambda i, s: (i, 0))
-    return pl.pallas_call(
+    return gated_call(
+        after,
         back_three_kernel,
-        grid_spec=pltpu.PrefetchScalarGridSpec(
+        grid_spec=dict(
             num_scalar_prefetch=1,
             grid=(n // ROWS,),
             in_specs=[pl.BlockSpec((24, 1024), lambda i, s: (0, 0)), rows, rows, rows]
-            + [pl.BlockSpec(memory_space=ANYM)] * 8,
+            + [pl.BlockSpec(memory_space=ANYM)],
             out_specs=[
                 rows,
                 rows,
@@ -1172,45 +1246,48 @@
             jax.ShapeDtypeStruct((1024, n), BF),
             jax.ShapeDtypeStruct((8, 1024), F32),
         ],
-        compiler_params=params_of(48),
+        compiler_params=params_of(60),
         cost_estimate=cost(2.2e9, 20e6),
+        through=through,
         name="back_three",
     )(info, par, dn, h, g, *pieces)
 
 
 def back_two_kernel(info, par, dq_ref, h_ref, dh2_ref, *rest):
-    pieces, rest = rest[:8], rest[8:]
+    pieces, rest = rest[:1], rest[1:]
     dh_ref, do_ref, gt_ref, sum_ref, wq, wo, sems = rest
     step = pl.program_id(0)
 
     @pl.when(step == 0)
     def _():
-        start_weight(info, pieces, "zxy", 1536, 512, wq, sems.at[0])
-        start_weight(info, pieces, "zxy", 1024, 512, wo, sems.at[1])
+        start_all(pieces, 1536, 512, wq, sems.at[0])
+        start_all(pieces, 1024, 512, wo, sems.at[1])
         sum_ref[...] = jnp.zeros(sum_ref.shape, F32)
+        for slab in range(2):
+            wait_weight(wq, sems.at[0], slab)
+        for slab in range(2):
+            wait_weight(wo, sems.at[1], slab)
 
     dn = None
     for slab in range(2):
 
-        @pl.when(step == 0)
-        def _():
-            wait_weight(wq, sems.at[0], slab)
 
         term = mm_nt(dq_ref[:, slab * 512 : slab * 512 + 512], wq[slab])
         dn = term if dn is None else dn + term
     back_rows(par, 1, dn, h_ref[...], dh2_ref[...], dh_ref, gt_ref, sum_ref, do_ref, wo, sems.at[1])
 
 
-def call_back_two(info, par, dq, h, dh2, pieces):
+def call_back_two(info, par, dq, h, dh2, pieces, after=(), through=()):
     n = h.shape[0]
     rows = pl.BlockSpec((ROWS, 1024), lambda i, s: (i, 0))
-    return pl.pallas_call(
+    return gated_call(
+        after,
         back_two_kernel,
-        grid_spec=pltpu.PrefetchScalarGridSpec(
+        grid_spec=dict(
             num_scalar_prefetch=1,
             grid=(n // ROWS,),
             in_specs=[pl.BlockSpec((24, 1024), lambda i, s: (0, 0)), rows, rows, rows]
-            + [pl.BlockSpec(memory_space=ANYM)] * 8,
+            + [pl.BlockSpec(memory_space=ANYM)],
             out_specs=[
                 rows,
                 rows,
@@ -1225,72 +1302,76 @@
             jax.ShapeDtypeStruct((1024, n), BF),
             jax.ShapeDtypeStruct((8, 1024), F32),
         ],
-        compiler_params=params_of(48),
+        compiler_params=params_of(60),
         cost_estimate=cost(4.3e9, 24e6),
+        through=through,
         name="back_two",
     )(info, par, dq, h, dh2, *pieces)
 
 
 def memory_back_kernel(info, dk_ref, dv_ref, *rest):
-    pieces, rest = rest[:8], rest[8:]
+    pieces, rest = rest[:1], rest[1:]
     out_ref, wk, wv, sems = rest
 
     @pl.when(pl.program_id(0) == 0)
     def _():
-        start_weight(info, pieces, "zxy", 0, 512, wk, sems.at[0])
-        start_weight(info, pieces, "zxy", 512, 512, wv, sems.at[1])
+        start_all(pieces, 0, 512, wk, sems.at[0])
+        start_all(pieces, 512, 512, wv, sems.at[1])
+        for slab in range(2):
+            wait_weight(wk, sems.at[0], slab)
+        for slab in range(2):
+            wait_weight(wv, sems.at[1], slab)
 
     total = None
     for t, (ref, weight) in enumerate(((dk_ref, wk), (dv_ref, wv))):
         for slab in range(2):
 
-            @pl.when(pl.program_id(0) == 0)
-            def _():
-                wait_weight(weight, sems.at[t], slab)
 
             term = mm_nt(ref[:, slab * 512 : slab * 512 + 512], weight[slab])
             total = term if total is None else total + term
     out_ref[...] = total.astype(BF)
 
 
-def call_memory_back(info, dk, dv, pieces):
+def call_memory_back(info, dk, dv, pieces, after=(), through=()):
     n = dk.shape[0]
-    rows = pl.BlockSpec((ROWS, 1024), lambda i, s: (i, 0))
-    return pl.pallas_call(
+    steps = n // 2 // ROWS
+    rows = pl.BlockSpec((ROWS, 1024), lambda i, s: (lax.rem(i + steps * s[3], 2 * steps), 0))
+    return gated_call(
+        after,
         memory_back_kernel,
-        grid_spec=pltpu.PrefetchScalarGridSpec(
+        grid_spec=dict(
             num_scalar_prefetch=1,
             grid=(n // ROWS,),
-            in_specs=[rows, rows] + [pl.BlockSpec(memory_space=ANYM)] * 8,
-            out_specs=rows,
+            in_specs=[rows, rows] + [pl.BlockSpec(memory_space=ANYM)],
+            out_specs=pl.BlockSpec((ROWS, 1024), lambda i, s: (i, 0)),
             scratch_shapes=[VM((2, 1024, 512), BF)] * 2 + [pltpu.SemaphoreType.DMA((2, 2))],
         ),
         out_shape=jax.ShapeDtypeStruct((n, 1024), BF),
-        compiler_params=params_of(48),
+        compiler_params=params_of(60),
         cost_estimate=cost(4.3e9, 12e6),
+        through=through,
         name="memory_back",
     )(info, dk, dv, *pieces)
 
 
 def back_one_kernel(info, par, dq_ref, dk_ref, dv_ref, x_ref, dh1_ref, *rest):
-    pieces, rest = rest[:24], rest[24:]
+    pieces, rest = rest[:10], rest[10:]
     out_ref, sum_ref, wq, wk, wv, sems = rest
     weights = (wq, wk, wv)
     step = pl.program_id(0)
 
     @pl.when(step == 0)
     def _():
+        start_self(info, pieces, weights, sems)
+        sum_ref[...] = jnp.zeros(sum_ref.shape, F32)
         for t in range(3):
-            start_weight(info, pieces[8 * t : 8 * t + 8], KINDS[t], 0, 512, weights[t], sems.at[t])
-        sum_ref[...] = jnp.zeros(sum_ref.shape, F32)
+            for slab in range(2):
+                wait_weight(weights[t], sems.at[t], slab)
 
     dn = None
     for t, ref in enumerate((dq_ref, dk_ref, dv_ref)):
         for slab in range(2):
 
-            @pl.when(step == 0)
-            def _():
-                wait_weight(weights[t], sems.at[t], slab)
 
             term = mm_nt(ref[:, slab * 512 : slab * 512 + 512], weights[t][slab])
             dn = term if dn is None else dn + term
@@ -1301,24 +1382,37 @@
     sum_ref[1:2, :] += row_sum(dn)
 
 
-def call_back_one(info, par, dq, dk, dv, x, dh1, pieces):
+def call_back_one(info, par, dq, dk, dv, x, dh1, pieces, other, after=(), through=()):
     n = x.shape[0]
-    rows = pl.BlockSpec((ROWS, 1024), lambda i, s: (i, 0))
-    return pl.pallas_call(
+    steps = n // 2 // ROWS
+    rows = pl.BlockSpec((ROWS, 1024), lambda i, s: (i + steps * own_or_other(s, other), 0))
+    return gated_call(
+        after,
         back_one_kernel,
-        grid_spec=pltpu.PrefetchScalarGridSpec(
+        grid_spec=dict(
             num_scalar_prefetch=1,
-            grid=(n // ROWS,),
+            grid=(steps,),
             in_specs=[pl.BlockSpec((24, 1024), lambda i, s: (0, 0)), rows, rows, rows, rows, rows]
-            + [pl.BlockSpec(memory_space=ANYM)] * 24,
-            out_specs=[rows, pl.BlockSpec((8, 1024), lambda i, s: (0, 0))],
+            + [pl.BlockSpec(memory_space=ANYM)] * 10,
+            out_specs=[pl.BlockSpec((ROWS, 1024), lambda i, s: (i, 0)), pl.BlockSpec((8, 1024), lambda i, s: (0, 0))],
             scratch_shapes=[VM((2, 1024, 512), BF)] * 3 + [pltpu.SemaphoreType.DMA((3, 2))],
         ),
-        out_shape=[jax.ShapeDtypeStruct((n, 1024), BF), jax.ShapeDtypeStruct((8, 1024), F32)],
-        compiler_params=params_of(48),
+        out_shape=[jax.ShapeDtypeStruct((n // 2, 1024), BF), jax.ShapeDtypeStruct((8, 1024), F32)],
+        compiler_params=params_of(60),
         cost_estimate=cost(6.4e9, 20e6),
+        through=through,
         name="back_one",
     )(info, par, dq, dk, dv, x, dh1, *pieces)
+
+
+def block_out(kind, width, total):
+    if kind == "zxy":
+        shape, block = (2, 2, 4, 64, total), (2, 1, 4, 64, width)
+        spec = lambda index: pl.BlockSpec(block, index(lambda x, t: (0, x, 0, 0, t)))
+    else:
+        shape, block = (4, 2, 2, 64, total), (4, 2, 1, 64, width)
+        spec = lambda index: pl.BlockSpec(block, index(lambda x, t: (0, 0, x, 0, t)))
+    return (jax.ShapeDtypeStruct(shape, BF), spec)
 
 
 def weight_grad_kernel(kind, picks, count, info, *refs):
@@ -1335,13 +1429,14 @@
                 store_blocks(info, temp, send_ref, keep_ref, zrel, kind, 512)
 
 
-def call_weight_grad(info, kind, lefts, rights, picks, name):
+def call_weight_grad(info, kind, lefts, rights, picks, name, after=(), through=()):
     n = rights[0].shape[0]
     shape, spec = block_out(kind, 512, 512 * len(rights))
     index = lambda f: (lambda x, t, s: f(x, t))
-    return pl.pallas_call(
+    return gated_call(
+        after,
         partial(weight_grad_kernel, kind, picks, len(lefts)),
-        grid_spec=pltpu.PrefetchScalarGridSpec(
+        grid_spec=dict(
             num_scalar_prefetch=1,
             grid=(2, len(rights)),
             in_specs=[pl.BlockSpec((1024, n), lambda x, t, s: (0, 0))] * len(lefts)
@@ -1350,16 +1445,85 @@
             scratch_shapes=[VM((256, 512), BF)],
         ),
         out_shape=[shape, shape],
-        compiler_params=params_of(48),
-        cost_estimate=cost(2.15e9 * len(rights), 4e6 * len(rights) + 2e6 * len(lefts)),
+        compiler_params=params_of(60),
+        cost_estimate=cost(10.3e9 * len(rights), 1e6),
+        through=through,
         name=name,
     )(info, *lefts, *rights)
 
 
+def half_grad_kernel(picks, count, info, *refs):
+    lefts, rights = refs[:count], refs[count : count + len(picks)]
+    send_ref, keep_ref, temp = refs[count + len(picks) :]
+    for t, pick in enumerate(picks):
+
+        @pl.when(pl.program_id(0) == t)
+        def _():
+            for zrel in range(4):
+                zz = lax.rem(info[0] + zrel, 4)
+                rows = pl.ds(pl.multiple_of(zz * 256, 256), 256)
+                temp[...] = mm(lefts[pick][rows, :], rights[t][...]).astype(BF)
+                for yrel in range(2):
+                    yy = info[1] if yrel == 0 else 1 - info[1]
+                    for crel, target in enumerate((keep_ref, send_ref)):
+                        cc = info[2] if crel == 0 else 1 - info[2]
+                        row = pl.multiple_of(yy * 128 + cc * 64, 64)
+                        target[yrel, zrel, :, :] = temp[pl.ds(row, 64), :]
+
+
+def call_half_grad(info, other, lefts, rights, picks, name, after=(), through=()):
+    n = rights[0].shape[0]
+    shape = jax.ShapeDtypeStruct((2, 4, 64, 512 * len(rights)), BF)
+    spec = pl.BlockSpec((2, 4, 64, 512), lambda t, s: (0, 0, 0, t))
+    return gated_call(
+        after,
+        partial(half_grad_kernel, picks, len(lefts)),
+        grid_spec=dict(
+            num_scalar_prefetch=1,
+            grid=(len(rights),),
+            in_specs=[pl.BlockSpec((1024, n), lambda t, s: (0, 0))] * len(lefts)
+            + [pl.BlockSpec((n, 512), lambda t, s: (0, own_or_other(s, other)))] * len(rights),
+            out_specs=[spec, spec],
+            scratch_shapes=[VM((256, 512), BF)],
+        ),
+        out_shape=[shape, shape],
+        compiler_params=params_of(60),
+        cost_estimate=cost(10e9, 1e6),
+        through=through,
+        name=name,
+    )(info, *lefts, *rights)
+
+
+def pack_kernel(one_a, one_b, two, three, cot, own, cross, inner, out_ref):
+    out_ref[...] = jnp.zeros(out_ref.shape, F32)
+    out_ref[0:1, :] = one_a[0:1, :] + one_b[0:1, :]
+    out_ref[3:4, :] = one_a[1:2, :] + one_b[1:2, :]
+    for k, ref in ((1, two), (2, three)):
+        out_ref[k : k + 1, :] = ref[0:1, :]
+        out_ref[3 + k : 4 + k, :] = ref[1:2, :]
+        out_ref[5 + k : 6 + k, :] = ref[2:3, :]
+    out_ref[8:9, :] = cot[0:1, :]
+    out_ref[9:11, :] = own[0:2, :]
+    out_ref[11:13, :] = cross[0:2, :]
+    for k in range(4):
+        out_ref[13 + k : 14 + k, :] = inner[0:1, k * 1024 : k * 1024 + 1024]
+
+
+def call_pack(*sums):
+    return pl.pallas_call(
+        pack_kernel,
+        out_shape=jax.ShapeDtypeStruct((24, 1024), F32),
+        compiler_params=params_of(60),
+        name="pack_sums",
+    )(*sums)
+
+
 def along(axis_bit):
     return [(i, i ^ axis_bit) for i in range(16)]
 
 
+NEAR_Z = [(i, i ^ 4) for i in range(16)]
+FAR_Z = [(i, i ^ 8) for i in range(16)]
 RING = [(i, (i + 4) % 16) for i in range(16)]
 
 
@@ -1379,79 +1543,219 @@
     return lax.ppermute(value, "dp", RING)
 
 
-def gather_flow(shard, kind):
-    if kind == "zxy":
-        one = next_z(shard)
-        two = next_z(one)
-        three = next_z(two)
-        base = jnp.stack([shard, one, two, three])
-        over_x = swap_x(base)
-        quads = [base, over_x, swap_y(base), swap_y(over_x)]
-    else:
-        over_x = swap_x(shard)
-        base = jnp.stack([shard, over_x, swap_y(shard), swap_y(over_x)])
-        one = next_z(base)
-        two = next_z(one)
-        quads = [base, one, two, next_z(two)]
-    return quads + [swap_core(quad) for quad in quads]
+class Cell:
+    def __init__(self, value):
+        self.value = value
+
+
+def values_of(items):
+    return [item.value if isinstance(item, Cell) else item for item in items]
+
+
+class GatherZXY:
+    def __init__(self, shard):
+        self.steps = [Cell(shard)]
+
+    def z(self):
+        self.steps.append(Cell(next_z(self.steps[-1].value)))
+        return self.steps[-1]
+
+    def x(self):
+        self.base = Cell(jnp.stack(values_of(self.steps)))
+        self.over_x = Cell(swap_x(self.base.value))
+        return self.over_x
+
+    def y(self):
+        self.over_y = Cell(swap_y(self.base.value))
+        return self.over_y
+
+    def xy(self):
+        self.over_xy = Cell(swap_y(self.over_x.value))
+        return self.over_xy
+
+    def core(self):
+        self.quads = [self.base, self.over_x, self.over_y, self.over_xy]
+        self.other = Cell(swap_core(jnp.concatenate(values_of(self.quads), 0)))
+        return self.other
+
+    def pieces(self):
+        return values_of(self.quads + [self.other])
+
+
+class GatherXYZ:
+    def __init__(self, shard):
+        self.shard = Cell(shard)
+
+    def x(self):
+        self.pair = Cell(jnp.stack([self.shard.value, swap_x(self.shard.value)]))
+        return self.pair
+
+    def y(self):
+        over_y = swap_y(self.pair.value)
+        self.quads = [Cell(jnp.concatenate([self.pair.value, over_y], 0))]
+        return self.quads[0]
+
+    def z(self):
+        self.quads.append(Cell(next_z(self.quads[-1].value)))
+        return self.quads[-1]
+
+    def core(self):
+        self.other = Cell(swap_core(jnp.concatenate(values_of(self.quads), 0)))
+        return self.other
+
+    def pieces(self):
+        return values_of(self.quads + [self.other])
+
+
+def hold(cells, after):
+    def kernel(*refs):
+        pass
+
+    gated_call(
+        after,
+        kernel,
+        through=cells,
+        grid_spec=dict(num_scalar_prefetch=0, grid=(), in_specs=[], out_specs=[]),
+        out_shape=[],
+        compiler_params=params_of(60),
+        name="hold",
+    )()
+
+
+def sum_small(value):
+    value = value + swap_core(value)
+    value = value + swap_x(value)
+    value = value + swap_y(value)
+    value = value + lax.ppermute(value, "dp", NEAR_Z)
+    return value + lax.ppermute(value, "dp", FAR_Z)
 
 
 def join(kept, received):
     return (kept.astype(F32) + received.astype(F32)).astype(kept.dtype)
 
 
-def reduce_ring(parts):
-    moving = next_z(parts[3])
-    moving = next_z(join(parts[2], moving))
-    moving = next_z(join(parts[1], moving))
-    return (parts[0], moving)
-
-
-def reduce_flow(send, keep, kind):
-    received = swap_core(send)
-    if kind == "zxy":
-        arrived = swap_y(join(keep[1], received[1]))
-        kept = join(keep[0], received[0])
-        across = swap_x(join(kept[1], arrived[1]))
-        kept = join(kept[0], arrived[0])
-        parts = [join(kept[k], across[k]) for k in range(4)]
-        last, moving = reduce_ring(parts)
-        return last.astype(F32) + moving.astype(F32)
-    parts = [join(keep[k], received[k]) for k in range(4)]
-    last, moving = reduce_ring(parts)
-    whole = join(last, moving)
-    arrived = swap_y(whole[1])
-    kept = join(whole[0], arrived)
-    return kept[0].astype(F32) + swap_x(kept[1]).astype(F32)
+class ReduceZXY:
+    def __init__(self, send, keep):
+        self.send, self.keep, self.moving = Cell(send), keep, None
+
+    def core(self):
+        self.received = Cell(swap_core(self.send.value))
+
+    def y(self):
+        got = self.received.value
+        arrived = swap_y(join(self.keep[1], got[1]))
+        self.keep, self.also = join(self.keep[0], got[0]), None
+        self.received = Cell(arrived)
+
+    def x(self):
+        got = self.received.value
+        arrived = swap_x(join(self.keep[1], got[1]))
+        self.keep, self.also = self.keep[0], got[0]
+        self.received = Cell(arrived)
+        self.left = 4
+
+    def z(self):
+        self.moving = Cell(next_z(self.total(BF)))
+
+    def total(self, kind):
+        self.left -= 1
+        k = self.left
+        value = self.keep[k].astype(F32) + self.also[k].astype(F32) + self.received.value[k].astype(F32)
+        if self.moving is not None:
+            value = value + self.moving.value.astype(F32)
+        return value.astype(kind)
+
+    def result(self):
+        return self.total(F32)
+
+
+class ReduceXYZ:
+    def __init__(self, send, keep):
+        self.send, self.keep, self.moving = Cell(send), keep, None
+
+    def core(self):
+        self.received = Cell(swap_core(self.send.value))
+        self.left = 4
+
+    def z(self):
+        self.left -= 1
+        self.moving = Cell(next_z(self.total(BF, ())))
+
+    def total(self, kind, index):
+        k = self.left
+        value = self.keep[k][index].astype(F32) + self.received.value[k][index].astype(F32)
+        if self.moving is not None:
+            value = value + self.moving.value[index].astype(F32)
+        return value.astype(kind)
+
+    def y(self):
+        self.left -= 1
+        self.arrived = Cell(swap_y(self.total(BF, 1)))
+
+    def x(self):
+        self.across = Cell(swap_x((self.total(F32, (0, 1)) + self.arrived.value[1].astype(F32)).astype(BF)))
+
+    def result(self):
+        return self.total(F32, (0, 0)) + self.arrived.value[0].astype(F32) + self.across.value.astype(F32)
 
 
 def join_halves(mine, other, me):
     return jnp.where(me == 0, jnp.concatenate([mine, other], 0), jnp.concatenate([other, mine], 0))
 
 
-def whole_sequence(local, me):
-    mine = lax.dynamic_index_in_dim(local, me, 1, keepdims=False)
-    theirs = lax.dynamic_index_in_dim(local, 1 - me, 1, keepdims=False)
-    return join_halves(mine, swap_x(theirs), me)
-
-
-def both_sequences(whole, me):
-    half = whole.shape[0] // 2
-    mine = lax.dynamic_slice_in_dim(whole, me * half, half, 0)
-    theirs = lax.dynamic_slice_in_dim(whole, (1 - me) * half, half, 0)
-    other = swap_x(theirs)
+class Exchange:
+    def __init__(self, local, me):
+        self.me = me
+        self.mine = jnp.where(me == 0, local[:, 0], local[:, 1])
+        self.theirs = Cell(jnp.where(me == 0, local[:, 1], local[:, 0]))
+
+    def go(self):
+        self.other = swap_x(self.theirs.value)
+
+    def whole(self):
+        return join_halves(self.mine, self.other, self.me)
+
+
+def both_sequences(mine, other, me):
     return jnp.where(me == 0, jnp.stack([mine, other], 1), jnp.stack([other, mine], 1))
 
 
-def own_first(values, dp, me):
-    rest = values.shape[2:]
-    v = values.reshape((4, 2, 2, 2) + rest)
-    z, y, c = dp // 4, (dp // 2) % 2, dp % 2
-    v = lax.dynamic_slice_in_dim(jnp.concatenate([v, v], 0), z, 4, 0)
-    v = jnp.where(y == 1, v[:, ::-1], v)
-    v = jnp.where(c == 1, v[:, :, ::-1], v)
-    v = jnp.where(me == 1, v[:, :, :, ::-1], v)
-    return jnp.transpose(v, (2, 1, 3, 0) + tuple(range(4, v.ndim)))
+class ReduceHalves:
+    def __init__(self, send, keep):
+        self.send, self.keep, self.across = Cell(send), keep, None
+
+    def core(self):
+        self.received = Cell(swap_core(self.send.value))
+
+    def y(self):
+        self.arrived = Cell(swap_y(join(self.keep[1], self.received.value[1])))
+
+    def sum(self, k):
+        terms = (self.keep[0], self.received.value[0], self.arrived.value)
+        if self.across is not None:
+            terms += (self.across.value,)
+        return sum(term[k].astype(F32) for term in terms)
+
+    def x(self):
+        return Cell(swap_x(self.sum(slice(None)).astype(BF)))
+
+    def z(self, moving=None):
+        k = 3 if moving is None else moving[0] - 1
+        value = self.sum(k) if moving is None else self.sum(k) + moving[1].astype(F32)
+        return (k, next_z(value.astype(BF)))
+
+
+SMALL = 17 * 1024
+
+
+def place_small(norm_gains, feature_biases, head_biases, inner_bias, dp, me):
+    column = 32 * (2 * dp + me)
+    put = lax.dynamic_update_slice
+    gains = put(jnp.zeros((3, 1024), F32), norm_gains, (0, column))
+    shifts = put(jnp.zeros((6, 1024), F32), feature_biases, (0, column))
+    heads = put(jnp.zeros((4, 16, 64), F32), head_biases.astype(F32), (0, me * 8, dp * 4))
+    inner = put(jnp.zeros((16, 256), F32), inner_bias.astype(F32), (me * 8, dp * 16))
+    return jnp.concatenate([gains, shifts, heads.reshape(4, 1024), inner.reshape(4, 1024)], 0)
 
 
 def one_sequence_body(
@@ -1482,86 +1786,116 @@
     scales = jnp.mean(counts) / jnp.sum(matches * counts[None, :], -1)
     scale = jnp.broadcast_to(lax.dynamic_index_in_dim(scales, me, 0, keepdims=False), (8, 128))
 
-    small = jnp.concatenate(
-        [
-            norm_gains.reshape(-1),
-            feature_biases.reshape(-1),
-            head_biases.astype(F32).reshape(-1),
-            inner_bias.astype(F32).reshape(-1),
-        ]
-    )
-    small = lax.all_gather(small, ("dp", "mp"), axis=0, tiled=False)
-    gains = small[:, :96].reshape(32, 3, 32).transpose(1, 0, 2).reshape(3, 1024)
-    shifts = small[:, 96:288].reshape(32, 6, 32).transpose(1, 0, 2).reshape(6, 1024)
-    heads = small[:, 288:416].reshape(16, 2, 4, 8, 4).transpose(2, 1, 3, 0, 4).reshape(4, 1024)
-    inner = small[:, 416:544].reshape(16, 2, 8, 16).transpose(1, 2, 0, 3).reshape(1, 4096)
-    par = jnp.concatenate([gains, shifts, heads, jnp.zeros((11, 1024), F32)], 0)
-    inner = jnp.broadcast_to(inner, (8, 4096))
-
-    x = whole_sequence(tokens, me)
-    w_self = [gather_flow(self_in[t], KINDS[t]) for t in range(3)]
-    pieces_self = [piece for flow in w_self for piece in flow]
-    mixed_shard = jnp.concatenate([cross_in[1], cross_in[2], self_out.T, cross_in[0], cross_out.T], 1)
-    w_mid = gather_flow(mixed_shard, "zxy")
-    mem = whole_sequence(memory, me)
-    w_in = gather_flow(fc_in, "zxy")
-    w_out = gather_flow(fc_out.T, "xyz")
-    cot = whole_sequence(cotangent, me)
-
-    q1, k1, v1, n1_t = call_qkv(info, par, x, pieces_self)
-    o1, lse1 = call_attend(info, q1, k1, v1, True)
+    small = place_small(norm_gains, feature_biases, head_biases, inner_bias, dp, me)
+    info = Cell(info)
+    x = Exchange(tokens, me)
+    own_k = GatherXYZ(self_in[1])
+    own_qv = GatherZXY(jnp.concatenate([self_in[0], self_in[2]], 1))
+    middle = jnp.concatenate([cross_in[1], cross_in[2], self_out.T, cross_in[0]], 1)
+    w_mid = [lax.all_gather(middle, ("dp", "mp"), axis=0, tiled=False)]
+    outer = jnp.concatenate([fc_in, fc_out.T, cross_out.T], 1)
+    w_out = [lax.all_gather(outer, ("dp", "mp"), axis=0, tiled=False)]
+    mem, cot = Exchange(memory, me), Exchange(cotangent, me)
+    own_k.x(), own_qv.z(), x.go()
+    small = small + swap_core(small)
+    own_k.y(), own_qv.z()
+    small = small + swap_x(small)
+    own_k.z(), own_qv.z()
+    small = small + swap_y(small)
+    own_k.z(), own_qv.x(), own_qv.y()
+    small = Cell(small + lax.ppermute(small, "dp", NEAR_Z))
+    hold([mem.theirs, own_k.quads[2], own_qv.over_x, small], [])
+    own_k.z(), own_qv.xy()
+    small = small.value + lax.ppermute(small.value, "dp", FAR_Z)
+    own_k.core(), own_qv.core()
+    par = jnp.concatenate([small[:13], jnp.zeros((11, 1024), F32)], 0)
+    inner = jnp.broadcast_to(small[13:17].reshape(1, 4096), (8, 4096))
+    x = x.whole()
+    hold([info, mem.theirs], [own_k.other, own_qv.other, x])
+    w_self = own_qv.pieces() + own_k.pieces()
+    mem.go()
+    q1, k1, v1, n1_t = call_qkv(info, par, x, w_self)
+    attended = call_attend(info, q1, k1, v1, True, 0, 4)
+    o1, lse1 = call_attend(info, q1, k1, v1, True, 4, 4, attended)
+    h1, q2, n2_t = call_after_self(info, par, x, o1, w_mid)
+    mem = mem.whole()
+    hold([info, cot.theirs], [h1, mem])
+    cot.go()
     k2, v2, mem_t = call_kv(info, par, mem, w_mid)
-    h1, q2, n2_t = call_after_self(info, par, x, o1, w_mid)
-    o2, lse2 = call_attend(info, q2, k2, v2, False)
-    h2, n3, n3_t, g3, g3_t, g_sum = call_after_cross(info, par, scale, h1, o2, cot, w_mid)
-    out, dn3, send_in, keep_in, send_out, keep_out, d_inner = call_ffn(
-        info, par, inner, n3, n3_t, g3, g3_t, h2, w_in, w_out
-    )
-    output = both_sequences(out, me)
-    sum_fc_in = reduce_flow(send_in, keep_in, "zxy")
-    sum_fc_out = reduce_flow(send_out, keep_out, "xyz")
-    dh2, do2, g2_t, sums3 = call_back_three(info, par, dn3, h2, g3, w_mid)
-    dq2, dk2, dv2, bias2 = call_attend_back(info, q2, k2, v2, o2, do2, lse2, False)
-    grad_memory = both_sequences(call_memory_back(info, dk2, dv2, w_mid), me).astype(F32)
-    cross_grads = call_weight_grad(
-        info, "zxy", [mem_t, n2_t, g2_t], [dk2, dv2, dq2, o2], (0, 0, 1, 2), "weight_grad_cross"
-    )
-    sum_cross = reduce_flow(*cross_grads, "zxy")
+    o2, lse2 = call_attend(info, q2, k2, v2, False, 0, 8)
+    h2, n3, n3_t, g3, g3_t, g_sum = call_after_cross(info, par, scale, h1, o2, cot.whole(), w_out)
+    out, dn3, send_fc, keep_fc, d_inner = call_ffn(info, par, inner, n3, n3_t, g3, g3_t, h2, w_out)
+
+    half = out.shape[0] // 2
+    sum_f = ReduceZXY(send_fc, keep_fc)
+    sum_f.core()
+    out_other = swap_x(out[half:])
+    dh2, do2, g2_t, sums3 = call_back_three(info, par, dn3, h2, g3, w_out)
+    hold([info, sum_f.received], [do2])
+    sum_f.y()
+    dq2, dk2, dv2, bias2 = call_attend_back(info, q2, k2, v2, o2, do2, lse2, False, 0, 8)
     dh1, do1, g1_t, sums2 = call_back_two(info, par, dq2, h1, dh2, w_mid)
-    dq1, dk1, dv1, bias1 = call_attend_back(info, q1, k1, v1, o1, do1, lse1, True)
-    self_grads = call_weight_grad(info, "zxy", [n1_t, g1_t], [dq1, dk1, dv1, o1], (0, 0, 0, 1), "weight_grad_self")
-    sum_self = reduce_flow(*self_grads, "zxy")
-    grad_x, sums1 = call_back_one(info, par, dq1, dk1, dv1, x, dh1, pieces_self)
-    grad_tokens = both_sequences(grad_x, me).astype(F32)
-
-    d_gains = jnp.stack([sums1[0], sums2[0], sums3[0]])
-    d_shifts = jnp.stack([sums1[1], sums2[1], sums3[1], sums2[2], sums3[2], g_sum[0]])
-    d_heads = jnp.concatenate([bias1[:2], bias2[:2]], 0)
-    d_small = jnp.concatenate(
-        [
-            d_gains.reshape(3, 32, 32).transpose(1, 0, 2).reshape(32, 96),
-            d_shifts.reshape(6, 32, 32).transpose(1, 0, 2).reshape(32, 192),
-            d_heads.reshape(4, 2, 8, 16, 4).transpose(3, 1, 0, 2, 4).reshape(32, 128),
-            d_inner[0].reshape(2, 8, 16, 16).transpose(2, 0, 1, 3).reshape(32, 128),
-        ],
-        1,
-    )
-    d_small = own_first(d_small.reshape(16, 2, 544), dp, me)
-    total = reduce_flow(d_small[1], d_small[0], "zxy")
+    cross = call_weight_grad(
+        info, "zxy", [mem_t, n2_t, g2_t, g1_t], [dk2, dv2, dq2, o2, o1], (0, 0, 1, 2, 3), "weight_grad_cross", after=[do1]
+    )
+    sum_c = ReduceZXY(*cross)
+    hold([info, sum_c.send, sum_f.received], [out_other, sum_c.keep])
+    sum_c.core(), sum_f.x()
+    grad_mem = Cell(call_memory_back(info, dk2, dv2, w_mid))
+    hold([info, sum_c.received, grad_mem], [])
+    sum_c.y()
+    memory_other = swap_x(grad_mem.value[half:])
+    back = call_attend_back(info, q1, k1, v1, o1, do1, lse1, True, 0, 4, other=True)
+    hold([info, sum_f.received], [back[0], memory_other])
+    sum_f.z()
+    sum_s1 = ReduceHalves(*call_half_grad(info, True, [n1_t], back[:3], (0, 0, 0), "weight_grad_self_1"))
+    hold([info, sum_s1.send, sum_f.moving], [sum_s1.keep])
+    sum_s1.core(), sum_f.z()
+    back = call_attend_back(info, q1, k1, v1, o1, do1, lse1, True, 0, 2, back, other=False)
+    hold([info, sum_s1.received, sum_c.received, sum_f.moving], [back[0]])
+    sum_s1.y(), sum_c.x(), sum_f.z()
+    dq1, dk1, dv1, bias1 = call_attend_back(info, q1, k1, v1, o1, do1, lse1, True, 2, 2, back, other=False)
+    hold([info, sum_s1.arrived], [bias1, sum_f.moving])
+    across = sum_s1.x()
+    sum_s0 = ReduceHalves(*call_half_grad(info, False, [n1_t], [dq1, dk1, dv1], (0, 0, 0), "weight_grad_self_0"))
+    hold([info, sum_s0.send, sum_c.received], [sum_s0.keep])
+    sum_s0.core(), sum_c.z()
+    grad_other, sums1a = call_back_one(info, par, dq1, dk1, dv1, x, dh1, w_self, True)
+    grad_other = Cell(grad_other)
+    hold([info, sum_s0.received, sum_c.moving, grad_other, across], [])
+    sum_s0.y(), sum_c.z()
+    tokens_other = swap_x(grad_other.value)
+    grad_own, sums1b = call_back_one(info, par, dq1, dk1, dv1, x, dh1, w_self, False)
+    d_small = Cell(call_pack(sums1a, sums1b, sums2, sums3, g_sum, bias1, bias2, d_inner))
+    hold([sum_s0.arrived, sum_c.moving, d_small], [tokens_other])
+    sum_s0.across = across
+    moving = sum_s0.z()
+    d_small = sum_small(d_small.value)
+    moving = sum_s0.z(moving)
+    sum_c.z()
+    moving = sum_s0.z(moving)
+    output = both_sequences(out[:half], out_other, me)
+    grad_tokens = both_sequences(grad_own, tokens_other, me).astype(F32)
+    grad_memory = both_sequences(grad_mem.value[:half], memory_other, me).astype(F32)
+    fc = sum_f.result().reshape(64, 4, 2, 512)
+    self_all = sum_s0.sum(0) + moving[1].astype(F32)
+    column = 32 * (2 * dp + me)
+    take = lax.dynamic_slice
+    crossed = sum_c.result()
     return (
         output,
         grad_tokens,
         grad_memory,
-        jnp.stack([sum_self[:, :512], sum_self[:, 512:1024], sum_self[:, 1024:1536]]),
-        sum_self[:, 1536:].T,
-        jnp.stack([sum_cross[:, 1024:1536], sum_cross[:, :512], sum_cross[:, 512:1024]]),
-        sum_cross[:, 1536:].T,
-        sum_fc_in,
-        sum_fc_out.T,
-        total[288:416].reshape(4, 8, 4),
-        total[416:].reshape(8, 16),
-        total[:96].reshape(3, 32),
-        total[96:288].reshape(6, 32),
+        jnp.stack([self_all[:, :512], self_all[:, 512:1024], self_all[:, 1024:]]),
+        crossed[:, 2048:].T,
+        jnp.stack([crossed[:, 1024:1536], crossed[:, :512], crossed[:, 512:1024]]),
+        crossed[:, 1536:2048].T,
+        fc[:, :, 0].reshape(64, 2048),
+        fc[:, :, 1].reshape(64, 2048).T,
+        take(d_small[9:13].reshape(4, 16, 64), (0, me * 8, dp * 4), (4, 8, 4)),
+        take(d_small[13:17].reshape(16, 256), (me * 8, dp * 16), (8, 16)),
+        take(d_small[:3], (0, column), (3, 32)),
+        take(d_small[3:9], (0, column), (6, 32)),
     )
 
 

time: 1020 us -> 769 us (0.75)
  waiting for transfers between devices: 385 us -> 185 us
  Pallas kernels: 397 us -> 360 us
  other arithmetic: 51.8 us -> 82 us
  local copies, waits for them, and re-layouts: 96.3 us -> 72.6 us
  starting transfers between devices: 65.8 us -> 45.6 us
    unnamed x2, waiting for transfers between devices: 105 us -> 0.03 us
    ppermute x33 -> x15, waiting for transfers between devices: 92.8 us -> 23.1 us  [next_z(): return lax.ppermute(value, 'dp', RING)]
    ppermute x17 -> x9, waiting for transfers between devices: 92.1 us -> 39.6 us  [swap_y(): return lax.ppermute(value, 'dp', along(2))]
    pallas_call x15 -> x34, Pallas kernels: 397 us -> 360 us  [the longest x33 359 us: run(): results = call(*values_of(operands), *after, *passed)]
    all_gather x0 -> x2, waiting for transfers between devices: none -> 25.9 us  [the longest x1 25.9 us: one_sequence_body(): w_out = [lax.all_gather(outer, ('dp', 'mp'), axis=0, tiled=False)]]
    ppermute x0 -> x4, waiting for transfers between devices: none -> 25.2 us  [the longest x1 8.73 us: one_sequence_body(): small = small.value + lax.ppermute(small.value, 'dp', FAR_Z)]
    convert_element_type x2 -> x13, other arithmetic: 2.43 us -> 21.8 us  [the longest x6 11.3 us: total(): return value.astype(kind)]
    dynamic_slice x2 -> x4, local copies, waits for them, and re-layouts: 19 us -> 2.06 us  [the longest x1 0.67 us: one_sequence_body(): take(d_small[13:17].reshape(16, 256), (me * 8, dp * 16), (8, 16))]
  transfers between devices with their start and end apart: 97 -> 51, of which waited for: 40 -> 23; matrix products, arithmetic and copies ran while one was open for 13% -> 17% of each run, Pallas kernels for 17% -> 36%
where the time goes in v2:
time: 769 us; the launch traced here: 761 us
  Pallas kernels  360 us (47%)
  waiting for transfers between devices  185 us (24%)
  other arithmetic  82 us (11%)
  local copies, waits for them, and re-layouts  72.6 us (9%)
  starting transfers between devices  45.6 us (6%)
  between operations  15.7 us (2%)
    pallas_call x33, Pallas kernels, run(): results = call(*values_of(operands), *after, *passed)  359 us
    ppermute x13, waiting for transfers between devices, swap_x(): return lax.ppermute(value, 'mp', [(0, 1), (1, 0)])  70.7 us
    ppermute x9, waiting for transfers between devices, swap_y(): return lax.ppermute(value, 'dp', along(2))  39.6 us
    unnamed x119, local copies, waits for them, and re-layouts  34.8 us
    convert_element_type x6, other arithmetic, join(): return (kept.astype(F32) + received.astype(F32)).astype(kept.dtype)  27 us
    all_gather x1, waiting for transfers between devices, one_sequence_body(): w_out = [lax.all_gather(outer, ('dp', 'mp'), axis=0, tiled=False)]  25.9 us
    ppermute x15, waiting for transfers between devices, next_z(): return lax.ppermute(value, 'dp', RING)  23.1 us
    ppermute x15, starting transfers between devices, next_z(): return lax.ppermute(value, 'dp', RING)  17.1 us
  transfers between devices with their start and end apart: 51, of which 23 were waited for; matrix products, arithmetic and copies ran while one was open for 17% of the time, Pallas kernels for 36%

profile of v2, /device:TPU:0, one launch (start us, length us, event | category | flops | bytes accessed | tf_op | source)
XLA Modules:
  0.0 760.8 jit_solution(13358670444882711745)
XLA Ops:
  49.2 12.7 %collective-permute-done.9 = f32[17,1024]{1,0:T(8,128)S(1)} collective-permute-done((f32[17,1024]{1,0:T(8,128)S(1)}, f32[17,1024]{1,0:T(8,128)S(1)}, u32[]{:S(2)}, u32[]{:S(2)}) %collective-permute-start.9) | collective-permute-done | bytes 69664 | tf_op jit(solution)/shard_map/ppermute | solution.py:1531
  81.3 19.8 %collective-permute-done.14.refs_5_.refs_9_ = bf16[4,64,1024]{2,1,0:T(8,128)(2,1)S(1)} collective-permute-done((bf16[4,64,1024]{2,1,0:T(8,128)(2,1)S(1)}, bf16[4,64,1024]{2,1,0:T(8,128)(2,1)S(1)}, u32[]{:S(2)}, u32[]{:S(2)}) %collective-permute-start.14) | collective-permute-done | bytes 524320 | tf_op jit(solution)/shard_map/ppermute | solution.py:1535
  102.0 9.2 %collective-permute-done.15.refs_6_.refs_10_ = bf16[4,64,1024]{2,1,0:T(8,128)(2,1)S(1)} collective-permute-done((bf16[4,64,1024]{2,1,0:T(8,128)(2,1)}, bf16[4,64,1024]{2,1,0:T(8,128)(2,1)S(1)}, u32[]{:S(2)}, u32[]{:S(2)}) %collective-permute-start.15) | collective-permute-done | bytes 524320 | tf_op jit(solution)/shard_map/ppermute | solution.py:1535
  121.7 7.2 collective-permute-done.12.refs_11_.refs_15_
  140.2 8.7 %collective-permute-done.18 = f32[17,1024]{1,0:T(8,128)S(1)} collective-permute-done((f32[17,1024]{1,0:T(8,128)S(1)}, f32[17,1024]{1,0:T(8,128)S(1)}, u32[]{:S(2)}, u32[]{:S(2)}) %collective-permute-start.18) | collective-permute-done | bytes 69664 | tf_op jit(solution)/shard_map/ppermute | solution.py:1809
  154.9 13.8 %project_self.1 = (bf16[1024,1024]{1,0:T(8,128)(2,1)}, bf16[1024,1024]{1,0:T(8,128)(2,1)}, bf16[1024,1024]{1,0:T(8,128)(2,1)}, bf16[1024,1024]{1,0:T(8,128)(2,1)}) custom-call(s32[8]{0:T(128)} %get-tuple-element.115.refs_0_.refs_2_, f32[24,1024]{1,0:T(8,128)} %concatenate.52.refs_1_, bf16[1024,1024]{1,0:T(8,128)(2,1)} %maximum_select_fusion.refs_2_.refs_5_, ...), custom_call_target="tpu_custom_call" | custom-call | flops 6400000000 | bytes 16000000 | tf_op jit(solution)/shard_map/project_self/pallas_call | solution.py:536
  168.8 11.0 %attend_self.2 = (bf16[1024,1024]{1,0:T(8,128)(2,1)}, f32[8,1024,128]{2,1,0:T(8,128)}) custom-call(s32[8]{0:T(128)} %get-tuple-element.115.refs_0_.refs_2_, bf16[1024,1024]{1,0:T(8,128)(2,1)} %get-tuple-element.117.refs_1_, bf16[1024,1024]{1,0:T(8,128)(2,1)} %get-tuple-element.118.refs_2_, bf16[1024,1024]{1,0:T(8,128)(2,1)} %get-tuple-element.119.refs_3_), custom_call_target="tpu_custom_call" | custom-call | flops 34500001792 | bytes 1000000 | tf_op jit(solution)/shard_map/attend_self/pallas_call | solution.py:536
  179.8 11.2 %attend_self.3 = (bf16[1024,1024]{1,0:T(8,128)(2,1)}, f32[8,1024,128]{2,1,0:T(8,128)}) custom-call(s32[8]{0:T(128)} %get-tuple-element.115.refs_0_.refs_2_, bf16[1024,1024]{1,0:T(8,128)(2,1)} %get-tuple-element.117.refs_1_, bf16[1024,1024]{1,0:T(8,128)(2,1)} %get-tuple-element.118.refs_2_, ...), custom_call_target="tpu_custom_call", output_to_operand_aliasing={{0}: (4, {}), {1}: (5, {})} | custom-call | flops 34500001792 | bytes 1000000 | tf_op jit(solution)/shard_map/attend_self/pallas_call | solution.py:536
  198.8 11.7 %after_self.1 = (f32[1024,1024]{1,0:T(8,128)}, bf16[1024,1024]{1,0:T(8,128)(2,1)}, bf16[1024,1024]{1,0:T(8,128)(2,1)}) custom-call(s32[8]{0:T(128)} %get-tuple-element.115.refs_0_.refs_2_, f32[24,1024]{1,0:T(8,128)} %concatenate.52.refs_1_, bf16[1024,1024]{1,0:T(8,128)(2,1)} %maximum_select_fusion.refs_2_.refs_5_, ...), custom_call_target="tpu_custom_call" | custom-call | flops 4300000256 | bytes 16000000 | tf_op jit(solution)/shard_map/after_self/pallas_call | solution.py:536
  211.3 10.2 %project_memory.1 = (bf16[1024,1024]{1,0:T(8,128)(2,1)}, bf16[1024,1024]{1,0:T(8,128)(2,1)}, bf16[1024,1024]{1,0:T(8,128)(2,1)}) custom-call(s32[8]{0:T(128)} %get-tuple-element.125.refs_0_.refs_1_, f32[24,1024]{1,0:T(8,128)} %concatenate.52.refs_1_, bf16[1024,1024]{1,0:T(8,128)(2,1)} %maximum_select_fusion.1.refs_1_.refs_2_, bf16[32,64,2048]{2,1,0:T(8,128)(2,1)} %bitcast.193), custom_call_target="tpu_custom_call" | custom-call | flops 4300000256 | bytes 12000000 | tf_op jit(solution)/shard_map/project_memory/pallas_call | solution.py:536
  221.5 25.1 %attend_cross.1 = (bf16[1024,1024]{1,0:T(8,128)(2,1)}, f32[8,1024,128]{2,1,0:T(8,128)}) custom-call(s32[8]{0:T(128)} %get-tuple-element.125.refs_0_.refs_1_, bf16[1024,1024]{1,0:T(8,128)(2,1)} %get-tuple-element.126.refs_1_, bf16[1024,1024]{1,0:T(8,128)(2,1)} %get-tuple-element.127.refs_2_, bf16[1024,1024]{1,0:T(8,128)(2,1)} %get-tuple-element.128.refs_3_), custom_call_target="tpu_custom_call" | custom-call | flops 110399995904 | bytes 1000000 | tf_op jit(solution)/shard_map/attend_cross/pallas_call | solution.py:536
  246.6 12.1 %collective-permute-done.20 = bf16[512,1024]{1,0:T(8,128)(2,1)S(1)} collective-permute-done((bf16[512,1024]{1,0:T(8,128)(2,1)}, bf16[512,1024]{1,0:T(8,128)(2,1)S(1)}, u32[]{:S(2)}, u32[]{:S(2)}) %collective-permute-start.20) | collective-permute-done | bytes 1048608 | tf_op jit(solution)/shard_map/ppermute | solution.py:1531
  261.1 25.9 %all-gather.7.cloned.1.call-done = bf16[2048,4608]{1,0:T(8,128)(2,1)} async-done(((bf16[64,4608]{1,0:T(8,128)(2,1)}), bf16[2048,4608]{1,0:T(8,128)(2,1)}) %all-gather.7.cloned.1.call-update) | async-done | bytes 18874384 | tf_op jit(solution)/shard_map/all_gather | solution.py:1797
  288.3 12.9 %after_cross.1 = (f32[1024,1024]{1,0:T(8,128)}, bf16[1024,1024]{1,0:T(8,128)(2,1)}, bf16[1024,1024]{1,0:T(8,128)(2,1)}, bf16[1024,1024]{1,0:T(8,128)(2,1)}, bf16...) custom-call(s32[8]{0:T(128)} %get-tuple-element.125.refs_0_.refs_1_, f32[24,1024]{1,0:T(8,128)} %concatenate.52.refs_1_, ...), custom_call_target="tpu_custom_call" | custom-call | flops 2200000000 | bytes 26000000 | tf_op jit(solution)/shard_map/after_cross/pallas_call | solution.py:536
  301.9 75.4 %feedforward.1 = (bf16[1024,1024]{1,0:T(8,128)(2,1)}, f32[1024,1024]{1,0:T(8,128)}, bf16[2,2,4,64,4096]{4,3,2,1,0:T(8,128)(2,1)}, bf16[2,2,4,64,4096]{4,3,2,1,0:T(8,128)(2,1)}, f32[8,4096]{1,0:T(8,128)}) custom-call(s32[8]{0:T(128)} %get-tuple-element.125.refs_0_.refs_1_, f32[24,1024]{1,0:T(8,128)} %concatenate.52.refs_1_, ...), custom_call_target="tpu_custom_call" | custom-call | flops 51499999232 | bytes 60000000 | tf_op jit(solution)/shard_map/feedforward/pallas_call | solution.py:536
  382.0 12.3 %back_three.1 = (f32[1024,1024]{1,0:T(8,128)}, bf16[1024,1024]{1,0:T(8,128)(2,1)}, bf16[1024,1024]{1,0:T(8,128)(2,1)}, f32[8,1024]{1,0:T(8,128)}) custom-call(s32[8]{0:T(128)} %get-tuple-element.125.refs_0_.refs_1_, f32[24,1024]{1,0:T(8,128)} %concatenate.52.refs_1_, f32[1024,1024]{1,0:T(8,128)} %get-tuple-element.137.refs_2_, ...), custom_call_target="tpu_custom_call" | custom-call | flops 2200000000 | bytes 20000000 | tf_op jit(solution)/shard_map/back_three/pallas_call | solution.py:536
  394.4 9.7 %add_convert_fusion = (bf16[1,2,4,64,4096]{4,3,2,1,0:T(8,128)(2,1)}, bf16[2,4,64,4096]{3,2,1,0:T(8,128)(2,1)}) fusion(bf16[2,2,4,64,4096]{4,3,2,1,0:T(8,128)(2,1)} %get-tuple-element.154, bf16[2,2,4,64,4096]{4,3,2,1,0:T(8,128)(2,1)} %get-tuple-element.153), kind=kLoop, calls=%fused_computation | loop fusion | flops 16777216 | bytes 25165824 | tf_op jit(solution)/shard_map/convert_element_type | solution.py:1634
  404.2 49.1 %attend_back_cross.1 = (bf16[1024,1024]{1,0:T(8,128)(2,1)}, bf16[1024,1024]{1,0:T(8,128)(2,1)}, bf16[1024,1024]{1,0:T(8,128)(2,1)}, f32[8,1024]{1,0:T(8,128)}) custom-call(s32[8]{0:T(128)} %get-tuple-element.140.refs_0_.refs_2_, bf16[1024,1024]{1,0:T(8,128)(2,1)} %get-tuple-element.126.refs_1_, bf16[1024,1024]{1,0:T(8,128)(2,1)} %get-tuple-element.127.refs_2_, ...), custom_call_target="tpu_custom_call" | custom-call | flops 142599995392 | bytes 1000000 | tf_op jit(solution)/shard_map/attend_back_cross/pallas_call | solution.py:536
  453.3 13.7 %back_two.1 = (f32[1024,1024]{1,0:T(8,128)}, bf16[1024,1024]{1,0:T(8,128)(2,1)}, bf16[1024,1024]{1,0:T(8,128)(2,1)}, f32[8,1024]{1,0:T(8,128)}) custom-call(s32[8]{0:T(128)} %get-tuple-element.140.refs_0_.refs_2_, f32[24,1024]{1,0:T(8,128)} %concatenate.52.refs_1_, bf16[1024,1024]{1,0:T(8,128)(2,1)} %get-tuple-element.145.refs_2_.refs_7_, ...), custom_call_target="tpu_custom_call" | custom-call | flops 4300000256 | bytes 24000000 | tf_op jit(solution)/shard_map/back_two/pallas_call | solution.py:536
  467.0 22.7 %weight_grad_cross.1 = (bf16[2,2,4,64,2560]{4,3,2,1,0:T(8,128)(2,1)}, bf16[2,2,4,64,2560]{4,3,2,1,0:T(8,128)(2,1)}) custom-call(s32[8]{0:T(128)} %get-tuple-element.140.refs_0_.refs_2_, bf16[1024,1024]{1,0:T(8,128)(2,1)} %get-tuple-element.141.refs_1_, bf16[1024,1024]{1,0:T(8,128)(2,1)} %get-tuple-element.142.refs_2_, ...), custom_call_target="tpu_custom_call" | custom-call | flops 51499999232 | bytes 1000000 | tf_op jit(solution)/shard_map/weight_grad_cross/pallas_call | solution.py:536
  489.7 7.0 collective-permute-done.23.refs_4_
  507.7 10.2 %memory_back.1.refs_2_ = bf16[1024,1024]{1,0:T(8,128)(2,1)} custom-call(s32[8]{0:T(128)} %get-tuple-element.155.refs_0_, bf16[1024,1024]{1,0:T(8,128)(2,1)} %get-tuple-element.148.refs_5_.refs_1_, bf16[1024,1024]{1,0:T(8,128)(2,1)} %get-tuple-element.149.refs_6_.refs_2_, bf16[32,64,2048]{2,1,0:T(8,128)(2,1)} %bitcast.195), custom_call_target="tpu_custom_call" | custom-call | flops 4300000256 | bytes 12000000 | tf_op jit(solution)/shard_map/memory_back/pallas_call | solution.py:536
  528.8 19.1 %attend_back_self.3 = (bf16[1024,1024]{1,0:T(8,128)(2,1)}, bf16[1024,1024]{1,0:T(8,128)(2,1)}, bf16[1024,1024]{1,0:T(8,128)(2,1)}, f32[8,1024]{1,0:T(8,128)}) custom-call(s32[8]{0:T(128)} %get-tuple-element.157.refs_0_.refs_2_, bf16[1024,1024]{1,0:T(8,128)(2,1)} %get-tuple-element.117.refs_1_, bf16[1024,1024]{1,0:T(8,128)(2,1)} %get-tuple-element.118.refs_2_, ...), custom_call_target="tpu_custom_call" | custom-call | flops 44562501632 | bytes 1000000 | tf_op jit(solution)/shard_map/attend_back_self/pallas_call | solution.py:536
  547.9 28.6 %collective-permute-done.25.refs_1_ = bf16[512,1024]{1,0:T(8,128)(2,1)S(1)} collective-permute-done((bf16[512,1024]{1,0:T(8,128)(2,1)}, bf16[512,1024]{1,0:T(8,128)(2,1)S(1)}, u32[]{:S(2)}, u32[]{:S(2)}) %collective-permute-start.25) | collective-permute-done | bytes 1048608 | tf_op jit(solution)/shard_map/ppermute | solution.py:1531
  588.2 8.1 %weight_grad_self_1.1 = (bf16[2,4,64,1536]{3,2,1,0:T(8,128)(2,1)}, bf16[2,4,64,1536]{3,2,1,0:T(8,128)(2,1)}) custom-call(s32[8]{0:T(128)} %get-tuple-element.162.refs_0_.refs_1_, bf16[1024,1024]{1,0:T(8,128)(2,1)} %get-tuple-element.163.refs_1_, bf16[1024,1024]{1,0:T(8,128)(2,1)} %get-tuple-element.159.refs_0_.refs_2_.refs_7_, ...), custom_call_target="tpu_custom_call" | custom-call | flops 10000000000 | bytes 1000000 | tf_op jit(solution)/shard_map/weight_grad_self_1/pallas_call | solution.py:536
  603.0 10.9 %attend_back_self.4 = (bf16[1024,1024]{1,0:T(8,128)(2,1)}, bf16[1024,1024]{1,0:T(8,128)(2,1)}, bf16[1024,1024]{1,0:T(8,128)(2,1)}, f32[8,1024]{1,0:T(8,128)}) custom-call(s32[8]{0:T(128)} %get-tuple-element.169.refs_0_.refs_1_, ...), custom_call_target="tpu_custom_call", output_to_operand_aliasing={{0}: (7, {}), {1}: (8, {}), {2}: (9, {}), {3}: (10, {})} | custom-call | flops 22281250816 | bytes 1000000 | tf_op jit(solution)/shard_map/attend_back_self/pallas_call | solution.py:536
  628.1 10.9 %attend_back_self.5 = (bf16[1024,1024]{1,0:T(8,128)(2,1)}, bf16[1024,1024]{1,0:T(8,128)(2,1)}, bf16[1024,1024]{1,0:T(8,128)(2,1)}, f32[8,1024]{1,0:T(8,128)}) custom-call(s32[8]{0:T(128)} %get-tuple-element.175.refs_0_.refs_2_, ...), custom_call_target="tpu_custom_call", output_to_operand_aliasing={{0}: (7, {}), {1}: (8, {}), {2}: (9, {}), {3}: (10, {})} | custom-call | flops 22281250816 | bytes 1000000 | tf_op jit(solution)/shard_map/attend_back_self/pallas_call | solution.py:536
  652.9 8.3 %weight_grad_self_0.1 = (bf16[2,4,64,1536]{3,2,1,0:T(8,128)(2,1)}, bf16[2,4,64,1536]{3,2,1,0:T(8,128)(2,1)}) custom-call(s32[8]{0:T(128)} %get-tuple-element.182.refs_0_.refs_1_, bf16[1024,1024]{1,0:T(8,128)(2,1)} %get-tuple-element.163.refs_1_, bf16[1024,1024]{1,0:T(8,128)(2,1)} %get-tuple-element.183.refs_2_, ...), custom_call_target="tpu_custom_call" | custom-call | flops 10000000000 | bytes 1000000 | tf_op jit(solution)/shard_map/weight_grad_self_0/pallas_call | solution.py:536
  667.8 11.0 %back_one.2 = (bf16[512,1024]{1,0:T(8,128)(2,1)}, f32[8,1024]{1,0:T(8,128)}) custom-call(s32[8]{0:T(128)} %get-tuple-element.189.refs_0_, f32[24,1024]{1,0:T(8,128)} %concatenate.52.refs_1_, bf16[1024,1024]{1,0:T(8,128)(2,1)} %get-tuple-element.183.refs_2_, bf16[1024,1024]{1,0:T(8,128)(2,1)} %get-tuple-element.184.refs_3_, ...), custom_call_target="tpu_custom_call" | custom-call | flops 6400000000 | bytes 20000000 | tf_op jit(solution)/shard_map/back_one/pallas_call | solution.py:536
  691.5 11.0 %back_one.3 = (bf16[512,1024]{1,0:T(8,128)(2,1)}, f32[8,1024]{1,0:T(8,128)}) custom-call(s32[8]{0:T(128)} %get-tuple-element.195.refs_0_, f32[24,1024]{1,0:T(8,128)} %concatenate.52.refs_1_, bf16[1024,1024]{1,0:T(8,128)(2,1)} %get-tuple-element.183.refs_2_, bf16[1024,1024]{1,0:T(8,128)(2,1)} %get-tuple-element.184.refs_3_, ...), custom_call_target="tpu_custom_call" | custom-call | flops 6400000000 | bytes 20000000 | tf_op jit(solution)/shard_map/back_one/pallas_call | solution.py:536
  706.2 6.2 collective-permute-done.37.refs_0_
  740.1 8.7 %collective-permute-done.48 = f32[24,1024]{1,0:T(8,128)S(1)} collective-permute-done((f32[24,1024]{1,0:T(8,128)S(1)}, f32[24,1024]{1,0:T(8,128)S(1)}, u32[]{:S(2)}, u32[]{:S(2)}) %collective-permute-start.48) | collective-permute-done | bytes 98336 | tf_op jit(solution)/shard_map/ppermute | solution.py:1630
  (319 shorter events, 230.7 us)
Async XLA Ops:
  7.2 191.6 %all-gather.5.cloned.1.call-start = ((), (), s32[]{:S(2)}) async-start(), calls=%async_computation | async-start | bytes 8650752 | tf_op jit(solution)/shard_map/all_gather | solution.py:1795
  9.9 277.1 %all-gather.7.cloned.1.call-start = ((), (), s32[]{:S(2)}) async-start(), calls=%async_computation.1 | async-start | bytes 19464192 | tf_op jit(solution)/shard_map/all_gather | solution.py:1797
  14.3 23.3 %collective-permute-start.8 = (f32[17,1024]{1,0:T(8,128)}, f32[17,1024]{1,0:T(8,128)}, u32[]{:S(2)}, u32[]{:S(2)}) collective-permute-start(f32[17,1024]{1,0:T(8,128)} %pad_maximum_fusion.8), channel_id=1, source_target_pairs={{0,2},{2,0},{4,6},{6,4},{8,10},{10,8},{12,14},{14,12},{16,18},{18,... | collective-permute-start | bytes 208904 | tf_op jit(solution)/shard_map/ppermute | solution.py:1539
  16.8 14.9 %collective-permute-start = (bf16[64,512]{1,0:T(8,128)(2,1)}, bf16[64,512]{1,0:T(8,128)(2,1)S(1)}, u32[]{:S(2)}, u32[]{:S(2)}) collective-permute-start(bf16[64,512]{1,0:T(8,128)(2,1)} %get-tuple-element.271), channel_id=1, source_target_pairs={{0,1},{1,0},{2,3},{3,2},{4,5},{5,4},{6,7},{7,6},{8,9},{9,8},{10,11... | collective-permute-start | bytes 196616 | tf_op jit(solution)/shard_map/ppermute | solution.py:1531
  26.1 124.2 %collective-permute-start.17 = (bf16[512,1024]{1,0:T(8,128)(2,1)}, bf16[512,1024]{1,0:T(8,128)(2,1)}, u32[]{:S(2)}, u32[]{:S(2)}) collective-permute-start(bf16[512,1024]{1,0:T(8,128)(2,1)} %get-tuple-element.248), channel_id=1, source_target_pairs={{0,1},{1,0},{2,3},{3,2},{4,5},{5,4},{6,7},{7,6},{8,9},{9,8},{10,11... | collective-permute-start | bytes 3145736 | tf_op jit(solution)/shard_map/ppermute | solution.py:1531
  38.5 23.4 %collective-permute-start.9 = (f32[17,1024]{1,0:T(8,128)S(1)}, f32[17,1024]{1,0:T(8,128)S(1)}, u32[]{:S(2)}, u32[]{:S(2)}) collective-permute-start(f32[17,1024]{1,0:T(8,128)S(1)} %fusion.30), channel_id=1, source_target_pairs={{0,1},{1,0},{2,3},{3,2},{4,5},{5,4},{6,7},{7,6},{8,9},{9,8},{10,11... | collective-permute-start | bytes 208904 | tf_op jit(solution)/shard_map/ppermute | solution.py:1531
  39.3 24.2 %collective-permute-start.2 = (bf16[4,64,512]{2,1,0:T(8,128)(2,1)S(1)}, bf16[4,64,512]{2,1,0:T(8,128)(2,1)S(1)}, u32[]{:S(2)}, u32[]{:S(2)}) collective-permute-start(bf16[4,64,512]{2,1,0:T(8,128)(2,1)S(1)} %pad_maximum_fusion.4.refs_8_.refs_12_), channel_id=1, source_target_pairs={{0,8},{2,10},{4,12},{6,14},{8,16},{10,18},{12,20},{14,22},{16,24},... | collective-permute-start | bytes 786440 | tf_op jit(solution)/shard_map/ppermute | solution.py:1543
  47.0 29.5 %collective-permute-start.7 = (bf16[4,64,1024]{2,1,0:T(8,128)(2,1)S(1)}, bf16[4,64,1024]{2,1,0:T(8,128)(2,1)S(1)}, u32[]{:S(2)}, u32[]{:S(2)}) collective-permute-start(bf16[4,64,1024]{2,1,0:T(8,128)(2,1)S(1)} %pad_maximum_fusion.1.refs_3_.refs_7_), channel_id=1, source_target_pairs={{0,1},{1,0},{2,3},{3,2},{4,5},{5,4},{6,7},{7,6},{8,9},{9,8},{10,11... | collective-permute-start | bytes 1572872 | tf_op jit(solution)/shard_map/ppermute | solution.py:1531
  75.1 26.0 %collective-permute-start.14 = (bf16[4,64,1024]{2,1,0:T(8,128)(2,1)S(1)}, bf16[4,64,1024]{2,1,0:T(8,128)(2,1)S(1)}, u32[]{:S(2)}, u32[]{:S(2)}) collective-permute-start(bf16[4,64,1024]{2,1,0:T(8,128)(2,1)S(1)} %pad_maximum_fusion.1.refs_3_.refs_7_), channel_id=1, source_target_pairs={{0,4},{2,6},{4,0},{6,2},{8,12},{10,14},{12,8},{14,10},{16,20},{18,... | collective-permute-start | bytes 1572872 | tf_op jit(solution)/shard_map/ppermute | solution.py:1535
  77.4 33.8 %collective-permute-start.15 = (bf16[4,64,1024]{2,1,0:T(8,128)(2,1)}, bf16[4,64,1024]{2,1,0:T(8,128)(2,1)S(1)}, u32[]{:S(2)}, u32[]{:S(2)}) collective-permute-start(bf16[4,64,1024]{2,1,0:T(8,128)(2,1)} %get-tuple-element.113.refs_4_.refs_8_), channel_id=1, source_target_pairs={{0,4},{2,6},{4,0},{6,2},{8,12},{10,14},{12,8},{14,10},{16,20},{18,... | collective-permute-start | bytes 1572872 | tf_op jit(solution)/shard_map/ppermute | solution.py:1535
  112.2 41.9 %collective-permute-start.16 = (bf16[16,64,1024]{2,1,0:T(8,128)(2,1)}, bf16[16,64,1024]{2,1,0:T(8,128)(2,1)}, u32[]{:S(2)}, u32[]{:S(2)}) collective-permute-start(bf16[16,64,1024]{2,1,0:T(8,128)(2,1)} %constant_dynamic-update-slice_fusion.6), channel_id=1, source_target_pairs={{0,2},{2,0},{4,6},{6,4},{8,10},{10,8},{12,14},{14,12},{16,18},{18,... | collective-permute-start | bytes 6291464 | tf_op jit(solution)/shard_map/ppermute | solution.py:1539
  130.3 23.8 %collective-permute-start.13 = (bf16[16,64,512]{2,1,0:T(8,128)(2,1)}, bf16[16,64,512]{2,1,0:T(8,128)(2,1)}, u32[]{:S(2)}, u32[]{:S(2)}) collective-permute-start(bf16[16,64,512]{2,1,0:T(8,128)(2,1)} %constant_dynamic-update-slice_fusion), channel_id=1, source_target_pairs={{0,2},{2,0},{4,6},{6,4},{8,10},{10,8},{12,14},{14,12},{16,18},{18,... | collective-permute-start | bytes 3145736 | tf_op jit(solution)/shard_map/ppermute | solution.py:1539
  135.2 13.7 %collective-permute-start.18 = (f32[17,1024]{1,0:T(8,128)S(1)}, f32[17,1024]{1,0:T(8,128)S(1)}, u32[]{:S(2)}, u32[]{:S(2)}) collective-permute-start(f32[17,1024]{1,0:T(8,128)S(1)} %copy-done.28), channel_id=1, source_target_pairs={{0,16},{2,18},{4,20},{6,22},{8,24},{10,26},{12,28},{14,30},{16,0},... | collective-permute-start | bytes 208904 | tf_op jit(solution)/shard_map/ppermute | solution.py:1809
  154.2 42.3 %collective-permute-start.19 = (bf16[512,1024]{1,0:T(8,128)(2,1)}, bf16[512,1024]{1,0:T(8,128)(2,1)S(1)}, u32[]{:S(2)}, u32[]{:S(2)}) collective-permute-start(bf16[512,1024]{1,0:T(8,128)(2,1)} %get-tuple-element.124), channel_id=1, source_target_pairs={{0,1},{1,0},{2,3},{3,2},{4,5},{5,4},{6,7},{7,6},{8,9},{9,8},{10,11... | collective-permute-start | bytes 3145736 | tf_op jit(solution)/shard_map/ppermute | solution.py:1531
  210.5 48.2 %collective-permute-start.20 = (bf16[512,1024]{1,0:T(8,128)(2,1)}, bf16[512,1024]{1,0:T(8,128)(2,1)S(1)}, u32[]{:S(2)}, u32[]{:S(2)}) collective-permute-start(bf16[512,1024]{1,0:T(8,128)(2,1)} %get-tuple-element.130), channel_id=1, source_target_pairs={{0,1},{1,0},{2,3},{3,2},{4,5},{5,4},{6,7},{7,6},{8,9},{9,8},{10,11... | collective-permute-start | bytes 3145736 | tf_op jit(solution)/shard_map/ppermute | solution.py:1531
  377.3 17.0 %collective-permute-start.22 = (bf16[2,2,4,64,4096]{4,3,2,1,0:T(8,128)(2,1)}, bf16[2,2,4,64,4096]{4,3,2,1,0:T(8,128)(2,1)}, u32[]{:S(2)}, u32[]{:S(2)}) collective-permute-start(bf16[2,2,4,64,4096]{4,3,2,1,0:T(8,128)(2,1)} %get-tuple-element.139), channel_id=1, source_target_pairs={{0,2},{2,0},{4,6},{6,4},{8,10},{10,8},{12,14},{14,12},{16,18},{18,... | collective-permute-start | bytes 25165832 | tf_op jit(solution)/shard_map/ppermute | solution.py:1539
  380.7 109.1 %collective-permute-start.21 = (bf16[512,1024]{1,0:T(8,128)(2,1)}, bf16[512,1024]{1,0:T(8,128)(2,1)}, u32[]{:S(2)}, u32[]{:S(2)}) collective-permute-start(bf16[512,1024]{1,0:T(8,128)(2,1)} %get-tuple-element.252), channel_id=1, source_target_pairs={{0,1},{1,0},{2,3},{3,2},{4,5},{5,4},{6,7},{7,6},{8,9},{9,8},{10,11... | collective-permute-start | bytes 3145736 | tf_op jit(solution)/shard_map/ppermute | solution.py:1531
  404.0 92.8 %collective-permute-start.23 = (bf16[2,4,64,4096]{3,2,1,0:T(8,128)(2,1)}, bf16[2,4,64,4096]{3,2,1,0:T(8,128)(2,1)}, u32[]{:S(2)}, u32[]{:S(2)}) collective-permute-start(bf16[2,4,64,4096]{3,2,1,0:T(8,128)(2,1)} %get-tuple-element.240), channel_id=1, source_target_pairs={{0,4},{2,6},{4,0},{6,2},{8,12},{10,14},{12,8},{14,10},{16,20},{18,... | collective-permute-start | bytes 12582920 | tf_op jit(solution)/shard_map/ppermute | solution.py:1535
  496.8 21.1 %collective-permute-start.24 = (bf16[2,2,4,64,2560]{4,3,2,1,0:T(8,128)(2,1)}, bf16[2,2,4,64,2560]{4,3,2,1,0:T(8,128)(2,1)}, u32[]{:S(2)}, u32[]{:S(2)}) collective-permute-start(bf16[2,2,4,64,2560]{4,3,2,1,0:T(8,128)(2,1)} %get-tuple-element.156), channel_id=1, source_target_pairs={{0,2},{2,0},{4,6},{6,4},{8,10},{10,8},{12,14},{14,12},{16,18},{18,... | collective-permute-start | bytes 15728648 | tf_op jit(solution)/shard_map/ppermute | solution.py:1539
  507.0 77.1 %collective-permute-start.26 = (bf16[4,64,4096]{2,1,0:T(8,128)(2,1)}, bf16[4,64,4096]{2,1,0:T(8,128)(2,1)}, u32[]{:S(2)}, u32[]{:S(2)}) collective-permute-start(bf16[4,64,4096]{2,1,0:T(8,128)(2,1)} %fusion.4), channel_id=1, source_target_pairs={{0,1},{1,0},{2,3},{3,2},{4,5},{5,4},{6,7},{7,6},{8,9},{9,8},{10,11... | collective-permute-start | bytes 6291464 | tf_op jit(solution)/shard_map/ppermute | solution.py:1531
  527.2 49.3 %collective-permute-start.25 = (bf16[512,1024]{1,0:T(8,128)(2,1)}, bf16[512,1024]{1,0:T(8,128)(2,1)S(1)}, u32[]{:S(2)}, u32[]{:S(2)}) collective-permute-start(bf16[512,1024]{1,0:T(8,128)(2,1)} %get-tuple-element.250), channel_id=1, source_target_pairs={{0,1},{1,0},{2,3},{3,2},{4,5},{5,4},{6,7},{7,6},{8,9},{9,8},{10,11... | collective-permute-start | bytes 3145736 | tf_op jit(solution)/shard_map/ppermute | solution.py:1531
  528.6 86.9 %collective-permute-start.29 = (bf16[2,4,64,2560]{3,2,1,0:T(8,128)(2,1)}, bf16[2,4,64,2560]{3,2,1,0:T(8,128)(2,1)S(1)}, u32[]{:S(2)}, u32[]{:S(2)}) collective-permute-start(bf16[2,4,64,2560]{3,2,1,0:T(8,128)(2,1)} %get-tuple-element.242), channel_id=1, source_target_pairs={{0,4},{2,6},{4,0},{6,2},{8,12},{10,14},{12,8},{14,10},{16,20},{18,... | collective-permute-start | bytes 7864328 | tf_op jit(solution)/shard_map/ppermute | solution.py:1535
  585.7 14.0 %collective-permute-start.27 = (bf16[64,4096]{1,0:T(8,128)(2,1)S(1)}, bf16[64,4096]{1,0:T(8,128)(2,1)S(1)}, u32[]{:S(2)}, u32[]{:S(2)}) collective-permute-start(bf16[64,4096]{1,0:T(8,128)(2,1)S(1)} %fusion.14), channel_id=1, source_target_pairs={{0,8},{2,10},{4,12},{6,14},{8,16},{10,18},{12,20},{14,22},{16,24},... | collective-permute-start | bytes 1572872 | tf_op jit(solution)/shard_map/ppermute | solution.py:1543
  619.8 19.2 %collective-permute-start.31 = (bf16[64,4096]{1,0:T(8,128)(2,1)}, bf16[64,4096]{1,0:T(8,128)(2,1)S(1)}, u32[]{:S(2)}, u32[]{:S(2)}) collective-permute-start(bf16[64,4096]{1,0:T(8,128)(2,1)} %fusion.11), channel_id=1, source_target_pairs={{0,8},{2,10},{4,12},{6,14},{8,16},{10,18},{12,20},{14,22},{16,24},... | collective-permute-start | bytes 1572872 | tf_op jit(solution)/shard_map/ppermute | solution.py:1543
  622.8 29.3 %collective-permute-start.32 = (bf16[4,64,1536]{2,1,0:T(8,128)(2,1)}, bf16[4,64,1536]{2,1,0:T(8,128)(2,1)S(1)}, u32[]{:S(2)}, u32[]{:S(2)}) collective-permute-start(bf16[4,64,1536]{2,1,0:T(8,128)(2,1)} %fusion.15), channel_id=1, source_target_pairs={{0,4},{2,6},{4,0},{6,2},{8,12},{10,14},{12,8},{14,10},{16,20},{18,... | collective-permute-start | bytes 2359304 | tf_op jit(solution)/shard_map/ppermute | solution.py:1535
  626.6 34.6 %collective-permute-start.33 = (bf16[4,64,2560]{2,1,0:T(8,128)(2,1)}, bf16[4,64,2560]{2,1,0:T(8,128)(2,1)}, u32[]{:S(2)}, u32[]{:S(2)}) collective-permute-start(bf16[4,64,2560]{2,1,0:T(8,128)(2,1)} %fusion.8), channel_id=1, source_target_pairs={{0,1},{1,0},{2,3},{3,2},{4,5},{5,4},{6,7},{7,6},{8,9},{9,8},{10,11... | collective-permute-start | bytes 3932168 | tf_op jit(solution)/shard_map/ppermute | solution.py:1531
  661.3 23.0 %collective-permute-start.34 = (bf16[2,4,64,1536]{3,2,1,0:T(8,128)(2,1)}, bf16[2,4,64,1536]{3,2,1,0:T(8,128)(2,1)}, u32[]{:S(2)}, u32[]{:S(2)}) collective-permute-start(bf16[2,4,64,1536]{3,2,1,0:T(8,128)(2,1)} %get-tuple-element.190), channel_id=1, source_target_pairs={{0,2},{2,0},{4,6},{6,4},{8,10},{10,8},{12,14},{14,12},{16,18},{18,... | collective-permute-start | bytes 4718600 | tf_op jit(solution)/shard_map/ppermute | solution.py:1539
  664.9 19.3 %collective-permute-start.36 = (bf16[4,64,1536]{2,1,0:T(8,128)(2,1)}, bf16[4,64,1536]{2,1,0:T(8,128)(2,1)S(1)}, u32[]{:S(2)}, u32[]{:S(2)}) collective-permute-start(bf16[4,64,1536]{2,1,0:T(8,128)(2,1)} %fusion.7), channel_id=1, source_target_pairs={{0,1},{1,0},{2,3},{3,2},{4,5},{5,4},{6,7},{7,6},{8,9},{9,8},{10,11... | collective-permute-start | bytes 2359304 | tf_op jit(solution)/shard_map/ppermute | solution.py:1531
  667.4 16.8 %collective-permute-start.35 = (bf16[64,2560]{1,0:T(8,128)(2,1)}, bf16[64,2560]{1,0:T(8,128)(2,1)S(1)}, u32[]{:S(2)}, u32[]{:S(2)}) collective-permute-start(bf16[64,2560]{1,0:T(8,128)(2,1)} %fusion.22), channel_id=1, source_target_pairs={{0,8},{2,10},{4,12},{6,14},{8,16},{10,18},{12,20},{14,22},{16,24},... | collective-permute-start | bytes 983048 | tf_op jit(solution)/shard_map/ppermute | solution.py:1543
  687.8 18.4 %collective-permute-start.38 = (bf16[4,64,1536]{2,1,0:T(8,128)(2,1)}, bf16[4,64,1536]{2,1,0:T(8,128)(2,1)S(1)}, u32[]{:S(2)}, u32[]{:S(2)}) collective-permute-start(bf16[4,64,1536]{2,1,0:T(8,128)(2,1)} %fusion.16), channel_id=1, source_target_pairs={{0,4},{2,6},{4,0},{6,2},{8,12},{10,14},{12,8},{14,10},{16,20},{18,... | collective-permute-start | bytes 2359304 | tf_op jit(solution)/shard_map/ppermute | solution.py:1535
  688.5 23.9 %collective-permute-start.37 = (bf16[512,1024]{1,0:T(8,128)(2,1)}, bf16[512,1024]{1,0:T(8,128)(2,1)}, u32[]{:S(2)}, u32[]{:S(2)}) collective-permute-start(bf16[512,1024]{1,0:T(8,128)(2,1)} %get-tuple-element.197), channel_id=1, source_target_pairs={{0,1},{1,0},{2,3},{3,2},{4,5},{5,4},{6,7},{7,6},{8,9},{9,8},{10,11... | collective-permute-start | bytes 3145736 | tf_op jit(solution)/shard_map/ppermute | solution.py:1531
  715.6 16.5 %collective-permute-start.43 = (bf16[64,2560]{1,0:T(8,128)(2,1)S(1)}, bf16[64,2560]{1,0:T(8,128)(2,1)S(1)}, u32[]{:S(2)}, u32[]{:S(2)}) collective-permute-start(bf16[64,2560]{1,0:T(8,128)(2,1)S(1)} %fusion.18), channel_id=1, source_target_pairs={{0,8},{2,10},{4,12},{6,14},{8,16},{10,18},{12,20},{14,22},{16,24},... | collective-permute-start | bytes 983048 | tf_op jit(solution)/shard_map/ppermute | solution.py:1543
  (70 other events, 559.4 us)
Sparse Core Ops, SparseCore 0:
  11.6 106.5 all-gather.4
  121.2 165.8 all-gather.6

commit v3 on v2

--- a/solution.py
+++ b/solution.py
@@ -1074,11 +1074,12 @@
 
 
 FFB = 512
+FFR = 512
 
 
 def ffn_kernel(info, par, bias_ref, n_ref, nt_ref, g_ref, gt_ref, h_ref, *rest):
-    pieces, rest = rest[:1], rest[1:]
-    (out_ref, dn_ref, send_ref, keep_ref, dbias_ref, w_in, w_out, acc, active, du, temp, sems) = rest
+    pieces, rest = rest[:6], rest[6:]
+    (out_ref, other_ref, dn_ref, send_ref, keep_ref, dbias_ref, w_in, w_out, acc, active, du, temp, sems) = rest
     half, part = pl.program_id(0), pl.program_id(1)
     parts = pl.num_programs(1)
     n = n_ref.shape[0]
@@ -1087,8 +1088,8 @@
 
     @pl.when(first_step)
     def _():
-        start_all(pieces, 0, 2048, w_in, sems.at[0])
-        start_all(pieces, 2048, 2048, w_out, sems.at[1])
+        start_all(pieces[:1], 2048, 2048, w_in, sems.at[0])
+        start_weight(info, pieces[1:], "xyz", 0, 2048, w_out, sems.at[1])
         acc[...] = jnp.zeros(acc.shape, F32)
         dn_ref[...] = jnp.zeros(dn_ref.shape, F32)
 
@@ -1101,33 +1102,41 @@
     first = w_in.at[slab, :, cols]
     second = w_out.at[slab, :, cols]
     total_bias = None
-    for chunk in range(n // ROWS):
-        rows = slice(chunk * ROWS, chunk * ROWS + ROWS)
-        u = mm(n_ref[rows, :], first[...]) + bias_ref[0:1, :]
+    chunks = [slice(start, start + FFR) for start in range(0, n, FFR)]
+
+    def products(rows):
+        return (mm(n_ref[rows, :], first[...]) + bias_ref[0:1, :], mm(g_ref[rows, :], second[...]))
+
+    ahead = products(chunks[0])
+    for index, rows in enumerate(chunks):
+        u, dr = ahead
+        if index + 1 < len(chunks):
+            ahead = products(chunks[index + 1])
         square = u * u
         bend = jnp.tanh(u * (GELU_A + GELU_A * GELU_B * square))
         half_up = 0.5 + 0.5 * bend
         r = (u * half_up).astype(BF)
         active[rows, :] = r
         slope = half_up + 0.5 * u * (1.0 - bend * bend) * (GELU_A + 3.0 * GELU_A * GELU_B * square)
-        dr = mm(g_ref[rows, :], second[...])
         d = (dr * slope).astype(BF)
         du[rows, :] = d
         sums = row_sum(d.astype(F32))
         total_bias = sums if total_bias is None else total_bias + sums
-        up = mm_nt(r, second[...])
-        down = mm_nt(d, first[...])
-
-        acc[rows, :] += up
-        dn_ref[rows, :] += down
+        acc[rows, :] += mm_nt(r, second[...])
+        dn_ref[rows, :] += mm_nt(d, first[...])
 
     dbias_ref[0:1, :] = total_bias
     for zrel in range(4):
         zz = lax.rem(info[0] + zrel, 4)
         rows = pl.ds(pl.multiple_of(zz * 256, 256), 256)
-        temp[zrel % 2, :, :FFB] = mm(nt_ref[rows, :], du[...]).astype(BF)
-        temp[zrel % 2, :, FFB:] = mm(gt_ref[rows, :], active[...]).astype(BF)
-        store_blocks(info, temp.at[zrel % 2], send_ref, keep_ref, zrel, "zxy", 2 * FFB)
+        for kind, (left, right) in enumerate(((nt_ref, du), (gt_ref, active))):
+            temp[kind] = mm(left[rows, :], right[...]).astype(BF)
+            for yrel in range(2):
+                yy = info[1] if yrel == 0 else 1 - info[1]
+                for crel, target in enumerate((keep_ref, send_ref)):
+                    cc = info[2] if crel == 0 else 1 - info[2]
+                    row = pl.multiple_of(yy * 128 + cc * 64, 64)
+                    target[yrel, 0, zrel, kind, :, :] = temp[kind, pl.ds(row, 64), :]
 
     @pl.when((half == 1) & (part == parts - 1))
     def _():
@@ -1135,14 +1144,16 @@
             start = lax.rem(info[3] * (n // 2) + chunk * ROWS, n)
             rows = pl.ds(pl.multiple_of(start, ROWS), ROWS)
             value = h_ref[rows, :] + acc[rows, :] + par[8:9, :]
-            out_ref[chunk * ROWS : chunk * ROWS + ROWS, :] = value.astype(BF)
+            target = out_ref if chunk * ROWS < n // 2 else other_ref
+            at = chunk * ROWS % (n // 2)
+            target[at : at + ROWS, :] = value.astype(BF)
 
 
 def call_ffn(info, par, bias, normed, normed_t, grad, grad_t, hidden, pieces, after=(), through=()):
     n = normed.shape[0]
     parts = 2048 // FFB
     whole = lambda shape: pl.BlockSpec(shape, lambda x, t, s: (0, 0))
-    blocks = pl.BlockSpec((2, 1, 4, 64, 2 * FFB), lambda x, t, s: (0, x, 0, 0, t))
+    blocks = pl.BlockSpec((2, 1, 4, 2, 64, FFB), lambda x, t, s: (0, x, 0, 0, 0, t))
     bias_spec = lambda rows: pl.BlockSpec((rows, FFB), lambda x, t, s: (0, lax.rem(x + s[3], 2) * parts + t))
     return gated_call(
         after,
@@ -1159,9 +1170,10 @@
                 whole((1024, n)),
                 whole((n, 1024)),
             ]
-            + [pl.BlockSpec(memory_space=ANYM)],
+            + [pl.BlockSpec(memory_space=ANYM)] * 6,
             out_specs=[
-                whole((n, 1024)),
+                whole((n // 2, 1024)),
+                whole((n // 2, 1024)),
                 whole((n, 1024)),
                 blocks,
                 blocks,
@@ -1173,15 +1185,16 @@
                 VM((n, 1024), F32),
                 VM((n, FFB), BF),
                 VM((n, FFB), BF),
-                VM((2, 256, 2 * FFB), BF),
+                VM((2, 256, FFB), BF),
                 pltpu.SemaphoreType.DMA((2, 2)),
             ],
         ),
         out_shape=[
-            jax.ShapeDtypeStruct((n, 1024), BF),
+            jax.ShapeDtypeStruct((n // 2, 1024), BF),
+            jax.ShapeDtypeStruct((n // 2, 1024), BF),
             jax.ShapeDtypeStruct((n, 1024), F32),
-            jax.ShapeDtypeStruct((2, 2, 4, 64, 4096), BF),
-            jax.ShapeDtypeStruct((2, 2, 4, 64, 4096), BF),
+            jax.ShapeDtypeStruct((2, 2, 4, 2, 64, 2048), BF),
+            jax.ShapeDtypeStruct((2, 2, 4, 2, 64, 2048), BF),
             jax.ShapeDtypeStruct((8, 4096), F32),
         ],
         compiler_params=params_of(60),
@@ -1311,7 +1324,7 @@
 
 def memory_back_kernel(info, dk_ref, dv_ref, *rest):
     pieces, rest = rest[:1], rest[1:]
-    out_ref, wk, wv, sems = rest
+    out_ref, other_ref, wk, wv, sems = rest
 
     @pl.when(pl.program_id(0) == 0)
     def _():
@@ -1329,7 +1342,15 @@
 
             term = mm_nt(ref[:, slab * 512 : slab * 512 + 512], weight[slab])
             total = term if total is None else total + term
-    out_ref[...] = total.astype(BF)
+    own = pl.program_id(0) < pl.num_programs(0) // 2
+
+    @pl.when(own)
+    def _():
+        out_ref[...] = total.astype(BF)
+
+    @pl.when(jnp.logical_not(own))
+    def _():
+        other_ref[...] = total.astype(BF)
 
 
 def call_memory_back(info, dk, dv, pieces, after=(), through=()):
@@ -1343,10 +1364,13 @@
             num_scalar_prefetch=1,
             grid=(n // ROWS,),
             in_specs=[rows, rows] + [pl.BlockSpec(memory_space=ANYM)],
-            out_specs=pl.BlockSpec((ROWS, 1024), lambda i, s: (i, 0)),
+            out_specs=[
+                pl.BlockSpec((ROWS, 1024), lambda i, s: (jnp.minimum(i, steps - 1), 0)),
+                pl.BlockSpec((ROWS, 1024), lambda i, s: (jnp.maximum(i - steps, 0), 0)),
+            ],
             scratch_shapes=[VM((2, 1024, 512), BF)] * 2 + [pltpu.SemaphoreType.DMA((2, 2))],
         ),
-        out_shape=jax.ShapeDtypeStruct((n, 1024), BF),
+        out_shape=[jax.ShapeDtypeStruct((n // 2, 1024), BF)] * 2,
         compiler_params=params_of(60),
         cost_estimate=cost(4.3e9, 12e6),
         through=through,
@@ -1522,9 +1546,9 @@
     return [(i, i ^ axis_bit) for i in range(16)]
 
 
-NEAR_Z = [(i, i ^ 4) for i in range(16)]
+RING = [(i, (i + 4) % 16) for i in range(16)]
 FAR_Z = [(i, i ^ 8) for i in range(16)]
-RING = [(i, (i + 4) % 16) for i in range(16)]
+BACK = [(i, (i + 12) % 16) for i in range(16)]
 
 
 def swap_x(value):
@@ -1622,12 +1646,11 @@
     )()
 
 
-def sum_small(value):
+def sum_rest(value):
     value = value + swap_core(value)
-    value = value + swap_x(value)
     value = value + swap_y(value)
-    value = value + lax.ppermute(value, "dp", NEAR_Z)
-    return value + lax.ppermute(value, "dp", FAR_Z)
+    one, two, three = next_z(value), lax.ppermute(value, "dp", FAR_Z), lax.ppermute(value, "dp", BACK)
+    return (value + two) + (one + three)
 
 
 def join(kept, received):
@@ -1788,71 +1811,72 @@
 
     small = place_small(norm_gains, feature_biases, head_biases, inner_bias, dp, me)
     info = Cell(info)
-    x = Exchange(tokens, me)
+    rest = jnp.concatenate([cross_in[1], cross_in[2], self_out.T, cross_in[0], fc_in, cross_out.T], 1)
+    w_rest = [lax.all_gather(rest, ("dp", "mp"), axis=0, tiled=False)]
     own_k = GatherXYZ(self_in[1])
     own_qv = GatherZXY(jnp.concatenate([self_in[0], self_in[2]], 1))
-    middle = jnp.concatenate([cross_in[1], cross_in[2], self_out.T, cross_in[0]], 1)
-    w_mid = [lax.all_gather(middle, ("dp", "mp"), axis=0, tiled=False)]
-    outer = jnp.concatenate([fc_in, fc_out.T, cross_out.T], 1)
-    w_out = [lax.all_gather(outer, ("dp", "mp"), axis=0, tiled=False)]
-    mem, cot = Exchange(memory, me), Exchange(cotangent, me)
-    own_k.x(), own_qv.z(), x.go()
-    small = small + swap_core(small)
-    own_k.y(), own_qv.z()
-    small = small + swap_x(small)
+    outer = GatherXYZ(fc_out.T)
+    x, mem, cot = Exchange(tokens, me), Exchange(memory, me), Exchange(cotangent, me)
+    small = Cell(small + swap_x(small))
+    own_k.x(), own_qv.z()
+    hold([x.theirs, small], [])
+    small = sum_rest(small.value)
+    own_k.y(), own_qv.z(), x.go()
     own_k.z(), own_qv.z()
-    small = small + swap_y(small)
     own_k.z(), own_qv.x(), own_qv.y()
-    small = Cell(small + lax.ppermute(small, "dp", NEAR_Z))
-    hold([mem.theirs, own_k.quads[2], own_qv.over_x, small], [])
-    own_k.z(), own_qv.xy()
-    small = small.value + lax.ppermute(small.value, "dp", FAR_Z)
-    own_k.core(), own_qv.core()
+    hold([mem.theirs, outer.shard, own_k.quads[2], own_qv.over_x], [x.other])
+    own_k.z(), own_qv.xy(), outer.x()
+    hold([own_k.quads[3], own_qv.over_xy, outer.pair], [])
+    own_k.core(), own_qv.core(), outer.y()
     par = jnp.concatenate([small[:13], jnp.zeros((11, 1024), F32)], 0)
     inner = jnp.broadcast_to(small[13:17].reshape(1, 4096), (8, 4096))
     x = x.whole()
-    hold([info, mem.theirs], [own_k.other, own_qv.other, x])
+    hold([info, outer.quads[0], mem.theirs], [own_k.other, own_qv.other, x, par, inner])
+    outer.z(), mem.go()
     w_self = own_qv.pieces() + own_k.pieces()
-    mem.go()
     q1, k1, v1, n1_t = call_qkv(info, par, x, w_self)
-    attended = call_attend(info, q1, k1, v1, True, 0, 4)
-    o1, lse1 = call_attend(info, q1, k1, v1, True, 4, 4, attended)
-    h1, q2, n2_t = call_after_self(info, par, x, o1, w_mid)
+    o1, lse1 = call_attend(info, q1, k1, v1, True, 0, 8)
+    hold([info, outer.quads[1], cot.theirs], [o1, mem.other])
+    outer.z(), cot.go()
+    h1, q2, n2_t = call_after_self(info, par, x, o1, w_rest)
     mem = mem.whole()
-    hold([info, cot.theirs], [h1, mem])
-    cot.go()
-    k2, v2, mem_t = call_kv(info, par, mem, w_mid)
+    k2, v2, mem_t = call_kv(info, par, mem, w_rest, after=[q2])
+    hold([info, outer.quads[2]], [k2])
+    outer.z()
     o2, lse2 = call_attend(info, q2, k2, v2, False, 0, 8)
-    h2, n3, n3_t, g3, g3_t, g_sum = call_after_cross(info, par, scale, h1, o2, cot.whole(), w_out)
-    out, dn3, send_fc, keep_fc, d_inner = call_ffn(info, par, inner, n3, n3_t, g3, g3_t, h2, w_out)
-
-    half = out.shape[0] // 2
+    hold([info, outer.quads[3]], [o2, cot.other])
+    outer.core()
+    h2, n3, n3_t, g3, g3_t, g_sum = call_after_cross(info, par, scale, h1, o2, cot.whole(), w_rest)
+    w_fc = w_rest + outer.pieces()
+    out, out_peer, dn3, send_fc, keep_fc, d_inner = call_ffn(info, par, inner, n3, n3_t, g3, g3_t, h2, w_fc)
+
     sum_f = ReduceZXY(send_fc, keep_fc)
     sum_f.core()
-    out_other = swap_x(out[half:])
-    dh2, do2, g2_t, sums3 = call_back_three(info, par, dn3, h2, g3, w_out)
+    out_other = swap_x(out_peer)
+    dh2, do2, g2_t, sums3 = call_back_three(info, par, dn3, h2, g3, w_rest)
     hold([info, sum_f.received], [do2])
     sum_f.y()
     dq2, dk2, dv2, bias2 = call_attend_back(info, q2, k2, v2, o2, do2, lse2, False, 0, 8)
-    dh1, do1, g1_t, sums2 = call_back_two(info, par, dq2, h1, dh2, w_mid)
+    dh1, do1, g1_t, sums2 = call_back_two(info, par, dq2, h1, dh2, w_rest)
     cross = call_weight_grad(
         info, "zxy", [mem_t, n2_t, g2_t, g1_t], [dk2, dv2, dq2, o2, o1], (0, 0, 1, 2, 3), "weight_grad_cross", after=[do1]
     )
     sum_c = ReduceZXY(*cross)
     hold([info, sum_c.send, sum_f.received], [out_other, sum_c.keep])
     sum_c.core(), sum_f.x()
-    grad_mem = Cell(call_memory_back(info, dk2, dv2, w_mid))
-    hold([info, sum_c.received, grad_mem], [])
+    grad_mem, mem_peer = call_memory_back(info, dk2, dv2, w_rest)
+    mem_peer = Cell(mem_peer)
+    hold([info, sum_c.received], [grad_mem])
     sum_c.y()
-    memory_other = swap_x(grad_mem.value[half:])
     back = call_attend_back(info, q1, k1, v1, o1, do1, lse1, True, 0, 4, other=True)
-    hold([info, sum_f.received], [back[0], memory_other])
+    hold([info, sum_f.received, mem_peer], [back[0]])
     sum_f.z()
+    memory_other = swap_x(mem_peer.value)
     sum_s1 = ReduceHalves(*call_half_grad(info, True, [n1_t], back[:3], (0, 0, 0), "weight_grad_self_1"))
     hold([info, sum_s1.send, sum_f.moving], [sum_s1.keep])
     sum_s1.core(), sum_f.z()
     back = call_attend_back(info, q1, k1, v1, o1, do1, lse1, True, 0, 2, back, other=False)
-    hold([info, sum_s1.received, sum_c.received, sum_f.moving], [back[0]])
+    hold([info, sum_s1.received, sum_c.received, sum_f.moving], [back[0], memory_other])
     sum_s1.y(), sum_c.x(), sum_f.z()
     dq1, dk1, dv1, bias1 = call_attend_back(info, q1, k1, v1, o1, do1, lse1, True, 2, 2, back, other=False)
     hold([info, sum_s1.arrived], [bias1, sum_f.moving])
@@ -1870,14 +1894,15 @@
     hold([sum_s0.arrived, sum_c.moving, d_small], [tokens_other])
     sum_s0.across = across
     moving = sum_s0.z()
-    d_small = sum_small(d_small.value)
+    d_small = sum_rest(d_small.value)
+    d_small = d_small + swap_x(d_small)
     moving = sum_s0.z(moving)
     sum_c.z()
     moving = sum_s0.z(moving)
-    output = both_sequences(out[:half], out_other, me)
+    output = both_sequences(out, out_other, me)
     grad_tokens = both_sequences(grad_own, tokens_other, me).astype(F32)
-    grad_memory = both_sequences(grad_mem.value[:half], memory_other, me).astype(F32)
-    fc = sum_f.result().reshape(64, 4, 2, 512)
+    grad_memory = both_sequences(grad_mem, memory_other, me).astype(F32)
+    fc = sum_f.result()
     self_all = sum_s0.sum(0) + moving[1].astype(F32)
     column = 32 * (2 * dp + me)
     take = lax.dynamic_slice
@@ -1890,8 +1915,8 @@
         crossed[:, 2048:].T,
         jnp.stack([crossed[:, 1024:1536], crossed[:, :512], crossed[:, 512:1024]]),
         crossed[:, 1536:2048].T,
-        fc[:, :, 0].reshape(64, 2048),
-        fc[:, :, 1].reshape(64, 2048).T,
+        fc[0],
+        fc[1].T,
         take(d_small[9:13].reshape(4, 16, 64), (0, me * 8, dp * 4), (4, 8, 4)),
         take(d_small[13:17].reshape(16, 256), (me * 8, dp * 16), (8, 16)),
         take(d_small[:3], (0, column), (3, 32)),

time: 769 us -> 728 us (0.947)
  waiting for transfers between devices: 185 us -> 147 us
    ppermute x15 -> x20, waiting for transfers between devices: 23.1 us -> 52.4 us  [next_z(): return lax.ppermute(value, 'dp', RING)]
    all_gather x2 -> x1, waiting for transfers between devices: 25.9 us -> 0.01 us  [one_sequence_body(): w_rest = [lax.all_gather(rest, ('dp', 'mp'), axis=0, tiled=False)]]
    ppermute x13 -> x14, waiting for transfers between devices: 70.7 us -> 46 us  [swap_x(): return lax.ppermute(value, 'mp', [(0, 1), (1, 0)])]
    ppermute x9 -> x10, waiting for transfers between devices: 39.6 us -> 27.8 us  [swap_y(): return lax.ppermute(value, 'dp', along(2))]
    unnamed x119 -> x111, local copies, waits for them, and re-layouts: 34.8 us -> 40.5 us
    ppermute x15 -> x20, starting transfers between devices: 17.1 us -> 21.5 us  [next_z(): return lax.ppermute(value, 'dp', RING)]
    pallas_call x33 -> x36, Pallas kernels: 359 us -> 354 us  [run(): results = call(*values_of(operands), *after, *passed)]
  transfers between devices with their start and end apart: 51 -> 58, of which waited for: 23 -> 26; matrix products, arithmetic and copies ran while one was open for 17% -> 17% of each run, Pallas kernels for 36% -> 39%
where the time goes in v3:
time: 728 us; the launch traced here: 718 us
  Pallas kernels  356 us (49%)
  waiting for transfers between devices  147 us (20%)
  other arithmetic  85.1 us (12%)
  local copies, waits for them, and re-layouts  66.2 us (9%)
  starting transfers between devices  47.8 us (7%)
  between operations  15.9 us (2%)
    pallas_call x36, Pallas kernels, run(): results = call(*values_of(operands), *after, *passed)  354 us
    ppermute x20, waiting for transfers between devices, next_z(): return lax.ppermute(value, 'dp', RING)  52.4 us
    ppermute x14, waiting for transfers between devices, swap_x(): return lax.ppermute(value, 'mp', [(0, 1), (1, 0)])  46 us
    unnamed x111, local copies, waits for them, and re-layouts  40.5 us
    ppermute x10, waiting for transfers between devices, swap_y(): return lax.ppermute(value, 'dp', along(2))  27.8 us
    convert_element_type x6, other arithmetic, join(): return (kept.astype(F32) + received.astype(F32)).astype(kept.dtype)  27.4 us
    ppermute x20, starting transfers between devices, next_z(): return lax.ppermute(value, 'dp', RING)  21.5 us
    ppermute x2, waiting for transfers between devices, sum_rest(): lax.ppermute(value, 'dp', FAR_Z)  17 us
  transfers between devices with their start and end apart: 58, of which 26 were waited for; matrix products, arithmetic and copies ran while one was open for 17% of the time, Pallas kernels for 39%

profile of v3, /device:TPU:0, one launch (start us, length us, event | category | flops | bytes accessed | tf_op | source)
XLA Modules:
  0.0 718.5 jit_solution(16094308253538109632)
XLA Ops:
  48.4 7.1 collective-permute-done.8
  61.4 13.1 %collective-permute-done.5.refs_3_ = bf16[4,64,512]{2,1,0:T(8,128)(2,1)S(1)} collective-permute-done((bf16[4,64,512]{2,1,0:T(8,128)(2,1)S(1)}, bf16[4,64,512]{2,1,0:T(8,128)(2,1)S(1)}, u32[]{:S(2)}, u32[]{:S(2)}) %collective-permute-start.5) | collective-permute-done | bytes 262176 | tf_op jit(solution)/shard_map/ppermute | solution.py:1567
  74.4 14.3 %collective-permute-done.9.refs_4_ = bf16[4,64,1024]{2,1,0:T(8,128)(2,1)S(1)} collective-permute-done((bf16[4,64,1024]{2,1,0:T(8,128)(2,1)}, bf16[4,64,1024]{2,1,0:T(8,128)(2,1)S(1)}, u32[]{:S(2)}, u32[]{:S(2)}) %collective-permute-start.9) | collective-permute-done | bytes 524320 | tf_op jit(solution)/shard_map/ppermute | solution.py:1555
  98.9 6.4 collective-permute-done.10.refs_0_
  132.8 9.1 %collective-permute-done.18 = f32[17,1024]{1,0:T(8,128)S(1)} collective-permute-done((f32[17,1024]{1,0:T(8,128)S(1)}, f32[17,1024]{1,0:T(8,128)S(1)}, u32[]{:S(2)}, u32[]{:S(2)}) %collective-permute-start.18) | collective-permute-done | bytes 69664 | tf_op jit(solution)/shard_map/ppermute | solution.py:1652
  147.4 9.9 %collective-permute-done.21 = bf16[2,64,2048]{2,1,0:T(8,128)(2,1)S(1)} collective-permute-done((bf16[2,64,2048]{2,1,0:T(8,128)(2,1)S(1)}, bf16[2,64,2048]{2,1,0:T(8,128)(2,1)S(1)}, u32[]{:S(2)}, u32[]{:S(2)}) %collective-permute-start.21) | collective-permute-done | bytes 524320 | tf_op jit(solution)/shard_map/ppermute | solution.py:1559
  162.2 13.9 %project_self.1 = (bf16[1024,1024]{1,0:T(8,128)(2,1)}, bf16[1024,1024]{1,0:T(8,128)(2,1)}, bf16[1024,1024]{1,0:T(8,128)(2,1)}, bf16[1024,1024]{1,0:T(8,128)(2,1)}) custom-call(s32[8]{0:T(128)} %get-tuple-element.133.refs_0_.refs_2_, f32[24,1024]{1,0:T(8,128)} %concatenate.55.refs_3_.refs_1_, bf16[1024,1024]{1,0:T(8,128)(2,1)} %maximum_select_fusion.refs_2_.refs_5_, ...), custom_call_target="tpu_custom_call" | custom-call | flops 6400000000 | bytes 16000000 | tf_op jit(solution)/shard_map/project_self/pallas_call | solution.py:536
  176.1 19.6 %attend_self.1 = (bf16[1024,1024]{1,0:T(8,128)(2,1)}, f32[8,1024,128]{2,1,0:T(8,128)}) custom-call(s32[8]{0:T(128)} %get-tuple-element.133.refs_0_.refs_2_, bf16[1024,1024]{1,0:T(8,128)(2,1)} %get-tuple-element.134.refs_1_, bf16[1024,1024]{1,0:T(8,128)(2,1)} %get-tuple-element.135.refs_2_, bf16[1024,1024]{1,0:T(8,128)(2,1)} %get-tuple-element.136.refs_3_), custom_call_target="tpu_custom_call" | custom-call | flops 69000003584 | bytes 1000000 | tf_op jit(solution)/shard_map/attend_self/pallas_call | solution.py:536
  207.4 11.6 %after_self.1 = (f32[1024,1024]{1,0:T(8,128)}, bf16[1024,1024]{1,0:T(8,128)(2,1)}, bf16[1024,1024]{1,0:T(8,128)(2,1)}) custom-call(s32[8]{0:T(128)} %get-tuple-element.140.refs_0_.refs_1_, f32[24,1024]{1,0:T(8,128)} %concatenate.55.refs_3_.refs_1_, bf16[1024,1024]{1,0:T(8,128)(2,1)} %maximum_select_fusion.refs_2_.refs_5_, ...), custom_call_target="tpu_custom_call" | custom-call | flops 4300000256 | bytes 16000000 | tf_op jit(solution)/shard_map/after_self/pallas_call | solution.py:536
  219.1 10.2 %project_memory.1 = (bf16[1024,1024]{1,0:T(8,128)(2,1)}, bf16[1024,1024]{1,0:T(8,128)(2,1)}, bf16[1024,1024]{1,0:T(8,128)(2,1)}) custom-call(s32[8]{0:T(128)} %get-tuple-element.140.refs_0_.refs_1_, f32[24,1024]{1,0:T(8,128)} %concatenate.55.refs_3_.refs_1_, bf16[1024,1024]{1,0:T(8,128)(2,1)} %maximum_select_fusion.1.refs_2_, ...), custom_call_target="tpu_custom_call" | custom-call | flops 4300000256 | bytes 12000000 | tf_op jit(solution)/shard_map/project_memory/pallas_call | solution.py:536
  229.4 24.5 %attend_cross.1 = (bf16[1024,1024]{1,0:T(8,128)(2,1)}, f32[8,1024,128]{2,1,0:T(8,128)}) custom-call(s32[8]{0:T(128)} %get-tuple-element.144.refs_0_.refs_2_, bf16[1024,1024]{1,0:T(8,128)(2,1)} %get-tuple-element.141.refs_4_.refs_1_, bf16[1024,1024]{1,0:T(8,128)(2,1)} %get-tuple-element.142.refs_0_.refs_2_, bf16[1024,1024]{1,0:T(8,128)(2,1)} %get-tuple-element.145.refs_3_), custom_call_target="tpu_custom_call" | custom-call | flops 110399995904 | bytes 1000000 | tf_op jit(solution)/shard_map/attend_cross/pallas_call | solution.py:536
  266.8 12.8 %after_cross.1 = (f32[1024,1024]{1,0:T(8,128)}, bf16[1024,1024]{1,0:T(8,128)(2,1)}, bf16[1024,1024]{1,0:T(8,128)(2,1)}, bf16[1024,1024]{1,0:T(8,128)(2,1)}, bf16...) custom-call(s32[8]{0:T(128)} %get-tuple-element.149.refs_0_.refs_1_, f32[24,1024]{1,0:T(8,128)} %concatenate.55.refs_3_.refs_1_, ...), custom_call_target="tpu_custom_call" | custom-call | flops 2200000000 | bytes 26000000 | tf_op jit(solution)/shard_map/after_cross/pallas_call | solution.py:536
  279.7 73.9 %feedforward.1 = (bf16[512,1024]{1,0:T(8,128)(2,1)}, bf16[512,1024]{1,0:T(8,128)(2,1)}, f32[1024,1024]{1,0:T(8,128)}, bf16[2,2,4,2,64,2048]{5,4,3,2,1,0:T(8,128)...) custom-call(s32[8]{0:T(128)} %get-tuple-element.149.refs_0_.refs_1_, ...), custom_call_target="tpu_custom_call" | custom-call | flops 51499999232 | bytes 60000000 | tf_op jit(solution)/shard_map/feedforward/pallas_call | solution.py:536
  354.7 12.4 %back_three.1 = (f32[1024,1024]{1,0:T(8,128)}, bf16[1024,1024]{1,0:T(8,128)(2,1)}, bf16[1024,1024]{1,0:T(8,128)(2,1)}, f32[8,1024]{1,0:T(8,128)}) custom-call(s32[8]{0:T(128)} %get-tuple-element.149.refs_0_.refs_1_, f32[24,1024]{1,0:T(8,128)} %concatenate.55.refs_3_.refs_1_, f32[1024,1024]{1,0:T(8,128)} %get-tuple-element.159.refs_2_, ...), custom_call_target="tpu_custom_call" | custom-call | flops 2200000000 | bytes 20000000 | tf_op jit(solution)/shard_map/back_three/pallas_call | solution.py:536
  367.3 10.1 %add_convert_fusion = (bf16[1,2,4,2,64,2048]{5,4,3,2,1,0:T(8,128)(2,1)}, bf16[2,4,2,64,2048]{4,3,2,1,0:T(8,128)(2,1)}) fusion(bf16[2,2,4,2,64,2048]{5,4,3,2,1,0:T(8,128)(2,1)} %get-tuple-element.176, bf16[2,2,4,2,64,2048]{5,4,3,2,1,0:T(8,128)(2,1)} %get-tuple-element.175), kind=kLoop, calls=%fused_computation | loop fusion | flops 16777216 | bytes 25165824 | tf_op jit(solution)/shard_map/convert_element_type | solution.py:1657
  378.1 49.2 %attend_back_cross.1 = (bf16[1024,1024]{1,0:T(8,128)(2,1)}, bf16[1024,1024]{1,0:T(8,128)(2,1)}, bf16[1024,1024]{1,0:T(8,128)(2,1)}, f32[8,1024]{1,0:T(8,128)}) custom-call(s32[8]{0:T(128)} %get-tuple-element.162.refs_0_.refs_2_, bf16[1024,1024]{1,0:T(8,128)(2,1)} %get-tuple-element.141.refs_4_.refs_1_, ...), custom_call_target="tpu_custom_call" | custom-call | flops 142599995392 | bytes 1000000 | tf_op jit(solution)/shard_map/attend_back_cross/pallas_call | solution.py:536
  427.3 13.7 %back_two.1 = (f32[1024,1024]{1,0:T(8,128)}, bf16[1024,1024]{1,0:T(8,128)(2,1)}, bf16[1024,1024]{1,0:T(8,128)(2,1)}, f32[8,1024]{1,0:T(8,128)}) custom-call(s32[8]{0:T(128)} %get-tuple-element.162.refs_0_.refs_2_, f32[24,1024]{1,0:T(8,128)} %concatenate.55.refs_3_.refs_1_, bf16[1024,1024]{1,0:T(8,128)(2,1)} %get-tuple-element.167.refs_2_.refs_7_, ...), custom_call_target="tpu_custom_call" | custom-call | flops 4300000256 | bytes 24000000 | tf_op jit(solution)/shard_map/back_two/pallas_call | solution.py:536
  441.0 23.0 %weight_grad_cross.1 = (bf16[2,2,4,64,2560]{4,3,2,1,0:T(8,128)(2,1)}, bf16[2,2,4,64,2560]{4,3,2,1,0:T(8,128)(2,1)}) custom-call(s32[8]{0:T(128)} %get-tuple-element.162.refs_0_.refs_2_, bf16[1024,1024]{1,0:T(8,128)(2,1)} %get-tuple-element.163.refs_1_, bf16[1024,1024]{1,0:T(8,128)(2,1)} %get-tuple-element.164.refs_2_, ...), custom_call_target="tpu_custom_call" | custom-call | flops 51499999232 | bytes 1000000 | tf_op jit(solution)/shard_map/weight_grad_cross/pallas_call | solution.py:536
  464.0 6.5 collective-permute-done.30.refs_4_
  481.6 10.6 %memory_back.1 = (bf16[512,1024]{1,0:T(8,128)(2,1)}, bf16[512,1024]{1,0:T(8,128)(2,1)}) custom-call(s32[8]{0:T(128)} %get-tuple-element.177.refs_0_.refs_1_, bf16[1024,1024]{1,0:T(8,128)(2,1)} %get-tuple-element.170.refs_5_.refs_1_, bf16[1024,1024]{1,0:T(8,128)(2,1)} %get-tuple-element.171.refs_6_.refs_2_, bf16[32,64,4608]{2,1,0:T(8,128)(2,1)} %bitcast.188), custom_call_target="tpu_custom_call" | custom-call | flops 4300000256 | bytes 12000000 | tf_op jit(solution)/shard_map/memory_back/pallas_call | solution.py:536
  499.2 18.8 %attend_back_self.3 = (bf16[1024,1024]{1,0:T(8,128)(2,1)}, bf16[1024,1024]{1,0:T(8,128)(2,1)}, bf16[1024,1024]{1,0:T(8,128)(2,1)}, f32[8,1024]{1,0:T(8,128)}) custom-call(s32[8]{0:T(128)} %get-tuple-element.180.refs_0_.refs_1_, bf16[1024,1024]{1,0:T(8,128)(2,1)} %get-tuple-element.134.refs_1_, bf16[1024,1024]{1,0:T(8,128)(2,1)} %get-tuple-element.135.refs_2_, ...), custom_call_target="tpu_custom_call" | custom-call | flops 44562501632 | bytes 1000000 | tf_op jit(solution)/shard_map/attend_back_self/pallas_call | solution.py:536
  517.9 10.4 %collective-permute-done.32.refs_2_ = bf16[4,2,64,2048]{3,2,1,0:T(8,128)(2,1)} collective-permute-done((bf16[4,2,64,2048]{3,2,1,0:T(8,128)(2,1)}, bf16[4,2,64,2048]{3,2,1,0:T(8,128)(2,1)}, u32[]{:S(2)}, u32[]{:S(2)}) %collective-permute-start.32) | collective-permute-done | bytes 2097184 | tf_op jit(solution)/shard_map/ppermute | solution.py:1555
  531.0 8.3 %weight_grad_self_1.1 = (bf16[2,4,64,1536]{3,2,1,0:T(8,128)(2,1)}, bf16[2,4,64,1536]{3,2,1,0:T(8,128)(2,1)}) custom-call(s32[8]{0:T(128)} %get-tuple-element.185.refs_0_.refs_1_, bf16[1024,1024]{1,0:T(8,128)(2,1)} %get-tuple-element.186.refs_1_, bf16[1024,1024]{1,0:T(8,128)(2,1)} %get-tuple-element.182.refs_0_.refs_2_.refs_7_, ...), custom_call_target="tpu_custom_call" | custom-call | flops 10000000000 | bytes 1000000 | tf_op jit(solution)/shard_map/weight_grad_self_1/pallas_call | solution.py:536
  547.7 11.0 %attend_back_self.4 = (bf16[1024,1024]{1,0:T(8,128)(2,1)}, bf16[1024,1024]{1,0:T(8,128)(2,1)}, bf16[1024,1024]{1,0:T(8,128)(2,1)}, f32[8,1024]{1,0:T(8,128)}) custom-call(s32[8]{0:T(128)} %get-tuple-element.192.refs_0_.refs_2_, ...), custom_call_target="tpu_custom_call", output_to_operand_aliasing={{0}: (7, {}), {1}: (8, {}), {2}: (9, {}), {3}: (10, {})} | custom-call | flops 22281250816 | bytes 1000000 | tf_op jit(solution)/shard_map/attend_back_self/pallas_call | solution.py:536
  578.4 10.8 %attend_back_self.5 = (bf16[1024,1024]{1,0:T(8,128)(2,1)}, bf16[1024,1024]{1,0:T(8,128)(2,1)}, bf16[1024,1024]{1,0:T(8,128)(2,1)}, f32[8,1024]{1,0:T(8,128)}) custom-call(s32[8]{0:T(128)} %get-tuple-element.199.refs_0_.refs_2_, ...), custom_call_target="tpu_custom_call", output_to_operand_aliasing={{0}: (7, {}), {1}: (8, {}), {2}: (9, {}), {3}: (10, {})} | custom-call | flops 22281250816 | bytes 1000000 | tf_op jit(solution)/shard_map/attend_back_self/pallas_call | solution.py:536
  594.9 8.1 %weight_grad_self_0.1 = (bf16[2,4,64,1536]{3,2,1,0:T(8,128)(2,1)}, bf16[2,4,64,1536]{3,2,1,0:T(8,128)(2,1)}) custom-call(s32[8]{0:T(128)} %get-tuple-element.206.refs_0_.refs_1_, bf16[1024,1024]{1,0:T(8,128)(2,1)} %get-tuple-element.186.refs_1_, bf16[1024,1024]{1,0:T(8,128)(2,1)} %get-tuple-element.207.refs_2_, ...), custom_call_target="tpu_custom_call" | custom-call | flops 10000000000 | bytes 1000000 | tf_op jit(solution)/shard_map/weight_grad_self_0/pallas_call | solution.py:536
  615.4 11.0 %back_one.2 = (bf16[512,1024]{1,0:T(8,128)(2,1)}, f32[8,1024]{1,0:T(8,128)}) custom-call(s32[8]{0:T(128)} %get-tuple-element.213.refs_0_, f32[24,1024]{1,0:T(8,128)} %concatenate.55.refs_3_.refs_1_, bf16[1024,1024]{1,0:T(8,128)(2,1)} %get-tuple-element.207.refs_2_, bf16[1024,1024]{1,0:T(8,128)(2,1)} %get-tuple-element.208.refs_3_, ...), custom_call_target="tpu_custom_call" | custom-call | flops 6400000000 | bytes 20000000 | tf_op jit(solution)/shard_map/back_one/pallas_call | solution.py:536
  626.4 6.8 collective-permute-done.43.refs_4_
  639.9 11.0 %back_one.3 = (bf16[512,1024]{1,0:T(8,128)(2,1)}, f32[8,1024]{1,0:T(8,128)}) custom-call(s32[8]{0:T(128)} %get-tuple-element.219.refs_0_, f32[24,1024]{1,0:T(8,128)} %concatenate.55.refs_3_.refs_1_, bf16[1024,1024]{1,0:T(8,128)(2,1)} %get-tuple-element.207.refs_2_, bf16[1024,1024]{1,0:T(8,128)(2,1)} %get-tuple-element.208.refs_3_, ...), custom_call_target="tpu_custom_call" | custom-call | flops 6400000000 | bytes 20000000 | tf_op jit(solution)/shard_map/back_one/pallas_call | solution.py:536
  655.0 6.8 collective-permute-done.44.refs_0_
  685.5 7.9 %collective-permute-done.53 = f32[24,1024]{1,0:T(8,128)S(1)} collective-permute-done((f32[24,1024]{1,0:T(8,128)S(1)}, f32[24,1024]{1,0:T(8,128)S(1)}, u32[]{:S(2)}, u32[]{:S(2)}) %collective-permute-start.53) | collective-permute-done | bytes 98336 | tf_op jit(solution)/shard_map/ppermute | solution.py:1652
  702.6 6.4 collective-permute-done.49
  (323 shorter events, 233.3 us)
Async XLA Ops:
  7.2 200.2 %all-gather.3.cloned.1.call-start = ((), (), s32[]{:S(2)}) async-start(), calls=%async_computation | async-start | bytes 19464192 | tf_op jit(solution)/shard_map/all_gather | solution.py:1815
  16.9 18.8 %collective-permute-start.3 = (f32[17,1024]{1,0:T(8,128)S(1)}, f32[17,1024]{1,0:T(8,128)S(1)}, u32[]{:S(2)}, u32[]{:S(2)}) collective-permute-start(f32[17,1024]{1,0:T(8,128)S(1)} %pad_maximum_fusion.9), channel_id=1, source_target_pairs={{0,1},{1,0},{2,3},{3,2},{4,5},{5,4},{6,7},{7,6},{8,9},{9,8},{10,11... | collective-permute-start | bytes 208904 | tf_op jit(solution)/shard_map/ppermute | solution.py:1555
  36.4 52.3 %collective-permute-start.4 = (bf16[512,1024]{1,0:T(8,128)(2,1)}, bf16[512,1024]{1,0:T(8,128)(2,1)}, u32[]{:S(2)}, u32[]{:S(2)}) collective-permute-start(bf16[512,1024]{1,0:T(8,128)(2,1)} %get-tuple-element.124), channel_id=1, source_target_pairs={{0,1},{1,0},{2,3},{3,2},{4,5},{5,4},{6,7},{7,6},{8,9},{9,8},{10,11... | collective-permute-start | bytes 3145736 | tf_op jit(solution)/shard_map/ppermute | solution.py:1555
  38.0 20.5 %collective-permute-start.2 = (bf16[4,64,512]{2,1,0:T(8,128)(2,1)S(1)}, bf16[4,64,512]{2,1,0:T(8,128)(2,1)S(1)}, u32[]{:S(2)}, u32[]{:S(2)}) collective-permute-start(bf16[4,64,512]{2,1,0:T(8,128)(2,1)S(1)} %pad_maximum_fusion.6.refs_8_.refs_12_), channel_id=1, source_target_pairs={{0,8},{2,10},{4,12},{6,14},{8,16},{10,18},{12,20},{14,22},{16,24},... | collective-permute-start | bytes 786440 | tf_op jit(solution)/shard_map/ppermute | solution.py:1567
  56.3 32.4 %collective-permute-start.9 = (bf16[4,64,1024]{2,1,0:T(8,128)(2,1)}, bf16[4,64,1024]{2,1,0:T(8,128)(2,1)S(1)}, u32[]{:S(2)}, u32[]{:S(2)}) collective-permute-start(bf16[4,64,1024]{2,1,0:T(8,128)(2,1)} %pad_maximum_fusion.2.refs_3_.refs_7_), channel_id=1, source_target_pairs={{0,1},{1,0},{2,3},{3,2},{4,5},{5,4},{6,7},{7,6},{8,9},{9,8},{10,11... | collective-permute-start | bytes 1572872 | tf_op jit(solution)/shard_map/ppermute | solution.py:1555
  59.2 36.8 %collective-permute-start.14 = (bf16[4,64,1024]{2,1,0:T(8,128)(2,1)}, bf16[4,64,1024]{2,1,0:T(8,128)(2,1)}, u32[]{:S(2)}, u32[]{:S(2)}) collective-permute-start(bf16[4,64,1024]{2,1,0:T(8,128)(2,1)} %pad_maximum_fusion.2.refs_3_.refs_7_), channel_id=1, source_target_pairs={{0,4},{2,6},{4,0},{6,2},{8,12},{10,14},{12,8},{14,10},{16,20},{18,... | collective-permute-start | bytes 1572872 | tf_op jit(solution)/shard_map/ppermute | solution.py:1559
  108.6 49.7 %collective-permute-start.15 = (bf16[16,64,1024]{2,1,0:T(8,128)(2,1)}, bf16[16,64,1024]{2,1,0:T(8,128)(2,1)}, u32[]{:S(2)}, u32[]{:S(2)}) collective-permute-start(bf16[16,64,1024]{2,1,0:T(8,128)(2,1)} %constant_dynamic-update-slice_fusion.6), channel_id=1, source_target_pairs={{0,2},{2,0},{4,6},{6,4},{8,10},{10,8},{12,14},{14,12},{16,18},{18,... | collective-permute-start | bytes 6291464 | tf_op jit(solution)/shard_map/ppermute | solution.py:1563
  123.1 18.8 %collective-permute-start.18 = (f32[17,1024]{1,0:T(8,128)S(1)}, f32[17,1024]{1,0:T(8,128)S(1)}, u32[]{:S(2)}, u32[]{:S(2)}) collective-permute-start(f32[17,1024]{1,0:T(8,128)S(1)} %add.273), channel_id=1, source_target_pairs={{0,16},{2,18},{4,20},{6,22},{8,24},{10,26},{12,28},{14,30},{16,0},... | collective-permute-start | bytes 208904 | tf_op jit(solution)/shard_map/ppermute | solution.py:1652
  125.3 33.0 %collective-permute-start.13 = (bf16[16,64,512]{2,1,0:T(8,128)(2,1)}, bf16[16,64,512]{2,1,0:T(8,128)(2,1)}, u32[]{:S(2)}, u32[]{:S(2)}) collective-permute-start(bf16[16,64,512]{2,1,0:T(8,128)(2,1)} %constant_dynamic-update-slice_fusion), channel_id=1, source_target_pairs={{0,2},{2,0},{4,6},{6,4},{8,10},{10,8},{12,14},{14,12},{16,18},{18,... | collective-permute-start | bytes 3145736 | tf_op jit(solution)/shard_map/ppermute | solution.py:1563
  132.8 24.5 %collective-permute-start.21 = (bf16[2,64,2048]{2,1,0:T(8,128)(2,1)S(1)}, bf16[2,64,2048]{2,1,0:T(8,128)(2,1)S(1)}, u32[]{:S(2)}, u32[]{:S(2)}) collective-permute-start(bf16[2,64,2048]{2,1,0:T(8,128)(2,1)S(1)} %copy-done.10), channel_id=1, source_target_pairs={{0,4},{2,6},{4,0},{6,2},{8,12},{10,14},{12,8},{14,10},{16,20},{18,... | collective-permute-start | bytes 1572872 | tf_op jit(solution)/shard_map/ppermute | solution.py:1559
  159.0 36.6 %collective-permute-start.22 = (bf16[512,1024]{1,0:T(8,128)(2,1)}, bf16[512,1024]{1,0:T(8,128)(2,1)S(1)}, u32[]{:S(2)}, u32[]{:S(2)}) collective-permute-start(bf16[512,1024]{1,0:T(8,128)(2,1)} %get-tuple-element.138), channel_id=1, source_target_pairs={{0,1},{1,0},{2,3},{3,2},{4,5},{5,4},{6,7},{7,6},{8,9},{9,8},{10,11... | collective-permute-start | bytes 3145736 | tf_op jit(solution)/shard_map/ppermute | solution.py:1555
  160.3 40.8 %collective-permute-start.23 = (bf16[4,64,2048]{2,1,0:T(8,128)(2,1)}, bf16[4,64,2048]{2,1,0:T(8,128)(2,1)S(1)}, u32[]{:S(2)}, u32[]{:S(2)}) collective-permute-start(bf16[4,64,2048]{2,1,0:T(8,128)(2,1)} %get-tuple-element.139.refs_9_), channel_id=1, source_target_pairs={{0,8},{2,10},{4,12},{6,14},{8,16},{10,18},{12,20},{14,22},{16,24},... | collective-permute-start | bytes 3145736 | tf_op jit(solution)/shard_map/ppermute | solution.py:1567
  202.1 27.2 %collective-permute-start.24 = (bf16[4,64,2048]{2,1,0:T(8,128)(2,1)}, bf16[4,64,2048]{2,1,0:T(8,128)(2,1)}, u32[]{:S(2)}, u32[]{:S(2)}) collective-permute-start(bf16[4,64,2048]{2,1,0:T(8,128)(2,1)} %get-tuple-element.143.refs_10_), channel_id=1, source_target_pairs={{0,8},{2,10},{4,12},{6,14},{8,16},{10,18},{12,20},{14,22},{16,24},... | collective-permute-start | bytes 3145736 | tf_op jit(solution)/shard_map/ppermute | solution.py:1567
  202.1 51.9 %collective-permute-start.25 = (bf16[512,1024]{1,0:T(8,128)(2,1)}, bf16[512,1024]{1,0:T(8,128)(2,1)S(1)}, u32[]{:S(2)}, u32[]{:S(2)}) collective-permute-start(bf16[512,1024]{1,0:T(8,128)(2,1)} %get-tuple-element.147), channel_id=1, source_target_pairs={{0,1},{1,0},{2,3},{3,2},{4,5},{5,4},{6,7},{7,6},{8,9},{9,8},{10,11... | collective-permute-start | bytes 3145736 | tf_op jit(solution)/shard_map/ppermute | solution.py:1555
  229.3 25.9 %collective-permute-start.26 = (bf16[4,64,2048]{2,1,0:T(8,128)(2,1)}, bf16[4,64,2048]{2,1,0:T(8,128)(2,1)S(1)}, u32[]{:S(2)}, u32[]{:S(2)}) collective-permute-start(bf16[4,64,2048]{2,1,0:T(8,128)(2,1)} %get-tuple-element.148.refs_11_), channel_id=1, source_target_pairs={{0,8},{2,10},{4,12},{6,14},{8,16},{10,18},{12,20},{14,22},{16,24},... | collective-permute-start | bytes 3145736 | tf_op jit(solution)/shard_map/ppermute | solution.py:1567
  261.2 18.5 %collective-permute-start.27 = (bf16[16,64,2048]{2,1,0:T(8,128)(2,1)}, bf16[16,64,2048]{2,1,0:T(8,128)(2,1)}, u32[]{:S(2)}, u32[]{:S(2)}) collective-permute-start(bf16[16,64,2048]{2,1,0:T(8,128)(2,1)} %pad_maximum_fusion), channel_id=1, source_target_pairs={{0,2},{2,0},{4,6},{6,4},{8,10},{10,8},{12,14},{14,12},{16,18},{18,... | collective-permute-start | bytes 12582920 | tf_op jit(solution)/shard_map/ppermute | solution.py:1563
  354.2 109.8 %collective-permute-start.28 = (bf16[512,1024]{1,0:T(8,128)(2,1)}, bf16[512,1024]{1,0:T(8,128)(2,1)}, u32[]{:S(2)}, u32[]{:S(2)}) collective-permute-start(bf16[512,1024]{1,0:T(8,128)(2,1)} %get-tuple-element.158), channel_id=1, source_target_pairs={{0,1},{1,0},{2,3},{3,2},{4,5},{5,4},{6,7},{7,6},{8,9},{9,8},{10,11... | collective-permute-start | bytes 3145736 | tf_op jit(solution)/shard_map/ppermute | solution.py:1555
  377.4 93.2 %collective-permute-start.30 = (bf16[2,4,2,64,2048]{4,3,2,1,0:T(8,128)(2,1)}, bf16[2,4,2,64,2048]{4,3,2,1,0:T(8,128)(2,1)}, u32[]{:S(2)}, u32[]{:S(2)}) collective-permute-start(bf16[2,4,2,64,2048]{4,3,2,1,0:T(8,128)(2,1)} %get-tuple-element.262), channel_id=1, source_target_pairs={{0,4},{2,6},{4,0},{6,2},{8,12},{10,14},{12,8},{14,10},{16,20},{18,... | collective-permute-start | bytes 12582920 | tf_op jit(solution)/shard_map/ppermute | solution.py:1559
  470.6 21.6 %collective-permute-start.31 = (bf16[2,2,4,64,2560]{4,3,2,1,0:T(8,128)(2,1)}, bf16[2,2,4,64,2560]{4,3,2,1,0:T(8,128)(2,1)}, u32[]{:S(2)}, u32[]{:S(2)}) collective-permute-start(bf16[2,2,4,64,2560]{4,3,2,1,0:T(8,128)(2,1)} %get-tuple-element.179), channel_id=1, source_target_pairs={{0,2},{2,0},{4,6},{6,4},{8,10},{10,8},{12,14},{14,12},{16,18},{18,... | collective-permute-start | bytes 15728648 | tf_op jit(solution)/shard_map/ppermute | solution.py:1563
  480.9 47.4 %collective-permute-start.32 = (bf16[4,2,64,2048]{3,2,1,0:T(8,128)(2,1)}, bf16[4,2,64,2048]{3,2,1,0:T(8,128)(2,1)}, u32[]{:S(2)}, u32[]{:S(2)}) collective-permute-start(bf16[4,2,64,2048]{3,2,1,0:T(8,128)(2,1)} %fusion.4), channel_id=1, source_target_pairs={{0,1},{1,0},{2,3},{3,2},{4,5},{5,4},{6,7},{7,6},{8,9},{9,8},{10,11... | collective-permute-start | bytes 6291464 | tf_op jit(solution)/shard_map/ppermute | solution.py:1555
  498.5 67.5 %collective-permute-start.36 = (bf16[2,4,64,2560]{3,2,1,0:T(8,128)(2,1)}, bf16[2,4,64,2560]{3,2,1,0:T(8,128)(2,1)S(1)}, u32[]{:S(2)}, u32[]{:S(2)}) collective-permute-start(bf16[2,4,64,2560]{3,2,1,0:T(8,128)(2,1)} %get-tuple-element.264), channel_id=1, source_target_pairs={{0,4},{2,6},{4,0},{6,2},{8,12},{10,14},{12,8},{14,10},{16,20},{18,... | collective-permute-start | bytes 7864328 | tf_op jit(solution)/shard_map/ppermute | solution.py:1559
  530.6 28.1 %collective-permute-start.34 = (bf16[512,1024]{1,0:T(8,128)(2,1)}, bf16[512,1024]{1,0:T(8,128)(2,1)}, u32[]{:S(2)}, u32[]{:S(2)}) collective-permute-start(bf16[512,1024]{1,0:T(8,128)(2,1)} %get-tuple-element.195), channel_id=1, source_target_pairs={{0,1},{1,0},{2,3},{3,2},{4,5},{5,4},{6,7},{7,6},{8,9},{9,8},{10,11... | collective-permute-start | bytes 3145736 | tf_op jit(solution)/shard_map/ppermute | solution.py:1555
  547.7 18.3 %collective-permute-start.37 = (bf16[2,64,2048]{2,1,0:T(8,128)(2,1)}, bf16[2,64,2048]{2,1,0:T(8,128)(2,1)}, u32[]{:S(2)}, u32[]{:S(2)}) collective-permute-start(bf16[2,64,2048]{2,1,0:T(8,128)(2,1)} %fusion.13), channel_id=1, source_target_pairs={{0,8},{2,10},{4,12},{6,14},{8,16},{10,18},{12,20},{14,22},{16,24},... | collective-permute-start | bytes 1572872 | tf_op jit(solution)/shard_map/ppermute | solution.py:1567
  570.3 18.9 %collective-permute-start.38 = (bf16[2,64,2048]{2,1,0:T(8,128)(2,1)}, bf16[2,64,2048]{2,1,0:T(8,128)(2,1)}, u32[]{:S(2)}, u32[]{:S(2)}) collective-permute-start(bf16[2,64,2048]{2,1,0:T(8,128)(2,1)} %fusion.11), channel_id=1, source_target_pairs={{0,8},{2,10},{4,12},{6,14},{8,16},{10,18},{12,20},{14,22},{16,24},... | collective-permute-start | bytes 1572872 | tf_op jit(solution)/shard_map/ppermute | solution.py:1567
  574.9 20.0 %collective-permute-start.39 = (bf16[4,64,1536]{2,1,0:T(8,128)(2,1)}, bf16[4,64,1536]{2,1,0:T(8,128)(2,1)}, u32[]{:S(2)}, u32[]{:S(2)}) collective-permute-start(bf16[4,64,1536]{2,1,0:T(8,128)(2,1)} %fusion.15), channel_id=1, source_target_pairs={{0,4},{2,6},{4,0},{6,2},{8,12},{10,14},{12,8},{14,10},{16,20},{18,... | collective-permute-start | bytes 2359304 | tf_op jit(solution)/shard_map/ppermute | solution.py:1559
  578.1 30.8 %collective-permute-start.40 = (bf16[4,64,2560]{2,1,0:T(8,128)(2,1)}, bf16[4,64,2560]{2,1,0:T(8,128)(2,1)S(1)}, u32[]{:S(2)}, u32[]{:S(2)}) collective-permute-start(bf16[4,64,2560]{2,1,0:T(8,128)(2,1)} %fusion.8), channel_id=1, source_target_pairs={{0,1},{1,0},{2,3},{3,2},{4,5},{5,4},{6,7},{7,6},{8,9},{9,8},{10,11... | collective-permute-start | bytes 3932168 | tf_op jit(solution)/shard_map/ppermute | solution.py:1555
  610.1 23.1 %collective-permute-start.41 = (bf16[2,4,64,1536]{3,2,1,0:T(8,128)(2,1)}, bf16[2,4,64,1536]{3,2,1,0:T(8,128)(2,1)}, u32[]{:S(2)}, u32[]{:S(2)}) collective-permute-start(bf16[2,4,64,1536]{3,2,1,0:T(8,128)(2,1)} %get-tuple-element.214), channel_id=1, source_target_pairs={{0,2},{2,0},{4,6},{6,4},{8,10},{10,8},{12,14},{14,12},{16,18},{18,... | collective-permute-start | bytes 4718600 | tf_op jit(solution)/shard_map/ppermute | solution.py:1563
  613.0 20.2 %collective-permute-start.43 = (bf16[4,64,1536]{2,1,0:T(8,128)(2,1)}, bf16[4,64,1536]{2,1,0:T(8,128)(2,1)}, u32[]{:S(2)}, u32[]{:S(2)}) collective-permute-start(bf16[4,64,1536]{2,1,0:T(8,128)(2,1)} %fusion.7), channel_id=1, source_target_pairs={{0,1},{1,0},{2,3},{3,2},{4,5},{5,4},{6,7},{7,6},{8,9},{9,8},{10,11... | collective-permute-start | bytes 2359304 | tf_op jit(solution)/shard_map/ppermute | solution.py:1555
  635.6 19.4 %collective-permute-start.45 = (bf16[4,64,1536]{2,1,0:T(8,128)(2,1)}, bf16[4,64,1536]{2,1,0:T(8,128)(2,1)}, u32[]{:S(2)}, u32[]{:S(2)}) collective-permute-start(bf16[4,64,1536]{2,1,0:T(8,128)(2,1)} %fusion.16), channel_id=1, source_target_pairs={{0,4},{2,6},{4,0},{6,2},{8,12},{10,14},{12,8},{14,10},{16,20},{18,... | collective-permute-start | bytes 2359304 | tf_op jit(solution)/shard_map/ppermute | solution.py:1559
  637.1 24.7 %collective-permute-start.44 = (bf16[512,1024]{1,0:T(8,128)(2,1)}, bf16[512,1024]{1,0:T(8,128)(2,1)}, u32[]{:S(2)}, u32[]{:S(2)}) collective-permute-start(bf16[512,1024]{1,0:T(8,128)(2,1)} %get-tuple-element.221), channel_id=1, source_target_pairs={{0,1},{1,0},{2,3},{3,2},{4,5},{5,4},{6,7},{7,6},{8,9},{9,8},{10,11... | collective-permute-start | bytes 3145736 | tf_op jit(solution)/shard_map/ppermute | solution.py:1555
  664.9 28.8 %collective-permute-start.50 = (bf16[64,2560]{1,0:T(8,128)(2,1)S(1)}, bf16[64,2560]{1,0:T(8,128)(2,1)S(1)}, u32[]{:S(2)}, u32[]{:S(2)}) collective-permute-start(bf16[64,2560]{1,0:T(8,128)(2,1)S(1)} %fusion.18), channel_id=1, source_target_pairs={{0,8},{2,10},{4,12},{6,14},{8,16},{10,18},{12,20},{14,22},{16,24},... | collective-permute-start | bytes 983048 | tf_op jit(solution)/shard_map/ppermute | solution.py:1567
  680.3 19.5 %collective-permute-start.48 = (bf16[64,1536]{1,0:T(8,128)(2,1)S(1)}, bf16[64,1536]{1,0:T(8,128)(2,1)}, u32[]{:S(2)}, u32[]{:S(2)}) collective-permute-start(bf16[64,1536]{1,0:T(8,128)(2,1)S(1)} %fusion.25), channel_id=1, source_target_pairs={{0,8},{2,10},{4,12},{6,14},{8,16},{10,18},{12,20},{14,22},{16,24},... | collective-permute-start | bytes 589832 | tf_op jit(solution)/shard_map/ppermute | solution.py:1567
  (71 other events, 602.3 us)
Sparse Core Ops, SparseCore 0:
  15.3 178.7 all-gather.2

commit v4 on v3

--- a/solution.py
+++ b/solution.py
@@ -943,7 +943,7 @@
 
 
         total = total + mm_nt(o_ref[:, slab * 512 : slab * 512 + 512], wo[slab])
-    h_ref[...] = total
+    h_ref[...] = total.astype(BF)
     unit, _ = ln_parts(total)
     normed = (unit * par[1:2, :] + par[4:5, :]).astype(BF)
     nt_ref[...] = transposed(normed)
@@ -970,7 +970,7 @@
             scratch_shapes=[VM((2, 1024, 512), BF)] * 2 + [pltpu.SemaphoreType.DMA((2, 2))],
         ),
         out_shape=[
-            jax.ShapeDtypeStruct((n, 1024), F32),
+            jax.ShapeDtypeStruct((n, 1024), BF),
             jax.ShapeDtypeStruct((n, 1024), BF),
             jax.ShapeDtypeStruct((1024, n), BF),
         ],
@@ -1005,12 +1005,12 @@
         gsum_ref[...] = jnp.zeros(gsum_ref.shape, F32)
 
     gsum_ref[0:1, :] += sums
-    total = h_in[...] + par[7:8, :]
+    total = h_in[...].astype(F32) + par[7:8, :]
     for slab in range(2):
 
 
         total = total + mm_nt(o_ref[:, slab * 512 : slab * 512 + 512], wo[slab])
-    h_ref[...] = total
+    h_ref[...] = total.astype(BF)
     unit, _ = ln_parts(total)
     normed = (unit * par[2:3, :] + par[5:6, :]).astype(BF)
     n_ref[...] = normed
@@ -1041,7 +1041,7 @@
             scratch_shapes=[VM((2, 1024, 512), BF), pltpu.SemaphoreType.DMA((2,))],
         ),
         out_shape=[
-            jax.ShapeDtypeStruct((n, 1024), F32),
+            jax.ShapeDtypeStruct((n, 1024), BF),
             act,
             act_t,
             act,
@@ -1079,7 +1079,7 @@
 
 def ffn_kernel(info, par, bias_ref, n_ref, nt_ref, g_ref, gt_ref, h_ref, *rest):
     pieces, rest = rest[:6], rest[6:]
-    (out_ref, other_ref, dn_ref, send_ref, keep_ref, dbias_ref, w_in, w_out, acc, active, du, temp, sems) = rest
+    (out_ref, other_ref, dn_ref, send_ref, keep_ref, dbias_ref, w_in, w_out, acc, dn_acc, active, du, temp, sems) = rest
     half, part = pl.program_id(0), pl.program_id(1)
     parts = pl.num_programs(1)
     n = n_ref.shape[0]
@@ -1091,7 +1091,7 @@
         start_all(pieces[:1], 2048, 2048, w_in, sems.at[0])
         start_weight(info, pieces[1:], "xyz", 0, 2048, w_out, sems.at[1])
         acc[...] = jnp.zeros(acc.shape, F32)
-        dn_ref[...] = jnp.zeros(dn_ref.shape, F32)
+        dn_acc[...] = jnp.zeros(dn_acc.shape, F32)
 
     @pl.when(part == 0)
     def _():
@@ -1123,7 +1123,7 @@
         sums = row_sum(d.astype(F32))
         total_bias = sums if total_bias is None else total_bias + sums
         acc[rows, :] += mm_nt(r, second[...])
-        dn_ref[rows, :] += mm_nt(d, first[...])
+        dn_acc[rows, :] += mm_nt(d, first[...])
 
     dbias_ref[0:1, :] = total_bias
     for zrel in range(4):
@@ -1140,10 +1140,11 @@
 
     @pl.when((half == 1) & (part == parts - 1))
     def _():
+        dn_ref[...] = dn_acc[...].astype(BF)
         for chunk in range(n // ROWS):
             start = lax.rem(info[3] * (n // 2) + chunk * ROWS, n)
             rows = pl.ds(pl.multiple_of(start, ROWS), ROWS)
-            value = h_ref[rows, :] + acc[rows, :] + par[8:9, :]
+            value = h_ref[rows, :].astype(F32) + acc[rows, :] + par[8:9, :]
             target = out_ref if chunk * ROWS < n // 2 else other_ref
             at = chunk * ROWS % (n // 2)
             target[at : at + ROWS, :] = value.astype(BF)
@@ -1183,6 +1184,7 @@
                 VM((2, 1024, 2048), BF),
                 VM((2, 1024, 2048), BF),
                 VM((n, 1024), F32),
+                VM((n, 1024), F32),
                 VM((n, FFB), BF),
                 VM((n, FFB), BF),
                 VM((2, 256, FFB), BF),
@@ -1192,7 +1194,7 @@
         out_shape=[
             jax.ShapeDtypeStruct((n // 2, 1024), BF),
             jax.ShapeDtypeStruct((n // 2, 1024), BF),
-            jax.ShapeDtypeStruct((n, 1024), F32),
+            jax.ShapeDtypeStruct((n, 1024), BF),
             jax.ShapeDtypeStruct((2, 2, 4, 2, 64, 2048), BF),
             jax.ShapeDtypeStruct((2, 2, 4, 2, 64, 2048), BF),
             jax.ShapeDtypeStruct((8, 4096), F32),
@@ -1216,13 +1218,13 @@
         for slab in range(2):
             wait_weight(wo, sems, slab)
 
-    back_rows(par, 2, dn_ref[...], h_ref[...], g_ref[...].astype(F32), dh_ref, gt_ref, sum_ref, do_ref, wo, sems)
+    back_rows(par, 2, dn_ref[...].astype(F32), h_ref[...].astype(F32), g_ref[...].astype(F32), dh_ref, gt_ref, sum_ref, do_ref, wo, sems)
 
 
 def back_rows(par, index, dn, hidden, residual, dh_ref, gt_ref, sum_ref, do_ref, wo, sems):
     unit, inverse = ln_parts(hidden)
     grad = residual + ln_back(dn, par[index : index + 1, :], unit, inverse)
-    dh_ref[...] = grad
+    dh_ref[...] = grad.astype(BF)
     sum_ref[0:1, :] += row_sum(dn * unit)
     sum_ref[1:2, :] += row_sum(dn)
     sum_ref[2:3, :] += row_sum(grad)
@@ -1254,7 +1256,7 @@
             scratch_shapes=[VM((2, 1024, 512), BF), pltpu.SemaphoreType.DMA((2,))],
         ),
         out_shape=[
-            jax.ShapeDtypeStruct((n, 1024), F32),
+            jax.ShapeDtypeStruct((n, 1024), BF),
             jax.ShapeDtypeStruct((n, 1024), BF),
             jax.ShapeDtypeStruct((1024, n), BF),
             jax.ShapeDtypeStruct((8, 1024), F32),
@@ -1287,7 +1289,7 @@
 
         term = mm_nt(dq_ref[:, slab * 512 : slab * 512 + 512], wq[slab])
         dn = term if dn is None else dn + term
-    back_rows(par, 1, dn, h_ref[...], dh2_ref[...], dh_ref, gt_ref, sum_ref, do_ref, wo, sems.at[1])
+    back_rows(par, 1, dn, h_ref[...].astype(F32), dh2_ref[...].astype(F32), dh_ref, gt_ref, sum_ref, do_ref, wo, sems.at[1])
 
 
 def call_back_two(info, par, dq, h, dh2, pieces, after=(), through=()):
@@ -1310,7 +1312,7 @@
             scratch_shapes=[VM((2, 1024, 512), BF)] * 2 + [pltpu.SemaphoreType.DMA((2, 2))],
         ),
         out_shape=[
-            jax.ShapeDtypeStruct((n, 1024), F32),
+            jax.ShapeDtypeStruct((n, 1024), BF),
             jax.ShapeDtypeStruct((n, 1024), BF),
             jax.ShapeDtypeStruct((1024, n), BF),
             jax.ShapeDtypeStruct((8, 1024), F32),
@@ -1400,7 +1402,7 @@
             term = mm_nt(ref[:, slab * 512 : slab * 512 + 512], weights[t][slab])
             dn = term if dn is None else dn + term
     unit, inverse = ln_parts(x_ref[...].astype(F32))
-    grad = dh1_ref[...] + ln_back(dn, par[0:1, :], unit, inverse)
+    grad = dh1_ref[...].astype(F32) + ln_back(dn, par[0:1, :], unit, inverse)
     out_ref[...] = grad.astype(BF)
     sum_ref[0:1, :] += row_sum(dn * unit)
     sum_ref[1:2, :] += row_sum(dn)
@@ -1869,20 +1871,20 @@
     hold([info, sum_c.received], [grad_mem])
     sum_c.y()
     back = call_attend_back(info, q1, k1, v1, o1, do1, lse1, True, 0, 4, other=True)
-    hold([info, sum_f.received, mem_peer], [back[0]])
-    sum_f.z()
+    hold([info, mem_peer], [back[0]])
     memory_other = swap_x(mem_peer.value)
     sum_s1 = ReduceHalves(*call_half_grad(info, True, [n1_t], back[:3], (0, 0, 0), "weight_grad_self_1"))
-    hold([info, sum_s1.send, sum_f.moving], [sum_s1.keep])
+    hold([info, sum_s1.send, sum_f.received], [sum_s1.keep])
     sum_s1.core(), sum_f.z()
     back = call_attend_back(info, q1, k1, v1, o1, do1, lse1, True, 0, 2, back, other=False)
-    hold([info, sum_s1.received, sum_c.received, sum_f.moving], [back[0], memory_other])
+    hold([info, sum_s1.received, sum_c.received, sum_f.moving], [back[0]])
     sum_s1.y(), sum_c.x(), sum_f.z()
     dq1, dk1, dv1, bias1 = call_attend_back(info, q1, k1, v1, o1, do1, lse1, True, 2, 2, back, other=False)
-    hold([info, sum_s1.arrived], [bias1, sum_f.moving])
+    hold([info, sum_s1.arrived, sum_f.moving], [bias1, memory_other])
     across = sum_s1.x()
+    sum_f.z()
     sum_s0 = ReduceHalves(*call_half_grad(info, False, [n1_t], [dq1, dk1, dv1], (0, 0, 0), "weight_grad_self_0"))
-    hold([info, sum_s0.send, sum_c.received], [sum_s0.keep])
+    hold([info, sum_s0.send, sum_c.received], [sum_s0.keep, sum_f.moving])
     sum_s0.core(), sum_c.z()
     grad_other, sums1a = call_back_one(info, par, dq1, dk1, dv1, x, dh1, w_self, True)
     grad_other = Cell(grad_other)

time: 728 us -> 714 us (0.981)
  waiting for transfers between devices: 147 us -> 134 us
    ppermute x14, waiting for transfers between devices: 46 us -> 31.6 us  [swap_x(): return lax.ppermute(value, 'mp', [(0, 1), (1, 0)])]
    unnamed x111 -> x115, local copies, waits for them, and re-layouts: 40.5 us -> 40.4 us
  transfers between devices with their start and end apart: 58 -> 58, of which waited for: 26 -> 24; matrix products, arithmetic and copies ran while one was open for 17% -> 17% of each run, Pallas kernels for 39% -> 39%
where the time goes in v4:
time: 714 us; the launch traced here: 705 us
  Pallas kernels  351 us (49%)
  waiting for transfers between devices  134 us (19%)
  other arithmetic  85.4 us (12%)
  local copies, waits for them, and re-layouts  66 us (9%)
  starting transfers between devices  53.3 us (7%)
  between operations  15.7 us (2%)
    pallas_call x36, Pallas kernels, run(): results = call(*values_of(operands), *after, *passed)  349 us
    ppermute x20, waiting for transfers between devices, next_z(): return lax.ppermute(value, 'dp', RING)  48.4 us
    unnamed x115, local copies, waits for them, and re-layouts  40.4 us
    ppermute x14, waiting for transfers between devices, swap_x(): return lax.ppermute(value, 'mp', [(0, 1), (1, 0)])  31.6 us
    ppermute x10, waiting for transfers between devices, swap_y(): return lax.ppermute(value, 'dp', along(2))  31.2 us
    convert_element_type x6, other arithmetic, join(): return (kept.astype(F32) + received.astype(F32)).astype(kept.dtype)  27.7 us
    ppermute x20, starting transfers between devices, next_z(): return lax.ppermute(value, 'dp', RING)  22.6 us
    ppermute x2, waiting for transfers between devices, sum_rest(): lax.ppermute(value, 'dp', FAR_Z)  16.9 us
  transfers between devices with their start and end apart: 58, of which 24 were waited for; matrix products, arithmetic and copies ran while one was open for 17% of the time, Pallas kernels for 39%

profile of v4, /device:TPU:0, one launch (start us, length us, event | category | flops | bytes accessed | tf_op | source)
XLA Modules:
  0.0 704.7 jit_solution(32796790307814740)
XLA Ops:
  48.3 7.1 %collective-permute-done.8 = bf16[64,1024]{1,0:T(8,128)(2,1)S(1)} collective-permute-done((bf16[64,1024]{1,0:T(8,128)(2,1)S(1)}, bf16[64,1024]{1,0:T(8,128)(2,1)S(1)}, u32[]{:S(2)}, u32[]{:S(2)}) %collective-permute-start.8) | collective-permute-done | bytes 131104 | tf_op jit(solution)/shard_map/ppermute | solution.py:1569
  61.4 13.1 %collective-permute-done.5.refs_3_ = bf16[4,64,512]{2,1,0:T(8,128)(2,1)S(1)} collective-permute-done((bf16[4,64,512]{2,1,0:T(8,128)(2,1)S(1)}, bf16[4,64,512]{2,1,0:T(8,128)(2,1)S(1)}, u32[]{:S(2)}, u32[]{:S(2)}) %collective-permute-start.5) | collective-permute-done | bytes 262176 | tf_op jit(solution)/shard_map/ppermute | solution.py:1569
  74.5 14.2 %collective-permute-done.9.refs_4_ = bf16[4,64,1024]{2,1,0:T(8,128)(2,1)S(1)} collective-permute-done((bf16[4,64,1024]{2,1,0:T(8,128)(2,1)}, bf16[4,64,1024]{2,1,0:T(8,128)(2,1)S(1)}, u32[]{:S(2)}, u32[]{:S(2)}) %collective-permute-start.9) | collective-permute-done | bytes 524320 | tf_op jit(solution)/shard_map/ppermute | solution.py:1557
  98.8 6.5 collective-permute-done.10.refs_0_
  114.7 6.3 collective-permute-done.17
  132.9 9.0 %collective-permute-done.18 = f32[17,1024]{1,0:T(8,128)S(1)} collective-permute-done((f32[17,1024]{1,0:T(8,128)S(1)}, f32[17,1024]{1,0:T(8,128)S(1)}, u32[]{:S(2)}, u32[]{:S(2)}) %collective-permute-start.18) | collective-permute-done | bytes 69664 | tf_op jit(solution)/shard_map/ppermute | solution.py:1654
  147.3 9.9 %collective-permute-done.21 = bf16[2,64,2048]{2,1,0:T(8,128)(2,1)S(1)} collective-permute-done((bf16[2,64,2048]{2,1,0:T(8,128)(2,1)S(1)}, bf16[2,64,2048]{2,1,0:T(8,128)(2,1)S(1)}, u32[]{:S(2)}, u32[]{:S(2)}) %collective-permute-start.21) | collective-permute-done | bytes 524320 | tf_op jit(solution)/shard_map/ppermute | solution.py:1561
  161.9 13.8 %project_self.1 = (bf16[1024,1024]{1,0:T(8,128)(2,1)}, bf16[1024,1024]{1,0:T(8,128)(2,1)}, bf16[1024,1024]{1,0:T(8,128)(2,1)}, bf16[1024,1024]{1,0:T(8,128)(2,1)}) custom-call(s32[8]{0:T(128)} %get-tuple-element.133.refs_0_.refs_2_, f32[24,1024]{1,0:T(8,128)} %concatenate.55.refs_3_.refs_1_, bf16[1024,1024]{1,0:T(8,128)(2,1)} %maximum_select_fusion.refs_2_.refs_5_, ...), custom_call_target="tpu_custom_call" | custom-call | flops 6400000000 | bytes 16000000 | tf_op jit(solution)/shard_map/project_self/pallas_call | solution.py:536
  175.8 19.4 %attend_self.1 = (bf16[1024,1024]{1,0:T(8,128)(2,1)}, f32[8,1024,128]{2,1,0:T(8,128)}) custom-call(s32[8]{0:T(128)} %get-tuple-element.133.refs_0_.refs_2_, bf16[1024,1024]{1,0:T(8,128)(2,1)} %get-tuple-element.134.refs_1_, bf16[1024,1024]{1,0:T(8,128)(2,1)} %get-tuple-element.135.refs_2_, bf16[1024,1024]{1,0:T(8,128)(2,1)} %get-tuple-element.136.refs_3_), custom_call_target="tpu_custom_call" | custom-call | flops 69000003584 | bytes 1000000 | tf_op jit(solution)/shard_map/attend_self/pallas_call | solution.py:536
  207.4 11.7 %after_self.1 = (bf16[1024,1024]{1,0:T(8,128)(2,1)}, bf16[1024,1024]{1,0:T(8,128)(2,1)}, bf16[1024,1024]{1,0:T(8,128)(2,1)}) custom-call(s32[8]{0:T(128)} %get-tuple-element.140.refs_0_.refs_1_, f32[24,1024]{1,0:T(8,128)} %concatenate.55.refs_3_.refs_1_, bf16[1024,1024]{1,0:T(8,128)(2,1)} %maximum_select_fusion.refs_2_.refs_5_, ...), custom_call_target="tpu_custom_call" | custom-call | flops 4300000256 | bytes 16000000 | tf_op jit(solution)/shard_map/after_self/pallas_call | solution.py:536
  219.1 10.2 %project_memory.1 = (bf16[1024,1024]{1,0:T(8,128)(2,1)}, bf16[1024,1024]{1,0:T(8,128)(2,1)}, bf16[1024,1024]{1,0:T(8,128)(2,1)}) custom-call(s32[8]{0:T(128)} %get-tuple-element.140.refs_0_.refs_1_, f32[24,1024]{1,0:T(8,128)} %concatenate.55.refs_3_.refs_1_, bf16[1024,1024]{1,0:T(8,128)(2,1)} %maximum_select_fusion.1.refs_2_, ...), custom_call_target="tpu_custom_call" | custom-call | flops 4300000256 | bytes 12000000 | tf_op jit(solution)/shard_map/project_memory/pallas_call | solution.py:536
  229.4 24.5 %attend_cross.1 = (bf16[1024,1024]{1,0:T(8,128)(2,1)}, f32[8,1024,128]{2,1,0:T(8,128)}) custom-call(s32[8]{0:T(128)} %get-tuple-element.144.refs_0_.refs_2_, bf16[1024,1024]{1,0:T(8,128)(2,1)} %get-tuple-element.141.refs_4_.refs_1_, bf16[1024,1024]{1,0:T(8,128)(2,1)} %get-tuple-element.142.refs_0_.refs_2_, bf16[1024,1024]{1,0:T(8,128)(2,1)} %get-tuple-element.145.refs_3_), custom_call_target="tpu_custom_call" | custom-call | flops 110399995904 | bytes 1000000 | tf_op jit(solution)/shard_map/attend_cross/pallas_call | solution.py:536
  266.9 11.0 %after_cross.1 = (bf16[1024,1024]{1,0:T(8,128)(2,1)}, bf16[1024,1024]{1,0:T(8,128)(2,1)}, bf16[1024,1024]{1,0:T(8,128)(2,1)}, bf16[1024,1024]{1,0:T(8,128)(2,1)}...) custom-call(s32[8]{0:T(128)} %get-tuple-element.149.refs_0_.refs_1_, f32[24,1024]{1,0:T(8,128)} %concatenate.55.refs_3_.refs_1_, ...), custom_call_target="tpu_custom_call" | custom-call | flops 2200000000 | bytes 26000000 | tf_op jit(solution)/shard_map/after_cross/pallas_call | solution.py:536
  277.9 73.3 %feedforward.1 = (bf16[512,1024]{1,0:T(8,128)(2,1)}, bf16[512,1024]{1,0:T(8,128)(2,1)}, bf16[1024,1024]{1,0:T(8,128)(2,1)}, bf16[2,2,4,2,64,2048]{5,4,3,2,1,0:T(...) custom-call(s32[8]{0:T(128)} %get-tuple-element.149.refs_0_.refs_1_, ...), custom_call_target="tpu_custom_call" | custom-call | flops 51499999232 | bytes 60000000 | tf_op jit(solution)/shard_map/feedforward/pallas_call | solution.py:536
  352.3 11.1 %back_three.1 = (bf16[1024,1024]{1,0:T(8,128)(2,1)}, bf16[1024,1024]{1,0:T(8,128)(2,1)}, bf16[1024,1024]{1,0:T(8,128)(2,1)}, f32[8,1024]{1,0:T(8,128)}) custom-call(s32[8]{0:T(128)} %get-tuple-element.149.refs_0_.refs_1_, f32[24,1024]{1,0:T(8,128)} %concatenate.55.refs_3_.refs_1_, bf16[1024,1024]{1,0:T(8,128)(2,1)} %get-tuple-element.159.refs_2_, ...), custom_call_target="tpu_custom_call" | custom-call | flops 2200000000 | bytes 20000000 | tf_op jit(solution)/shard_map/back_three/pallas_call | solution.py:536
  365.0 10.1 %add_convert_fusion = (bf16[1,2,4,2,64,2048]{5,4,3,2,1,0:T(8,128)(2,1)}, bf16[2,4,2,64,2048]{4,3,2,1,0:T(8,128)(2,1)}) fusion(bf16[2,2,4,2,64,2048]{5,4,3,2,1,0:T(8,128)(2,1)} %get-tuple-element.176, bf16[2,2,4,2,64,2048]{5,4,3,2,1,0:T(8,128)(2,1)} %get-tuple-element.175), kind=kLoop, calls=%fused_computation | loop fusion | flops 16777216 | bytes 25165824 | tf_op jit(solution)/shard_map/convert_element_type | solution.py:1659
  375.7 49.1 %attend_back_cross.1 = (bf16[1024,1024]{1,0:T(8,128)(2,1)}, bf16[1024,1024]{1,0:T(8,128)(2,1)}, bf16[1024,1024]{1,0:T(8,128)(2,1)}, f32[8,1024]{1,0:T(8,128)}) custom-call(s32[8]{0:T(128)} %get-tuple-element.162.refs_0_.refs_2_, bf16[1024,1024]{1,0:T(8,128)(2,1)} %get-tuple-element.141.refs_4_.refs_1_, ...), custom_call_target="tpu_custom_call" | custom-call | flops 142599995392 | bytes 1000000 | tf_op jit(solution)/shard_map/attend_back_cross/pallas_call | solution.py:536
  424.9 12.7 %back_two.1 = (bf16[1024,1024]{1,0:T(8,128)(2,1)}, bf16[1024,1024]{1,0:T(8,128)(2,1)}, bf16[1024,1024]{1,0:T(8,128)(2,1)}, f32[8,1024]{1,0:T(8,128)}) custom-call(s32[8]{0:T(128)} %get-tuple-element.162.refs_0_.refs_2_, f32[24,1024]{1,0:T(8,128)} %concatenate.55.refs_3_.refs_1_, bf16[1024,1024]{1,0:T(8,128)(2,1)} %get-tuple-element.167.refs_2_.refs_7_, ...), custom_call_target="tpu_custom_call" | custom-call | flops 4300000256 | bytes 24000000 | tf_op jit(solution)/shard_map/back_two/pallas_call | solution.py:536
  437.6 22.7 %weight_grad_cross.1 = (bf16[2,2,4,64,2560]{4,3,2,1,0:T(8,128)(2,1)}, bf16[2,2,4,64,2560]{4,3,2,1,0:T(8,128)(2,1)}) custom-call(s32[8]{0:T(128)} %get-tuple-element.162.refs_0_.refs_2_, bf16[1024,1024]{1,0:T(8,128)(2,1)} %get-tuple-element.163.refs_1_, bf16[1024,1024]{1,0:T(8,128)(2,1)} %get-tuple-element.164.refs_2_, ...), custom_call_target="tpu_custom_call" | custom-call | flops 51499999232 | bytes 1000000 | tf_op jit(solution)/shard_map/weight_grad_cross/pallas_call | solution.py:536
  460.3 7.9 %collective-permute-done.30.refs_4_ = bf16[2,4,2,64,2048]{4,3,2,1,0:T(8,128)(2,1)} collective-permute-done((bf16[2,4,2,64,2048]{4,3,2,1,0:T(8,128)(2,1)}, bf16[2,4,2,64,2048]{4,3,2,1,0:T(8,128)(2,1)}, u32[]{:S(2)}, u32[]{:S(2)}) %collective-permute-start.30) | collective-permute-done | bytes 4194336 | tf_op jit(solution)/shard_map/ppermute | solution.py:1561
  479.1 10.5 %memory_back.1 = (bf16[512,1024]{1,0:T(8,128)(2,1)}, bf16[512,1024]{1,0:T(8,128)(2,1)}) custom-call(s32[8]{0:T(128)} %get-tuple-element.177.refs_0_.refs_1_, bf16[1024,1024]{1,0:T(8,128)(2,1)} %get-tuple-element.170.refs_5_.refs_1_, bf16[1024,1024]{1,0:T(8,128)(2,1)} %get-tuple-element.171.refs_6_.refs_2_, bf16[32,64,4608]{2,1,0:T(8,128)(2,1)} %bitcast.188), custom_call_target="tpu_custom_call" | custom-call | flops 4300000256 | bytes 12000000 | tf_op jit(solution)/shard_map/memory_back/pallas_call | solution.py:536
  496.5 18.8 %attend_back_self.3 = (bf16[1024,1024]{1,0:T(8,128)(2,1)}, bf16[1024,1024]{1,0:T(8,128)(2,1)}, bf16[1024,1024]{1,0:T(8,128)(2,1)}, f32[8,1024]{1,0:T(8,128)}) custom-call(s32[8]{0:T(128)} %get-tuple-element.180.refs_0_.refs_1_, bf16[1024,1024]{1,0:T(8,128)(2,1)} %get-tuple-element.134.refs_1_, bf16[1024,1024]{1,0:T(8,128)(2,1)} %get-tuple-element.135.refs_2_, ...), custom_call_target="tpu_custom_call" | custom-call | flops 44562501632 | bytes 1000000 | tf_op jit(solution)/shard_map/attend_back_self/pallas_call | solution.py:536
  516.9 8.5 %weight_grad_self_1.1 = (bf16[2,4,64,1536]{3,2,1,0:T(8,128)(2,1)}, bf16[2,4,64,1536]{3,2,1,0:T(8,128)(2,1)}) custom-call(s32[8]{0:T(128)} %get-tuple-element.184.refs_0_.refs_1_, bf16[1024,1024]{1,0:T(8,128)(2,1)} %get-tuple-element.185.refs_1_, bf16[1024,1024]{1,0:T(8,128)(2,1)} %get-tuple-element.182.refs_0_.refs_2_.refs_7_, ...), custom_call_target="tpu_custom_call" | custom-call | flops 10000000000 | bytes 1000000 | tf_op jit(solution)/shard_map/weight_grad_self_1/pallas_call | solution.py:536
  530.6 11.0 %attend_back_self.4 = (bf16[1024,1024]{1,0:T(8,128)(2,1)}, bf16[1024,1024]{1,0:T(8,128)(2,1)}, bf16[1024,1024]{1,0:T(8,128)(2,1)}, f32[8,1024]{1,0:T(8,128)}) custom-call(s32[8]{0:T(128)} %get-tuple-element.191.refs_0_.refs_1_, ...), custom_call_target="tpu_custom_call", output_to_operand_aliasing={{0}: (7, {}), {1}: (8, {}), {2}: (9, {}), {3}: (10, {})} | custom-call | flops 22281250816 | bytes 1000000 | tf_op jit(solution)/shard_map/attend_back_self/pallas_call | solution.py:536
  541.6 7.0 collective-permute-done.36.refs_1_
  567.0 10.8 %attend_back_self.5 = (bf16[1024,1024]{1,0:T(8,128)(2,1)}, bf16[1024,1024]{1,0:T(8,128)(2,1)}, bf16[1024,1024]{1,0:T(8,128)(2,1)}, f32[8,1024]{1,0:T(8,128)}) custom-call(s32[8]{0:T(128)} %get-tuple-element.197.refs_0_.refs_2_, ...), custom_call_target="tpu_custom_call", output_to_operand_aliasing={{0}: (7, {}), {1}: (8, {}), {2}: (9, {}), {3}: (10, {})} | custom-call | flops 22281250816 | bytes 1000000 | tf_op jit(solution)/shard_map/attend_back_self/pallas_call | solution.py:536
  590.5 8.1 %weight_grad_self_0.1 = (bf16[2,4,64,1536]{3,2,1,0:T(8,128)(2,1)}, bf16[2,4,64,1536]{3,2,1,0:T(8,128)(2,1)}) custom-call(s32[8]{0:T(128)} %get-tuple-element.205.refs_0_.refs_2_, bf16[1024,1024]{1,0:T(8,128)(2,1)} %get-tuple-element.185.refs_1_, bf16[1024,1024]{1,0:T(8,128)(2,1)} %get-tuple-element.206.refs_2_, ...), custom_call_target="tpu_custom_call" | custom-call | flops 10000000000 | bytes 1000000 | tf_op jit(solution)/shard_map/weight_grad_self_0/pallas_call | solution.py:536
  604.1 10.9 %back_one.2 = (bf16[512,1024]{1,0:T(8,128)(2,1)}, f32[8,1024]{1,0:T(8,128)}) custom-call(s32[8]{0:T(128)} %get-tuple-element.213.refs_0_, f32[24,1024]{1,0:T(8,128)} %concatenate.55.refs_3_.refs_1_, bf16[1024,1024]{1,0:T(8,128)(2,1)} %get-tuple-element.206.refs_2_, bf16[1024,1024]{1,0:T(8,128)(2,1)} %get-tuple-element.207.refs_3_, ...), custom_call_target="tpu_custom_call" | custom-call | flops 6400000000 | bytes 20000000 | tf_op jit(solution)/shard_map/back_one/pallas_call | solution.py:536
  625.4 10.9 %back_one.3 = (bf16[512,1024]{1,0:T(8,128)(2,1)}, f32[8,1024]{1,0:T(8,128)}) custom-call(s32[8]{0:T(128)} %get-tuple-element.219.refs_0_, f32[24,1024]{1,0:T(8,128)} %concatenate.55.refs_3_.refs_1_, bf16[1024,1024]{1,0:T(8,128)(2,1)} %get-tuple-element.206.refs_2_, bf16[1024,1024]{1,0:T(8,128)(2,1)} %get-tuple-element.207.refs_3_, ...), custom_call_target="tpu_custom_call" | custom-call | flops 6400000000 | bytes 20000000 | tf_op jit(solution)/shard_map/back_one/pallas_call | solution.py:536
  641.5 6.8 collective-permute-done.44.refs_0_
  672.0 7.9 %collective-permute-done.53 = f32[24,1024]{1,0:T(8,128)S(1)} collective-permute-done((f32[24,1024]{1,0:T(8,128)S(1)}, f32[24,1024]{1,0:T(8,128)S(1)}, u32[]{:S(2)}, u32[]{:S(2)}) %collective-permute-start.53) | collective-permute-done | bytes 98336 | tf_op jit(solution)/shard_map/ppermute | solution.py:1654
  689.1 6.4 collective-permute-done.49
  (327 shorter events, 227.6 us)
Async XLA Ops:
  7.2 200.1 %all-gather.3.cloned.1.call-start = ((), (), s32[]{:S(2)}) async-start(), calls=%async_computation | async-start | bytes 19464192 | tf_op jit(solution)/shard_map/all_gather | solution.py:1817
  16.9 18.8 %collective-permute-start.3 = (f32[17,1024]{1,0:T(8,128)S(1)}, f32[17,1024]{1,0:T(8,128)S(1)}, u32[]{:S(2)}, u32[]{:S(2)}) collective-permute-start(f32[17,1024]{1,0:T(8,128)S(1)} %pad_maximum_fusion.9), channel_id=1, source_target_pairs={{0,1},{1,0},{2,3},{3,2},{4,5},{5,4},{6,7},{7,6},{8,9},{9,8},{10,11... | collective-permute-start | bytes 208904 | tf_op jit(solution)/shard_map/ppermute | solution.py:1557
  36.4 52.3 %collective-permute-start.4 = (bf16[512,1024]{1,0:T(8,128)(2,1)}, bf16[512,1024]{1,0:T(8,128)(2,1)}, u32[]{:S(2)}, u32[]{:S(2)}) collective-permute-start(bf16[512,1024]{1,0:T(8,128)(2,1)} %get-tuple-element.124), channel_id=1, source_target_pairs={{0,1},{1,0},{2,3},{3,2},{4,5},{5,4},{6,7},{7,6},{8,9},{9,8},{10,11... | collective-permute-start | bytes 3145736 | tf_op jit(solution)/shard_map/ppermute | solution.py:1557
  38.0 20.6 %collective-permute-start.2 = (bf16[4,64,512]{2,1,0:T(8,128)(2,1)S(1)}, bf16[4,64,512]{2,1,0:T(8,128)(2,1)S(1)}, u32[]{:S(2)}, u32[]{:S(2)}) collective-permute-start(bf16[4,64,512]{2,1,0:T(8,128)(2,1)S(1)} %pad_maximum_fusion.6.refs_8_.refs_12_), channel_id=1, source_target_pairs={{0,8},{2,10},{4,12},{6,14},{8,16},{10,18},{12,20},{14,22},{16,24},... | collective-permute-start | bytes 786440 | tf_op jit(solution)/shard_map/ppermute | solution.py:1569
  56.4 32.3 %collective-permute-start.9 = (bf16[4,64,1024]{2,1,0:T(8,128)(2,1)}, bf16[4,64,1024]{2,1,0:T(8,128)(2,1)S(1)}, u32[]{:S(2)}, u32[]{:S(2)}) collective-permute-start(bf16[4,64,1024]{2,1,0:T(8,128)(2,1)} %pad_maximum_fusion.2.refs_3_.refs_7_), channel_id=1, source_target_pairs={{0,1},{1,0},{2,3},{3,2},{4,5},{5,4},{6,7},{7,6},{8,9},{9,8},{10,11... | collective-permute-start | bytes 1572872 | tf_op jit(solution)/shard_map/ppermute | solution.py:1557
  59.3 36.7 %collective-permute-start.14 = (bf16[4,64,1024]{2,1,0:T(8,128)(2,1)}, bf16[4,64,1024]{2,1,0:T(8,128)(2,1)}, u32[]{:S(2)}, u32[]{:S(2)}) collective-permute-start(bf16[4,64,1024]{2,1,0:T(8,128)(2,1)} %pad_maximum_fusion.2.refs_3_.refs_7_), channel_id=1, source_target_pairs={{0,4},{2,6},{4,0},{6,2},{8,12},{10,14},{12,8},{14,10},{16,20},{18,... | collective-permute-start | bytes 1572872 | tf_op jit(solution)/shard_map/ppermute | solution.py:1561
  108.7 49.7 %collective-permute-start.15 = (bf16[16,64,1024]{2,1,0:T(8,128)(2,1)}, bf16[16,64,1024]{2,1,0:T(8,128)(2,1)}, u32[]{:S(2)}, u32[]{:S(2)}) collective-permute-start(bf16[16,64,1024]{2,1,0:T(8,128)(2,1)} %constant_dynamic-update-slice_fusion.6), channel_id=1, source_target_pairs={{0,2},{2,0},{4,6},{6,4},{8,10},{10,8},{12,14},{14,12},{16,18},{18,... | collective-permute-start | bytes 6291464 | tf_op jit(solution)/shard_map/ppermute | solution.py:1565
  123.2 18.7 %collective-permute-start.18 = (f32[17,1024]{1,0:T(8,128)S(1)}, f32[17,1024]{1,0:T(8,128)S(1)}, u32[]{:S(2)}, u32[]{:S(2)}) collective-permute-start(f32[17,1024]{1,0:T(8,128)S(1)} %add.273), channel_id=1, source_target_pairs={{0,16},{2,18},{4,20},{6,22},{8,24},{10,26},{12,28},{14,30},{16,0},... | collective-permute-start | bytes 208904 | tf_op jit(solution)/shard_map/ppermute | solution.py:1654
  125.3 33.0 %collective-permute-start.13 = (bf16[16,64,512]{2,1,0:T(8,128)(2,1)}, bf16[16,64,512]{2,1,0:T(8,128)(2,1)}, u32[]{:S(2)}, u32[]{:S(2)}) collective-permute-start(bf16[16,64,512]{2,1,0:T(8,128)(2,1)} %constant_dynamic-update-slice_fusion), channel_id=1, source_target_pairs={{0,2},{2,0},{4,6},{6,4},{8,10},{10,8},{12,14},{14,12},{16,18},{18,... | collective-permute-start | bytes 3145736 | tf_op jit(solution)/shard_map/ppermute | solution.py:1565
  132.8 24.4 %collective-permute-start.21 = (bf16[2,64,2048]{2,1,0:T(8,128)(2,1)S(1)}, bf16[2,64,2048]{2,1,0:T(8,128)(2,1)S(1)}, u32[]{:S(2)}, u32[]{:S(2)}) collective-permute-start(bf16[2,64,2048]{2,1,0:T(8,128)(2,1)S(1)} %copy-done.11), channel_id=1, source_target_pairs={{0,4},{2,6},{4,0},{6,2},{8,12},{10,14},{12,8},{14,10},{16,20},{18,... | collective-permute-start | bytes 1572872 | tf_op jit(solution)/shard_map/ppermute | solution.py:1561
  159.0 36.2 %collective-permute-start.22 = (bf16[512,1024]{1,0:T(8,128)(2,1)}, bf16[512,1024]{1,0:T(8,128)(2,1)S(1)}, u32[]{:S(2)}, u32[]{:S(2)}) collective-permute-start(bf16[512,1024]{1,0:T(8,128)(2,1)} %get-tuple-element.138), channel_id=1, source_target_pairs={{0,1},{1,0},{2,3},{3,2},{4,5},{5,4},{6,7},{7,6},{8,9},{9,8},{10,11... | collective-permute-start | bytes 3145736 | tf_op jit(solution)/shard_map/ppermute | solution.py:1557
  160.3 40.7 %collective-permute-start.23 = (bf16[4,64,2048]{2,1,0:T(8,128)(2,1)}, bf16[4,64,2048]{2,1,0:T(8,128)(2,1)S(1)}, u32[]{:S(2)}, u32[]{:S(2)}) collective-permute-start(bf16[4,64,2048]{2,1,0:T(8,128)(2,1)} %get-tuple-element.139.refs_9_), channel_id=1, source_target_pairs={{0,8},{2,10},{4,12},{6,14},{8,16},{10,18},{12,20},{14,22},{16,24},... | collective-permute-start | bytes 3145736 | tf_op jit(solution)/shard_map/ppermute | solution.py:1569
  202.1 27.2 %collective-permute-start.24 = (bf16[4,64,2048]{2,1,0:T(8,128)(2,1)}, bf16[4,64,2048]{2,1,0:T(8,128)(2,1)}, u32[]{:S(2)}, u32[]{:S(2)}) collective-permute-start(bf16[4,64,2048]{2,1,0:T(8,128)(2,1)} %get-tuple-element.143.refs_10_), channel_id=1, source_target_pairs={{0,8},{2,10},{4,12},{6,14},{8,16},{10,18},{12,20},{14,22},{16,24},... | collective-permute-start | bytes 3145736 | tf_op jit(solution)/shard_map/ppermute | solution.py:1569
  202.1 51.9 %collective-permute-start.25 = (bf16[512,1024]{1,0:T(8,128)(2,1)}, bf16[512,1024]{1,0:T(8,128)(2,1)S(1)}, u32[]{:S(2)}, u32[]{:S(2)}) collective-permute-start(bf16[512,1024]{1,0:T(8,128)(2,1)} %get-tuple-element.147), channel_id=1, source_target_pairs={{0,1},{1,0},{2,3},{3,2},{4,5},{5,4},{6,7},{7,6},{8,9},{9,8},{10,11... | collective-permute-start | bytes 3145736 | tf_op jit(solution)/shard_map/ppermute | solution.py:1557
  229.3 26.0 %collective-permute-start.26 = (bf16[4,64,2048]{2,1,0:T(8,128)(2,1)}, bf16[4,64,2048]{2,1,0:T(8,128)(2,1)S(1)}, u32[]{:S(2)}, u32[]{:S(2)}) collective-permute-start(bf16[4,64,2048]{2,1,0:T(8,128)(2,1)} %get-tuple-element.148.refs_11_), channel_id=1, source_target_pairs={{0,8},{2,10},{4,12},{6,14},{8,16},{10,18},{12,20},{14,22},{16,24},... | collective-permute-start | bytes 3145736 | tf_op jit(solution)/shard_map/ppermute | solution.py:1569
  351.8 108.5 %collective-permute-start.28 = (bf16[512,1024]{1,0:T(8,128)(2,1)}, bf16[512,1024]{1,0:T(8,128)(2,1)}, u32[]{:S(2)}, u32[]{:S(2)}) collective-permute-start(bf16[512,1024]{1,0:T(8,128)(2,1)} %get-tuple-element.158), channel_id=1, source_target_pairs={{0,1},{1,0},{2,3},{3,2},{4,5},{5,4},{6,7},{7,6},{8,9},{9,8},{10,11... | collective-permute-start | bytes 3145736 | tf_op jit(solution)/shard_map/ppermute | solution.py:1557
  375.1 93.2 %collective-permute-start.30 = (bf16[2,4,2,64,2048]{4,3,2,1,0:T(8,128)(2,1)}, bf16[2,4,2,64,2048]{4,3,2,1,0:T(8,128)(2,1)}, u32[]{:S(2)}, u32[]{:S(2)}) collective-permute-start(bf16[2,4,2,64,2048]{4,3,2,1,0:T(8,128)(2,1)} %get-tuple-element.262), channel_id=1, source_target_pairs={{0,4},{2,6},{4,0},{6,2},{8,12},{10,14},{12,8},{14,10},{16,20},{18,... | collective-permute-start | bytes 12582920 | tf_op jit(solution)/shard_map/ppermute | solution.py:1561
  468.2 21.4 %collective-permute-start.31 = (bf16[2,2,4,64,2560]{4,3,2,1,0:T(8,128)(2,1)}, bf16[2,2,4,64,2560]{4,3,2,1,0:T(8,128)(2,1)}, u32[]{:S(2)}, u32[]{:S(2)}) collective-permute-start(bf16[2,2,4,64,2560]{4,3,2,1,0:T(8,128)(2,1)} %get-tuple-element.179), channel_id=1, source_target_pairs={{0,2},{2,0},{4,6},{6,4},{8,10},{10,8},{12,14},{14,12},{16,18},{18,... | collective-permute-start | bytes 15728648 | tf_op jit(solution)/shard_map/ppermute | solution.py:1565
  478.7 48.9 %collective-permute-start.32 = (bf16[4,2,64,2048]{3,2,1,0:T(8,128)(2,1)}, bf16[4,2,64,2048]{3,2,1,0:T(8,128)(2,1)}, u32[]{:S(2)}, u32[]{:S(2)}) collective-permute-start(bf16[4,2,64,2048]{3,2,1,0:T(8,128)(2,1)} %fusion.4), channel_id=1, source_target_pairs={{0,1},{1,0},{2,3},{3,2},{4,5},{5,4},{6,7},{7,6},{8,9},{9,8},{10,11... | collective-permute-start | bytes 6291464 | tf_op jit(solution)/shard_map/ppermute | solution.py:1557
  496.0 59.9 %collective-permute-start.34 = (bf16[2,4,64,2560]{3,2,1,0:T(8,128)(2,1)}, bf16[2,4,64,2560]{3,2,1,0:T(8,128)(2,1)S(1)}, u32[]{:S(2)}, u32[]{:S(2)}) collective-permute-start(bf16[2,4,64,2560]{3,2,1,0:T(8,128)(2,1)} %get-tuple-element.264), channel_id=1, source_target_pairs={{0,4},{2,6},{4,0},{6,2},{8,12},{10,14},{12,8},{14,10},{16,20},{18,... | collective-permute-start | bytes 7864328 | tf_op jit(solution)/shard_map/ppermute | solution.py:1561
  515.3 33.3 %collective-permute-start.36 = (bf16[512,1024]{1,0:T(8,128)(2,1)}, bf16[512,1024]{1,0:T(8,128)(2,1)}, u32[]{:S(2)}, u32[]{:S(2)}) collective-permute-start(bf16[512,1024]{1,0:T(8,128)(2,1)} %get-tuple-element.202), channel_id=1, source_target_pairs={{0,1},{1,0},{2,3},{3,2},{4,5},{5,4},{6,7},{7,6},{8,9},{9,8},{10,11... | collective-permute-start | bytes 3145736 | tf_op jit(solution)/shard_map/ppermute | solution.py:1557
  529.9 25.9 %collective-permute-start.35 = (bf16[2,64,2048]{2,1,0:T(8,128)(2,1)}, bf16[2,64,2048]{2,1,0:T(8,128)(2,1)}, u32[]{:S(2)}, u32[]{:S(2)}) collective-permute-start(bf16[2,64,2048]{2,1,0:T(8,128)(2,1)} %fusion.14), channel_id=1, source_target_pairs={{0,8},{2,10},{4,12},{6,14},{8,16},{10,18},{12,20},{14,22},{16,24},... | collective-permute-start | bytes 1572872 | tf_op jit(solution)/shard_map/ppermute | solution.py:1569
  530.6 25.3 %collective-permute-start.33 = (bf16[2,4,64,1536]{3,2,1,0:T(8,128)(2,1)}, bf16[2,4,64,1536]{3,2,1,0:T(8,128)(2,1)}, u32[]{:S(2)}, u32[]{:S(2)}) collective-permute-start(bf16[2,4,64,1536]{3,2,1,0:T(8,128)(2,1)} %get-tuple-element.194), channel_id=1, source_target_pairs={{0,2},{2,0},{4,6},{6,4},{8,10},{10,8},{12,14},{14,12},{16,18},{18,... | collective-permute-start | bytes 4718600 | tf_op jit(solution)/shard_map/ppermute | solution.py:1565
  560.2 17.7 %collective-permute-start.38 = (bf16[2,64,2048]{2,1,0:T(8,128)(2,1)}, bf16[2,64,2048]{2,1,0:T(8,128)(2,1)}, u32[]{:S(2)}, u32[]{:S(2)}) collective-permute-start(bf16[2,64,2048]{2,1,0:T(8,128)(2,1)} %fusion.13), channel_id=1, source_target_pairs={{0,8},{2,10},{4,12},{6,14},{8,16},{10,18},{12,20},{14,22},{16,24},... | collective-permute-start | bytes 1572872 | tf_op jit(solution)/shard_map/ppermute | solution.py:1569
  563.2 18.1 %collective-permute-start.37 = (bf16[4,64,1536]{2,1,0:T(8,128)(2,1)}, bf16[4,64,1536]{2,1,0:T(8,128)(2,1)}, u32[]{:S(2)}, u32[]{:S(2)}) collective-permute-start(bf16[4,64,1536]{2,1,0:T(8,128)(2,1)} %fusion.15), channel_id=1, source_target_pairs={{0,4},{2,6},{4,0},{6,2},{8,12},{10,14},{12,8},{14,10},{16,20},{18,... | collective-permute-start | bytes 2359304 | tf_op jit(solution)/shard_map/ppermute | solution.py:1561
  566.4 32.2 %collective-permute-start.40 = (bf16[4,64,2560]{2,1,0:T(8,128)(2,1)}, bf16[4,64,2560]{2,1,0:T(8,128)(2,1)S(1)}, u32[]{:S(2)}, u32[]{:S(2)}) collective-permute-start(bf16[4,64,2560]{2,1,0:T(8,128)(2,1)} %fusion.8), channel_id=1, source_target_pairs={{0,1},{1,0},{2,3},{3,2},{4,5},{5,4},{6,7},{7,6},{8,9},{9,8},{10,11... | collective-permute-start | bytes 3932168 | tf_op jit(solution)/shard_map/ppermute | solution.py:1557
  590.0 27.9 %collective-permute-start.43 = (bf16[4,64,1536]{2,1,0:T(8,128)(2,1)}, bf16[4,64,1536]{2,1,0:T(8,128)(2,1)}, u32[]{:S(2)}, u32[]{:S(2)}) collective-permute-start(bf16[4,64,1536]{2,1,0:T(8,128)(2,1)} %fusion.7), channel_id=1, source_target_pairs={{0,1},{1,0},{2,3},{3,2},{4,5},{5,4},{6,7},{7,6},{8,9},{9,8},{10,11... | collective-permute-start | bytes 2359304 | tf_op jit(solution)/shard_map/ppermute | solution.py:1557
  600.9 17.0 %collective-permute-start.42 = (bf16[64,2560]{1,0:T(8,128)(2,1)S(1)}, bf16[64,2560]{1,0:T(8,128)(2,1)S(1)}, u32[]{:S(2)}, u32[]{:S(2)}) collective-permute-start(bf16[64,2560]{1,0:T(8,128)(2,1)S(1)} %fusion.22), channel_id=1, source_target_pairs={{0,8},{2,10},{4,12},{6,14},{8,16},{10,18},{12,20},{14,22},{16,24},... | collective-permute-start | bytes 983048 | tf_op jit(solution)/shard_map/ppermute | solution.py:1569
  621.2 20.3 %collective-permute-start.45 = (bf16[4,64,1536]{2,1,0:T(8,128)(2,1)}, bf16[4,64,1536]{2,1,0:T(8,128)(2,1)}, u32[]{:S(2)}, u32[]{:S(2)}) collective-permute-start(bf16[4,64,1536]{2,1,0:T(8,128)(2,1)} %fusion.16), channel_id=1, source_target_pairs={{0,4},{2,6},{4,0},{6,2},{8,12},{10,14},{12,8},{14,10},{16,20},{18,... | collective-permute-start | bytes 2359304 | tf_op jit(solution)/shard_map/ppermute | solution.py:1561
  622.7 25.6 %collective-permute-start.44 = (bf16[512,1024]{1,0:T(8,128)(2,1)}, bf16[512,1024]{1,0:T(8,128)(2,1)}, u32[]{:S(2)}, u32[]{:S(2)}) collective-permute-start(bf16[512,1024]{1,0:T(8,128)(2,1)} %get-tuple-element.221), channel_id=1, source_target_pairs={{0,1},{1,0},{2,3},{3,2},{4,5},{5,4},{6,7},{7,6},{8,9},{9,8},{10,11... | collective-permute-start | bytes 3145736 | tf_op jit(solution)/shard_map/ppermute | solution.py:1557
  651.1 29.4 %collective-permute-start.50 = (bf16[64,2560]{1,0:T(8,128)(2,1)S(1)}, bf16[64,2560]{1,0:T(8,128)(2,1)S(1)}, u32[]{:S(2)}, u32[]{:S(2)}) collective-permute-start(bf16[64,2560]{1,0:T(8,128)(2,1)S(1)} %fusion.18), channel_id=1, source_target_pairs={{0,8},{2,10},{4,12},{6,14},{8,16},{10,18},{12,20},{14,22},{16,24},... | collective-permute-start | bytes 983048 | tf_op jit(solution)/shard_map/ppermute | solution.py:1569
  666.8 19.4 %collective-permute-start.48 = (bf16[64,1536]{1,0:T(8,128)(2,1)S(1)}, bf16[64,1536]{1,0:T(8,128)(2,1)}, u32[]{:S(2)}, u32[]{:S(2)}) collective-permute-start(bf16[64,1536]{1,0:T(8,128)(2,1)S(1)} %fusion.25), channel_id=1, source_target_pairs={{0,8},{2,10},{4,12},{6,14},{8,16},{10,18},{12,20},{14,22},{16,24},... | collective-permute-start | bytes 589832 | tf_op jit(solution)/shard_map/ppermute | solution.py:1569
  (73 other events, 610.1 us)
Sparse Core Ops, SparseCore 0:
  15.3 178.9 all-gather.2
